TPU v7x, 256 devices: a whole 4x4x8 slice. The times are simulated.
256 devices in a mesh: rows: 32 (over z, x_lo, core), chan: 8 (over y, x_hi).
Axes of the slice: x: 4 (x_hi: 2, x_lo: 2; x = x_hi * 2 + x_lo), y: 4, z: 8, core: 2. Of those that a mesh axis runs over, the one named last changes fastest.
Arguments:
- feature: bfloat16 [96, 144, 1536], P('rows', None, 'chan'), may hold values from -6 to 6
- kernel: float32 [7, 7, 1536], P(None, None, 'chan'), may hold values from -0.875 to 0.875
- ln_gain: float32 [1536], replicated, may hold values from 0.1 to 1.9
- layer_scale: float32 [1536], replicated, may hold values from 0.1 to 1.9
- w_in: bfloat16 [1536, 6144], P(None, 'chan'), may hold values from -0.15625 to 0.15625
- w_out: bfloat16 [6144, 1536], P('chan'), may hold values from -0.078125 to 0.078125
- cotangent: bfloat16 [96, 144, 1536], P('rows'), may hold values from -6 to 6
Outputs:
- grad_feature: bfloat16 [96, 144, 1536], P('rows', None, 'chan')
- grad_w_in: float32 [1536, 6144], P('rows', 'chan')
- grad_w_out: float32 [6144, 1536], P('chan', 'rows')
- grad_kernel: float32 [7, 7, 1536], P(None, None, 'chan')
All inputs are finite; a program needn't handle non-finite values.
Results may differ from a plain program's by a relative error of at most 0.03.
Values may be sent and summed in bfloat16 or wider, within the bound.
No kernel may reach another device: no remote copies, remote signals or barrier semaphores. Data moves between devices by JAX's collectives and lax.ppermute only.
A program may use at most 128 MiB of HBM per device.

v0:
```python
import math

import jax
import jax.numpy as jnp
from jax import lax
from jax.sharding import PartitionSpec as P


def extended(cells, sides, width):
    for axis, dim in sides:
        count = lax.axis_size(axis)
        ends = count - 1
        head = lax.slice_in_dim(cells, 0, width, axis=dim)
        tail = lax.slice_in_dim(cells, cells.shape[dim] - width, cells.shape[dim], axis=dim)
        cells = jnp.concatenate(
            [
                lax.ppermute(tail, axis, [(i, (i + 1) % count) for i in range(ends)]),
                cells,
                lax.ppermute(head, axis, [((i + 1) % count, i) for i in range(ends)]),
            ],
            axis=dim,
        )
    return cells


def conv_taps(padded, kernel, height, width):
    result = jnp.zeros((height, width, kernel.shape[2]), jnp.float32)
    for tap_row in range(7):
        for tap_col in range(7):
            window = padded[tap_row : tap_row + height, tap_col : tap_col + width].astype(
                jnp.float32
            )
            result = result + window * kernel[tap_row, tap_col]
    return result


def conv_back(grad_pad, kernel, height, width):
    result = jnp.zeros((height, width, kernel.shape[2]), jnp.float32)
    for tap_row in range(7):
        for tap_col in range(7):
            window = grad_pad[
                6 - tap_row : 6 - tap_row + height, 6 - tap_col : 6 - tap_col + width
            ].astype(jnp.float32)
            result = result + window * kernel[tap_row, tap_col]
    return result


def kernel_terms(grad_conv, padded, height, width):
    grad_float = grad_conv.astype(jnp.float32)
    rows_list = []
    for tap_row in range(7):
        cols_list = []
        for tap_col in range(7):
            window = padded[tap_row : tap_row + height, tap_col : tap_col + width].astype(
                jnp.float32
            )
            cols_list.append(jnp.sum(grad_float * window, axis=(0, 1)))
        rows_list.append(jnp.stack(cols_list))
    return jnp.stack(rows_list)


def gelu_tanh(value):
    return jax.nn.gelu(value, approximate=True)


def shards(feature, kernel, ln_gain, layer_scale, w_in, w_out, cotangent):
    height, width, local_ch = feature.shape
    channels = cotangent.shape[2]
    pixels = height * width
    scale = 1.0 / math.sqrt(height * lax.axis_size("rows") * width)
    offset = lax.axis_index("chan") * local_ch
    rimmed = extended(feature, (("rows", 0),), 3)
    padded = jnp.pad(rimmed, ((0, 0), (3, 3), (0, 0)))
    conv_local = conv_taps(padded, kernel, height, width).astype(jnp.bfloat16)
    conv_full = lax.all_gather(conv_local, "chan", axis=2, tiled=True)
    values = conv_full.reshape(pixels, channels).astype(jnp.float32)
    mean = jnp.mean(values, axis=1, keepdims=True)
    centred = values - mean
    var = jnp.mean(centred * centred, axis=1, keepdims=True)
    rstd = 1.0 / jnp.sqrt(var + 1e-06)
    nhat = centred * rstd
    normed = (nhat * ln_gain).astype(jnp.bfloat16)
    hidden = jnp.dot(normed, w_in, preferred_element_type=jnp.float32)
    activ = gelu_tanh(hidden).astype(jnp.bfloat16)
    grad_mixed = (cotangent.reshape(pixels, channels).astype(jnp.float32) * layer_scale).astype(
        jnp.bfloat16
    )
    grad_activ = lax.dot_general(
        grad_mixed, w_out, (((1,), (1,)), ((), ())), preferred_element_type=jnp.float32
    )
    grad_hidden = jax.vjp(gelu_tanh, hidden)[1](grad_activ)[0].astype(jnp.bfloat16)
    part_out = (
        lax.dot_general(
            activ, grad_mixed, (((0,), (0,)), ((), ())), preferred_element_type=jnp.float32
        )
        * scale
    )
    grad_w_in = lax.psum_scatter(
        (
            lax.dot_general(
                normed, grad_hidden, (((0,), (0,)), ((), ())), preferred_element_type=jnp.float32
            )
            * scale
        ).astype(jnp.bfloat16),
        "rows",
        scatter_dimension=0,
        tiled=True,
    ).astype(jnp.float32)
    grad_w_out = lax.psum_scatter(
        part_out.astype(jnp.bfloat16), "rows", scatter_dimension=1, tiled=True
    ).astype(jnp.float32)
    nhat_own = lax.dynamic_slice_in_dim(nhat, offset, local_ch, 1)
    grad_normed = lax.psum(
        lax.dot_general(
            grad_hidden, w_in, (((1,), (1,)), ((), ())), preferred_element_type=jnp.float32
        ).astype(jnp.bfloat16),
        "chan",
    ).astype(jnp.float32)
    scaled_full = grad_normed * ln_gain
    first_mean = jnp.mean(scaled_full, axis=1, keepdims=True)
    second_mean = jnp.mean(scaled_full * nhat, axis=1, keepdims=True)
    scaled = lax.dynamic_slice_in_dim(scaled_full, offset, local_ch, 1)
    grad_local = rstd * (scaled - first_mean - nhat_own * second_mean)
    grad_conv = grad_local.astype(jnp.bfloat16).reshape(height, width, local_ch)
    grad_rimmed = extended(grad_conv, (("rows", 0),), 3)
    grad_pad = jnp.pad(grad_rimmed, ((0, 0), (3, 3), (0, 0)))
    cot_own = lax.dynamic_slice_in_dim(cotangent, offset, local_ch, 2).astype(jnp.float32)
    grad_feature = (cot_own + conv_back(grad_pad, kernel, height, width)).astype(jnp.bfloat16)
    kernel_part = kernel_terms(grad_conv, padded, height, width) * scale
    grad_kernel = lax.psum(kernel_part.astype(jnp.bfloat16), "rows").astype(jnp.float32)
    return (grad_feature, grad_w_in, grad_w_out, grad_kernel)


def solution(mesh):
    placed = (
        P("rows", None, "chan"),
        P(None, None, "chan"),
        P(),
        P(),
        P(None, "chan"),
        P("chan", None),
        P("rows", None, None),
    )
    return jax.shard_map(
        shards,
        mesh=mesh,
        in_specs=placed,
        out_specs=(
            P("rows", None, "chan"),
            P("rows", "chan"),
            P("chan", "rows"),
            P(None, None, "chan"),
        ),
        check_vma=False,
    )
```

profile of v0, /device:TPU:8, one launch (start us, length us, event | category | flops | bytes accessed | tf_op | source)
XLA Modules:
  0.0 466.2 jit_solution(12585294292784050014)
XLA Ops:
  7.2 1.4 collective-permute-start.1
  8.7 3.0 collective-permute-start
  14.0 1.5 fusion.152
  18.8 3.9 fusion.143
  23.9 1.7 fusion
  26.6 2.3 fusion.153
  28.9 67.8 %all-gather.2.cloned.1.call-done = bf16[3,144,1536]{1,0,2:T(4,128)(2,1)} async-done(((bf16[3,144,192]{1,0,2:T(4,128)(2,1)}), bf16[3,144,1536]{1,0,2:T(4,128)(2,1)}) %all-gather.2.cloned.1.call-update) | async-done | bytes 1327120 | tf_op jit(solution)/shard_map/all_gather | solution.py:75
  96.7 3.6 convert_reduce_fusion
  100.4 4.0 multiply_reduce_fusion
  104.5 5.9 %copy.61 = f32[3,144,1536]{2,1,0:T(8,128)} copy(bf16[3,144,1536]{1,0,2:T(4,128)(2,1)} %all-gather.2.cloned.1.call-done) | data formatting | bytes 3981312 | tf_op jit(solution)/shard_map/convert_element_type | solution.py:76
  110.4 2.2 fusion.1
  112.7 2.8 fusion.9
  116.3 2.3 convolution_convert_fusion
  118.7 4.7 %multiply_convert_fusion = bf16[768,1536]{0,1:T(8,128)(2,1)} fusion(bf16[432,1536]{1,0:T(8,128)(2,1)} %copy-done.10, f32[432,768]{1,0:T(8,128)} %get-tuple-element.124), kind=kOutput, calls=%fused_computation.51 | convolution fusion | flops 1024561152 | bytes 5013504 | tf_op jit(solution)/shard_map/dot_general | solution.py:93
  123.7 4.8 %multiply_convert_fusion.1 = bf16[1536,768]{1,0:T(8,128)(2,1)} fusion(bf16[432,768]{1,0:T(8,128)(2,1)} %copy-done.90, f32[432,1536]{1,0:T(8,128)} %copy-done.1, f32[1536]{0:T(1024)S(1)} %copy-done.83), kind=kOutput, calls=%fused_computation.52 | convolution fusion | flops 1022902272 | bytes 5683200 | tf_op jit(solution)/shard_map/dot_general | solution.py:100
  128.5 87.3 %all-reduce.4.cloned.1.call-done = bf16[432,1536]{1,0:T(8,128)(2,1)} async-done(((bf16[432,1536]{1,0:T(8,128)(2,1)}), bf16[432,1536]{1,0:T(8,128)(2,1)}) %all-reduce.4.cloned.1.call-update) | async-done | bytes 1327120 | tf_op jit(solution)/shard_map/psum | solution.py:113
  215.8 2.9 fusion.10
  218.7 1.7 multiply_convert_fusion.7
  221.7 3.7 collective-permute-start.2
  231.6 107.0 %psum.15 = bf16[7,7,192]{2,1,0:T(8,128)(2,1)S(1)} all-reduce(bf16[7,7,192]{2,1,0:T(8,128)(2,1)S(1)} %multiply_convert_fusion.8), channel_id=1, replica_groups=mesh['rows'=32,'chan'=8] {'rows'}, use_global_device_ids=true, to_apply=%region_56.57 | all-reduce | flops 9408 | bytes 37632 | tf_op jit(solution)/shard_map/psum | solution.py:130
  340.8 7.7 %add_convert_fusion = bf16[3,144,192]{2,1,0:T(8,128)(2,1)} fusion(bf16[3,144,192]{2,1,0:T(8,128)(2,1)} %collective-permute-done.2, bf16[3,144,192]{2,1,0:T(8,128)(2,1)S(1)} %bitcast.133, bf16[3,144,192]{2,1,0:T(8,128)(2,1)} %collective-permute-done.3, bf16[9,150,192]{2,1,0:T(8,128)(2,1)S(1)} %select_maximum_fusion, f32[192]{0:T(256)S(1)} %bitcast.229, ...), kind=kLoop, calls=%fused_computation.263 | loop fusion | flops 13353984 | bytes 7834372 | tf_op jit(solution)/shard_map/convert_element_type | solution.py:128
  348.5 1.6 convert_element_type.527
  350.0 108.1 %reduce-scatter.3.cloned.1.call-done = bf16[48,768]{1,0:T(8,128)(2,1)} async-done(((bf16[1536,768]{1,0:T(8,128)(2,1)}), bf16[48,768]{1,0:T(8,128)(2,1)}) %reduce-scatter.3.cloned.1.call-update) | async-done | bytes 73744 | tf_op jit(solution)/shard_map/reduce_scatter | solution.py:98
  458.1 1.6 convert_element_type.524
  (228 shorter events, 17.6 us)
Async XLA Ops:
  7.2 89.5 %all-gather.2.cloned.1.call-start = ((), (), s32[]{:S(2)}) async-start(), calls=%async_computation.2 | async-start | bytes 3538944 | tf_op jit(solution)/shard_map/all_gather | solution.py:75
  7.2 9.5 %collective-permute-start.1 = (bf16[3,144,192]{2,1,0:T(8,128)(2,1)}, bf16[3,144,192]{2,1,0:T(8,128)(2,1)S(1)}, u32[]{:S(2)}, u32[]{:S(2)}) collective-permute-start(bf16[3,144,192]{2,1,0:T(8,128)(2,1)} %param.7), channel_id=1, source_target_pairs={{8,0},{16,8},{24,16},{32,24},{40,32},{48,40},{56,48},{64,56},{72,6... | collective-permute-start | bytes 497672 | tf_op jit(solution)/shard_map/ppermute | solution.py:19
  8.7 6.9 %collective-permute-start = (bf16[3,144,192]{2,1,0:T(8,128)(2,1)}, bf16[3,144,192]{2,1,0:T(8,128)(2,1)S(1)}, u32[]{:S(2)}, u32[]{:S(2)}) collective-permute-start(bf16[3,144,192]{2,1,0:T(8,128)(2,1)} %param.7), channel_id=1, source_target_pairs={{0,8},{8,16},{16,24},{24,32},{32,40},{40,48},{48,56},{56,64},{64,7... | collective-permute-start | bytes 497672 | tf_op jit(solution)/shard_map/ppermute | solution.py:17
  23.8 192.0 %all-reduce.4.cloned.1.call-start = ((), (), s32[]{:S(2)}) async-start(), calls=%async_computation.3 | async-start | bytes 2654208 | tf_op jit(solution)/shard_map/psum | solution.py:113
  118.7 229.8 %reduce-scatter.5.cloned.1.call-start = ((), (), s32[]{:S(2)}) async-start(), calls=%async_computation.5 | async-start | bytes 2433024 | tf_op jit(solution)/shard_map/reduce_scatter | solution.py:109
  123.5 334.7 %reduce-scatter.3.cloned.1.call-start = ((), (), s32[]{:S(2)}) async-start(), calls=%async_computation.4 | async-start | bytes 2433024 | tf_op jit(solution)/shard_map/reduce_scatter | solution.py:98
  220.4 118.8 %collective-permute-start.3 = (bf16[3,144,192]{2,1,0:T(8,128)(2,1)S(1)}, bf16[3,144,192]{2,1,0:T(8,128)(2,1)}, u32[]{:S(2)}, u32[]{:S(2)}) collective-permute-start(bf16[3,144,192]{2,1,0:T(8,128)(2,1)S(1)} %bitcast.127), channel_id=1, source_target_pairs={{8,0},{16,8},{24,16},{32,24},{40,32},{48,40},{56,48},{64,56},{72,6... | collective-permute-start | bytes 497672 | tf_op jit(solution)/shard_map/ppermute | solution.py:19
  221.7 117.5 %collective-permute-start.2 = (bf16[3,144,192]{2,1,0:T(8,128)(2,1)S(1)}, bf16[3,144,192]{2,1,0:T(8,128)(2,1)}, u32[]{:S(2)}, u32[]{:S(2)}) collective-permute-start(bf16[3,144,192]{2,1,0:T(8,128)(2,1)S(1)} %bitcast.128), channel_id=1, source_target_pairs={{0,8},{8,16},{16,24},{24,32},{32,40},{40,48},{48,56},{56,64},{64,7... | collective-permute-start | bytes 497672 | tf_op jit(solution)/shard_map/ppermute | solution.py:17
  228.9 111.6 %copy-start.14 = (f32[1,1,192]{2,1,0:T(1,128)S(1)}, f32[1,1,192]{2,1,0:T(1,128)}, u32[]{:S(2)}) copy-start(f32[1,1,192]{2,1,0:T(1,128)} %copy-done.13) | copy-start | bytes 2308
  228.9 111.6 %copy-start.16 = (f32[1,1,192]{2,1,0:T(1,128)S(1)}, f32[1,1,192]{2,1,0:T(1,128)}, u32[]{:S(2)}) copy-start(f32[1,1,192]{2,1,0:T(1,128)} %copy-done.15) | copy-start | bytes 2308
  228.9 111.6 %copy-start.18 = (f32[1,1,192]{2,1,0:T(1,128)S(1)}, f32[1,1,192]{2,1,0:T(1,128)}, u32[]{:S(2)}) copy-start(f32[1,1,192]{2,1,0:T(1,128)} %copy-done.17) | copy-start | bytes 2308
  228.9 111.6 %copy-start.20 = (f32[1,1,192]{2,1,0:T(1,128)S(1)}, f32[1,1,192]{2,1,0:T(1,128)}, u32[]{:S(2)}) copy-start(f32[1,1,192]{2,1,0:T(1,128)} %copy-done.19) | copy-start | bytes 2308
  228.9 111.6 %copy-start.22 = (f32[1,1,192]{2,1,0:T(1,128)S(1)}, f32[1,1,192]{2,1,0:T(1,128)}, u32[]{:S(2)}) copy-start(f32[1,1,192]{2,1,0:T(1,128)} %copy-done.21) | copy-start | bytes 2308
  228.9 111.6 %copy-start.24 = (f32[1,1,192]{2,1,0:T(1,128)S(1)}, f32[1,1,192]{2,1,0:T(1,128)}, u32[]{:S(2)}) copy-start(f32[1,1,192]{2,1,0:T(1,128)} %copy-done.23) | copy-start | bytes 2308
  228.9 111.6 %copy-start.26 = (f32[1,1,192]{2,1,0:T(1,128)S(1)}, f32[1,1,192]{2,1,0:T(1,128)}, u32[]{:S(2)}) copy-start(f32[1,1,192]{2,1,0:T(1,128)} %copy-done.25) | copy-start | bytes 2308
  229.0 111.6 %copy-start.28 = (f32[1,1,192]{2,1,0:T(1,128)S(1)}, f32[1,1,192]{2,1,0:T(1,128)}, u32[]{:S(2)}) copy-start(f32[1,1,192]{2,1,0:T(1,128)} %copy-done.27) | copy-start | bytes 2308
  229.0 111.6 %copy-start.30 = (f32[1,1,192]{2,1,0:T(1,128)S(1)}, f32[1,1,192]{2,1,0:T(1,128)}, u32[]{:S(2)}) copy-start(f32[1,1,192]{2,1,0:T(1,128)} %copy-done.29) | copy-start | bytes 2308
  229.0 111.6 %copy-start.32 = (f32[1,1,192]{2,1,0:T(1,128)S(1)}, f32[1,1,192]{2,1,0:T(1,128)}, u32[]{:S(2)}) copy-start(f32[1,1,192]{2,1,0:T(1,128)} %copy-done.31) | copy-start | bytes 2308
  229.0 111.6 %copy-start.34 = (f32[1,1,192]{2,1,0:T(1,128)S(1)}, f32[1,1,192]{2,1,0:T(1,128)}, u32[]{:S(2)}) copy-start(f32[1,1,192]{2,1,0:T(1,128)} %copy-done.33) | copy-start | bytes 2308
  229.0 111.6 %copy-start.36 = (f32[1,1,192]{2,1,0:T(1,128)S(1)}, f32[1,1,192]{2,1,0:T(1,128)}, u32[]{:S(2)}) copy-start(f32[1,1,192]{2,1,0:T(1,128)} %copy-done.35) | copy-start | bytes 2308
  229.0 111.6 %copy-start.38 = (f32[1,1,192]{2,1,0:T(1,128)S(1)}, f32[1,1,192]{2,1,0:T(1,128)}, u32[]{:S(2)}) copy-start(f32[1,1,192]{2,1,0:T(1,128)} %copy-done.37) | copy-start | bytes 2308
  229.0 111.6 %copy-start.40 = (f32[1,1,192]{2,1,0:T(1,128)S(1)}, f32[1,1,192]{2,1,0:T(1,128)}, u32[]{:S(2)}) copy-start(f32[1,1,192]{2,1,0:T(1,128)} %copy-done.39) | copy-start | bytes 2308
  229.0 111.6 %copy-start.42 = (f32[1,1,192]{2,1,0:T(1,128)S(1)}, f32[1,1,192]{2,1,0:T(1,128)}, u32[]{:S(2)}) copy-start(f32[1,1,192]{2,1,0:T(1,128)} %copy-done.41) | copy-start | bytes 2308
  229.0 111.6 %copy-start.44 = (f32[1,1,192]{2,1,0:T(1,128)S(1)}, f32[1,1,192]{2,1,0:T(1,128)}, u32[]{:S(2)}) copy-start(f32[1,1,192]{2,1,0:T(1,128)} %copy-done.43) | copy-start | bytes 2308
  (75 other events, 2551.2 us)
Sparse Core Ops, SparseCore 0:
  23.9 72.7 all-gather.1
  118.8 96.9 all-reduce.3
  218.5 119.5 reduce-scatter.4
  340.6 117.4 reduce-scatter.2
where the time goes:
time: 467 us; the launch traced here: 466 us
  waiting for transfers between devices  263 us (56%)
  blocking collectives  107 us (23%)
  other arithmetic  37.3 us (8%)
  matrix products  16.9 us (4%)
  local copies, waits for them, and re-layouts  16.6 us (4%)
  between operations  15.2 us (3%)
  starting transfers between devices  9.85 us (2%)
    reduce_scatter x1, waiting for transfers between devices, shards(): lax.psum_scatter((lax.dot_general(normed, grad_hidden, (((0,), (0,)), (()...  108 us
    psum x1, blocking collectives, shards(): lax.psum(kernel_part.astype(jnp.bfloat16), 'rows').astype(jnp.float32)  107 us
    psum x1, waiting for transfers between devices, shards(): lax.psum(lax.dot_general(grad_hidden, w_in, (((1,), (1,)), ((), ())), pre...  87.3 us
    all_gather x1, waiting for transfers between devices, shards(): conv_full = lax.all_gather(conv_local, 'chan', axis=2, tiled=True)  67.8 us
  transfers between devices with their start and end apart: 8, of which 3 were waited for; matrix products, arithmetic and copies ran while one was open for 8% of the time, Pallas kernels for 0%

commit v1 on v0

v1 whole, which is shorter than its diff:
```python
import math

import jax
import jax.numpy as jnp
from jax import lax
from jax.experimental import pallas as pl
from jax.experimental.pallas import tpu as pltpu
from jax.sharding import PartitionSpec as P

F32 = jnp.float32
BF16 = jnp.bfloat16

ROWS = 3
COLS = 144
PIX = ROWS * COLS
HALF = COLS // 2
CH = 192
REM = ROWS * HALF
PACK = 656
MOM = 656
PAY = 704
GRP = 48
CALL = 1536
FF = 768
MAIN = 1024


def lanes(shape):
    return lax.broadcasted_iota(jnp.int32, shape, len(shape) - 1)


def swap(x):
    return pltpu.roll(x, 64, x.ndim - 1)


def limit(mib):
    return pltpu.CompilerParams(vmem_limit_bytes=mib * 1024 * 1024)


def pack_kernel(x_ref, o_ref):
    parts = []
    low = lanes((HALF, 128)) < 64
    for i in range(ROWS):
        row = x_ref[i].astype(F32)
        o_ref[i * COLS : (i + 1) * COLS, :] = row[:, :128].astype(BF16)
        rem = jnp.concatenate([row[:, 128:], row[:, 128:]], axis=1)
        parts.append(jnp.where(low, rem[:HALF], rem[HALF:]))
    parts.append(jnp.zeros((PACK - PIX - REM, 128), F32))
    o_ref[PIX:PACK, :] = jnp.concatenate(parts, axis=0).astype(BF16)


def fill_pads(blocks, main_pad, rem_pad):
    low = lanes((8, 128)) < 64
    for n, block in enumerate(blocks):
        main = block[:PIX, :].astype(F32)
        rem = block[PIX:PACK, :].astype(F32)
        for i in range(ROWS):
            r = n * ROWS + i
            main_pad[r, 0:8, :] = jnp.zeros((8, 128), F32)
            main_pad[r, 8 : 8 + COLS, :] = main[i * COLS : (i + 1) * COLS]
            main_pad[r, 8 + COLS : 16 + COLS, :] = jnp.zeros((8, 128), F32)
            part = rem[i * HALF : (i + 1) * HALF]
            rem_pad[r, 8 : 8 + HALF, :] = part
            rem_pad[r, 0:8, :] = jnp.where(low, 0.0, swap(part[HALF - 8 :]))
            rem_pad[r, 8 + HALF : 16 + HALF, :] = jnp.where(low, swap(part[:8]), 0.0)


def taps_block(pad, k_ref, lane0, start, count, flip):
    acc = [None] * ROWS
    for b in range(7):
        for r in range(9):
            window = pad[r, start + 5 + b : start + 5 + b + count, :]
            for i in range(ROWS):
                a = r - i
                if 0 <= a <= 6:
                    tap = (6 - a) * 7 + (6 - b) if flip else a * 7 + b
                    term = window * k_ref[tap : tap + 1, lane0 : lane0 + 128]
                    acc[i] = term if acc[i] is None else acc[i] + term
    return acc


def conv_kernel(top, own, bot, k_ref, o_ref, main_pad, rem_pad):
    fill_pads((top, own, bot), main_pad, rem_pad)
    for start in range(0, COLS, 48):
        acc = taps_block(main_pad, k_ref, 0, start, 48, False)
        for i in range(ROWS):
            o_ref[i * COLS + start : i * COLS + start + 48, :] = acc[i].astype(BF16)
    parts = [[] for _ in range(ROWS)]
    for start in range(0, HALF, 24):
        acc = taps_block(rem_pad, k_ref, 128, start, 24, False)
        for i in range(ROWS):
            parts[i].append(acc[i])
    flat = [p for row in parts for p in row] + [jnp.zeros((PACK - PIX - REM, 128), F32)]
    o_ref[PIX:PACK, :] = jnp.concatenate(flat, axis=0).astype(BF16)


def back_kernel(top, own, bot, k_ref, cot_ref, o_ref, main_pad, rem_pad):
    fill_pads((top, own, bot), main_pad, rem_pad)
    for start in range(0, COLS, 48):
        acc = taps_block(main_pad, k_ref, 0, start, 48, True)
        for i in range(ROWS):
            cot = cot_ref[i, start : start + 48, :128].astype(F32)
            o_ref[i, start : start + 48, :128] = (acc[i] + cot).astype(BF16)
    parts = [[] for _ in range(ROWS)]
    for start in range(0, HALF, 24):
        acc = taps_block(rem_pad, k_ref, 128, start, 24, True)
        for i in range(ROWS):
            parts[i].append(acc[i])
    for i in range(ROWS):
        rem = jnp.concatenate(parts[i], axis=0)
        both = jnp.concatenate([rem[:, :64], swap(rem)[:, :64]], axis=0)
        cot = cot_ref[i, :, 128:].astype(F32)
        o_ref[i, :, 128:] = (both + cot).astype(BF16)


def terms_kernel(scale, grad, top, own, bot, o_ref, main_pad, rem_pad):
    fill_pads((top, own, bot), main_pad, rem_pad)
    gmain = grad[:PIX, :].astype(F32)
    grem = grad[PIX:PACK, :].astype(F32)
    for pad, part, width, base, folded in (
        (main_pad, gmain, COLS, 0, False),
        (rem_pad, grem, HALF, 56, True),
    ):
        for b in range(7):
            acc = [jnp.zeros((8, 128), F32)] * 7
            for start in range(0, width, 8):
                windows = [pad[r, start + 5 + b : start + 13 + b, :] for r in range(9)]
                for i in range(ROWS):
                    g = part[i * width + start : i * width + start + 8]
                    for a in range(7):
                        acc[a] = acc[a] + g * windows[i + a]
            for a in range(7):
                total = jnp.sum(acc[a], axis=0, keepdims=True) * scale
                if folded:
                    total = total + swap(total)
                o_ref[base + a * 7 + b : base + a * 7 + b + 1, :] = total
    for base in (49, 105):
        o_ref[base : base + 7, :] = jnp.zeros((7, 128), F32)


def first_kernel(blk, cot, scale, w_out, w_in, mixed, activ_grad, w_slot):
    mixed[...] = (cot[...].astype(F32) * scale[...]).astype(BF16)
    activ_grad[...] = lax.dot_general(
        mixed[...], w_out[...], (((1,), (1,)), ((), ())), preferred_element_type=F32
    )
    for s in range(8):
        row = pl.multiple_of(blk[s] * CH, 64)
        w_slot[128 * s : 128 * s + 128, :] = w_in[pl.ds(row, 128), :]
        row = pl.multiple_of(blk[s] * CH + 128, 64)
        w_slot[MAIN + 64 * s : MAIN + 64 * s + 64, :] = w_in[pl.ds(row, 64), :]


def gelu_pair(v):
    c = math.sqrt(2.0 / math.pi)
    square = v * v
    t = jnp.tanh(c * v * (1.0 + 0.044715 * square))
    half = 0.5 * (1.0 + t)
    slope = half + 0.5 * v * (1.0 - t * t) * (c * (1.0 + 3.0 * 0.044715 * square))
    return v * half, slope


def split_hi_lo(value):
    hi = value.astype(BF16).astype(F32)
    return hi, value - hi


def middle_kernel(*refs):
    slots = refs[:8]
    gain, w_slot, activ_grad = refs[8:11]
    normed, activ, grad_hidden, mean_ref, rstd_ref = refs[11:16]
    payloads = refs[16:24]
    x, first, second = refs[24:]
    low = lanes((HALF, 128)) < 64
    for s in range(8):
        x[:, 128 * s : 128 * s + 128] = slots[s][:PIX, :].astype(F32)
    for t in range(4):
        even = slots[2 * t][PIX:PACK, :].astype(F32)
        odd = slots[2 * t + 1][PIX:PACK, :].astype(F32)
        at = MAIN + 128 * t
        for i in range(ROWS):
            e = even[i * HALF : (i + 1) * HALF]
            o = odd[i * HALF : (i + 1) * HALF]
            x[i * COLS : i * COLS + HALF, at : at + 128] = jnp.where(low, e, swap(o))
            x[i * COLS + HALF : (i + 1) * COLS, at : at + 128] = jnp.where(low, swap(e), o)
    for start in range(0, PIX, GRP):
        rows = slice(start, start + GRP)
        values = x[rows, :]
        mean = jnp.sum(values, axis=1, keepdims=True) * (1.0 / CALL)
        centred = values - mean
        var = jnp.sum(centred * centred, axis=1, keepdims=True) * (1.0 / CALL)
        rstd = 1.0 / jnp.sqrt(var + 1e-06)
        nhat = centred * rstd
        x[rows, :] = nhat
        normed[rows, :] = (nhat * gain[...]).astype(BF16)
        mean_ref[rows, :] = jnp.broadcast_to(mean, (GRP, 128))
        rstd_ref[rows, :] = jnp.broadcast_to(rstd, (GRP, 128))
    for n in range(0, FF, 256):
        hidden = jnp.dot(normed[...], w_slot[:, n : n + 256], preferred_element_type=F32)
        value, slope = gelu_pair(hidden)
        activ[:, n : n + 256] = value.astype(BF16)
        grad_hidden[:, n : n + 256] = (activ_grad[:, n : n + 256] * slope).astype(BF16)
    for t in range(4):
        for at, kind in ((256 * t, 0), (MAIN + 128 * t, 1)):
            width = 128 if kind else 256
            part = lax.dot_general(
                grad_hidden[...],
                w_slot[at : at + width, :],
                (((1,), (1,)), ((), ())),
                preferred_element_type=F32,
            )
            scaled = part * gain[:, at : at + width]
            cross = scaled * x[:, at : at + width]
            if kind == 0:
                scaled = scaled[:, :128] + scaled[:, 128:]
                cross = cross[:, :128] + cross[:, 128:]
                payloads[2 * t][:PIX, :] = part[:, :128].astype(BF16)
                payloads[2 * t + 1][:PIX, :] = part[:, 128:].astype(BF16)
            else:
                evens, odds = [], []
                for i in range(ROWS):
                    l = part[i * COLS : i * COLS + HALF]
                    r = part[i * COLS + HALF : (i + 1) * COLS]
                    evens.append(jnp.where(low, l, swap(r)))
                    odds.append(jnp.where(low, swap(l), r))
                tail = [jnp.zeros((PACK - PIX - REM, 128), F32)]
                payloads[2 * t][PIX:PACK, :] = jnp.concatenate(evens + tail).astype(BF16)
                payloads[2 * t + 1][PIX:PACK, :] = jnp.concatenate(odds + tail).astype(BF16)
            if t == 0 and kind == 0:
                first[...] = scaled
                second[...] = cross
            else:
                first[...] += scaled
                second[...] += cross
    lane = lanes((GRP, 128))
    moments = jnp.zeros((GRP, 128), F32)
    for g in range(PIX // GRP):
        rows = slice(g * GRP, (g + 1) * GRP)
        for q, ref in enumerate((first, second)):
            value = jnp.sum(ref[rows, :], axis=1, keepdims=True) * (1.0 / CALL)
            hi, lo = split_hi_lo(value)
            moments = jnp.where(lane == 32 * q + g, hi, moments)
            moments = jnp.where(lane == 32 * q + 16 + g, lo, moments)
    moments = moments.astype(BF16)
    for s in range(8):
        payloads[s][MOM:PAY, :] = moments


def sum_kernel(a, b, c, d, o_ref):
    total = a[...].astype(F32) + b[...].astype(F32) + c[...].astype(F32) + d[...].astype(F32)
    o_ref[:MOM, :] = total[:MOM].astype(BF16)
    moments = total[MOM:]
    whole = moments + pltpu.roll(moments, 128 - 16, 1)
    hi, lo = split_hi_lo(whole)
    low = (lanes((GRP, 128)) & 31) < 16
    o_ref[MOM:, :] = jnp.where(low, hi, pltpu.roll(lo, 16, 1)).astype(BF16)


def norm_back_kernel(a, b, c, d, e, conv, mean_ref, rstd_ref, gain, o_ref):
    refs = (a, b, c, d, e)
    total = sum(ref[...].astype(F32) for ref in refs[1:]) + a[...].astype(F32)
    moments = total[MOM:]
    whole = moments + pltpu.roll(moments, 128 - 16, 1)
    firsts, seconds = [], []
    for g in range(PIX // GRP):
        firsts.append(jnp.broadcast_to(whole[:, g : g + 1], (GRP, 128)))
        seconds.append(jnp.broadcast_to(whole[:, 32 + g : 33 + g], (GRP, 128)))
    first = jnp.concatenate(firsts)
    second = jnp.concatenate(seconds)
    mean = mean_ref[...]
    rstd = rstd_ref[...]
    main = rstd * (
        total[:PIX] * gain[0:1, :] - first - (conv[:PIX, :].astype(F32) - mean) * rstd * second
    )
    o_ref[:PIX, :] = main.astype(BF16)
    low = lanes((HALF, 128)) < 64

    def folded(v):
        return jnp.concatenate(
            [
                jnp.where(low, v[i * COLS : i * COLS + HALF], v[i * COLS + HALF : (i + 1) * COLS])
                for i in range(ROWS)
            ]
        )

    mean, rstd, first, second = folded(mean), folded(rstd), folded(first), folded(second)
    crem = conv[PIX:PACK, :].astype(F32)[:REM]
    rem = rstd * (total[PIX : PIX + REM] * gain[1:2, :] - first - (crem - mean) * rstd * second)
    rem = jnp.concatenate([rem, jnp.zeros((PACK - PIX - REM, 128), F32)])
    o_ref[PIX:PACK, :] = rem.astype(BF16)


def weights_kernel(scale, blk, place, normed, grad_hidden, activ, mixed, keep, send):
    own = place[0] == 0

    def put(z, w, xlo, rows, zero, one):
        zero, one = zero.astype(BF16), one.astype(BF16)
        keep[z, w, xlo, rows, :] = jnp.where(own, zero, one)
        send[z, w, xlo, rows, :] = jnp.where(own, one, zero)

    def product(left, right):
        return (
            lax.dot_general(left, right, (((0,), (0,)), ((), ())), preferred_element_type=F32)
            * scale
        )

    every = slice(0, 48)
    for t in range(4):
        part = product(mixed[:, 384 * t : 384 * t + 384], activ[...])
        for n in range(2):
            p = part[192 * n : 192 * n + 192]
            put(2 * t + n, 1, 0, every, p[0:48], p[48:96])
            put(2 * t + n, 1, 1, every, p[96:144], p[144:192])
    for t in range(4):
        part = product(normed[:, 256 * t : 256 * t + 256], grad_hidden[...])
        rest = product(normed[:, MAIN + 128 * t : MAIN + 128 * t + 128], grad_hidden[...])
        for n in range(2):
            p = part[128 * n : 128 * n + 128]
            q = rest[64 * n : 64 * n + 64]
            z = blk[2 * t + n]
            put(z, 0, 0, every, p[0:48], p[48:96])
            put(z, 0, 1, every, jnp.concatenate([p[96:128], q[0:16]]), q[16:64])


def call(kernel, outs, args, scratch=(), mib=32, smem=0, flops=0, moved=0):
    space = [pl.BlockSpec(memory_space=pltpu.SMEM)] * smem
    space += [pl.BlockSpec(memory_space=pltpu.VMEM)] * (len(args) - smem)
    single = not isinstance(outs, (list, tuple))
    shapes = [outs] if single else list(outs)
    result = pl.pallas_call(
        kernel,
        out_shape=shapes,
        in_specs=space,
        out_specs=[pl.BlockSpec(memory_space=pltpu.VMEM)] * len(shapes),
        scratch_shapes=list(scratch),
        compiler_params=limit(mib),
        cost_estimate=pl.CostEstimate(flops=flops, bytes_accessed=moved, transcendentals=0),
    )(*args)
    return result[0] if single else result


def shape(dims, dtype):
    return jax.ShapeDtypeStruct(dims, dtype)


def pads():
    return [pltpu.VMEM((9, COLS + 16, 128), F32), pltpu.VMEM((9, HALF + 16, 128), F32)]


def rows_perm(f):
    return [(i, f(i)) for i in range(32)]


def chan_shift(k, x):
    return [(i, ((i // 2 + k) % 4) * 2 + ((i % 2) ^ x)) for i in range(8)]


def halos(block):
    above = lax.ppermute(block, "rows", [(i, i + 1) for i in range(31)])
    below = lax.ppermute(block, "rows", [(i + 1, i) for i in range(31)])
    return above, below


def shards(feature, kernel, ln_gain, layer_scale, w_in, w_out, cotangent):
    scale = 1.0 / math.sqrt(32 * PIX)
    me = lax.axis_index("chan")
    row = lax.axis_index("rows")
    my_y, my_x = me // 2, me % 2
    slots = [(k, x) for k in range(4) for x in range(2)]
    blk = jnp.stack([((my_y + k) % 4) * 2 + (my_x ^ x) for k, x in slots]).astype(jnp.int32)
    place = jnp.stack([row % 2, (row // 2) % 2]).astype(jnp.int32)

    packed = call(pack_kernel, shape((PACK, 128), BF16), [feature])
    above, below = halos(packed)
    taps = kernel.reshape(49, CH)
    taps = jnp.concatenate([taps[:, :128], taps[:, 128:], taps[:, 128:]], axis=1)
    cot = cotangent.reshape(PIX, CALL)
    mixed, activ_grad, w_slot = call(
        first_kernel,
        [shape((PIX, CALL), BF16), shape((PIX, FF), F32), shape((CALL, FF), BF16)],
        [blk, cot, layer_scale.reshape(1, CALL), w_out, w_in],
        smem=1,
        flops=2 * PIX * CALL * FF,
        moved=8 << 20,
    )
    gains = ln_gain.reshape(8, CH)[blk]
    gain_slot = jnp.concatenate([gains[:, :128].reshape(1, -1), gains[:, 128:].reshape(1, -1)], axis=1)
    gain_own = jnp.stack([gains[0, :128], jnp.concatenate([gains[0, 128:], gains[0, 128:]])])
    cot_own = lax.dynamic_slice_in_dim(cotangent, me * CH, CH, 2)

    conv = call(
        conv_kernel, shape((PACK, 128), BF16), [above, packed, below, taps], pads(), flops=1 << 23, moved=1 << 20
    )

    def shift(block, k, x):
        return lax.ppermute(block, "chan", chan_shift(k, x))

    partner = shift(conv, 0, 1)
    gathered = {(0, 0): conv, (0, 1): partner}
    for k in (1, 3, 2):
        gathered[(4 - k) % 4, 0] = shift(conv, k, 0)
    for k in (1, 3, 2):
        gathered[(4 - k) % 4, 1] = shift(partner, k, 0)

    outs = call(
        middle_kernel,
        [
            shape((PIX, CALL), BF16),
            shape((PIX, FF), BF16),
            shape((PIX, FF), BF16),
            shape((PIX, 128), F32),
            shape((PIX, 128), F32),
        ]
        + [shape((PAY, 128), BF16)] * 8,
        [gathered[s] for s in slots] + [gain_slot, w_slot, activ_grad],
        [pltpu.VMEM((PIX, CALL), F32), pltpu.VMEM((PIX, 128), F32), pltpu.VMEM((PIX, 128), F32)],
        mib=40,
        flops=4 * PIX * CALL * FF,
        moved=8 << 20,
    )
    normed, activ, grad_hidden, mean, rstd = outs[:5]
    payload = dict(zip(slots, outs[5:]))

    other = [shift(payload[k, 1], k, 0) for k in (1, 3, 2)]
    mine = [shift(payload[k, 0], k, 0) for k in (1, 3, 2)]
    other_sum = call(sum_kernel, shape((PAY, 128), BF16), [payload[0, 1]] + other, moved=1 << 20)
    crossed = shift(other_sum, 0, 1)

    keep, send = call(
        lambda *refs: weights_kernel(scale, *refs),
        [shape((8, 2, 2, 48, FF), BF16)] * 2,
        [blk, place, normed, grad_hidden, activ, mixed],
        smem=2,
        mib=48,
        flops=4 * PIX * CALL * FF,
        moved=8 << 20,
    )
    got = lax.ppermute(send, "rows", rows_perm(lambda i: i ^ 1))
    both = (keep.astype(F32) + got.astype(F32)).astype(BF16).reshape(8, 192, FF)
    z_groups = [[z * 4 + q for z in range(8)] for q in range(4)]
    z_sum = lax.psum_scatter(
        both, "rows", scatter_dimension=0, axis_index_groups=z_groups, tiled=True
    ).reshape(2, 2, 48, FF)

    grad_conv = call(
        norm_back_kernel,
        shape((PACK, 128), BF16),
        [payload[0, 0]] + mine + [crossed, conv, mean, rstd, gain_own],
        moved=2 << 20,
    )
    grad_above, grad_below = halos(grad_conv)
    terms = call(
        lambda *refs: terms_kernel(scale, *refs),
        shape((112, 128), F32),
        [grad_conv, above, packed, below],
        pads(),
        flops=1 << 23,
        moved=1 << 20,
    )
    for f in (
        lambda i: i ^ 1,
        lambda i: i ^ 2,
        lambda i: i ^ 4,
        lambda i: i ^ 8,
        lambda i: i ^ 16,
    ):
        terms = terms + lax.ppermute(terms, "rows", rows_perm(f))
    grad_kernel = jnp.concatenate([terms[:49], terms[56:105, :64]], axis=1).reshape(7, 7, CH)

    grad_feature = call(
        back_kernel,
        shape((ROWS, COLS, CH), BF16),
        [grad_above, grad_conv, grad_below, taps, cot_own],
        pads(),
        flops=1 << 23,
        moved=1 << 20,
    )

    my_lo = place[1]
    away = lax.dynamic_index_in_dim(z_sum, 1 - my_lo, 1, keepdims=False)
    held = lax.dynamic_index_in_dim(z_sum, my_lo, 1, keepdims=False)
    final = held.astype(F32) + lax.ppermute(away, "rows", rows_perm(lambda i: i ^ 2)).astype(F32)
    return grad_feature, final[0], final[1].T, grad_kernel


def solution(mesh):
    placed = (
        P("rows", None, "chan"),
        P(None, None, "chan"),
        P(),
        P(),
        P(None, "chan"),
        P("chan", None),
        P("rows", None, None),
    )
    return jax.shard_map(
        shards,
        mesh=mesh,
        in_specs=placed,
        out_specs=(
            P("rows", None, "chan"),
            P("rows", "chan"),
            P("chan", "rows"),
            P(None, None, "chan"),
        ),
        check_vma=False,
    )
```

time: 467 us -> 132 us (0.28)
  the two profiles are of different devices: /device:TPU:8 before, /device:TPU:24 now
where the time goes in v1:
time: 132 us; the launch traced here: 131 us
  starting transfers between devices  47.1 us (36%)
  waiting for transfers between devices  35.4 us (27%)
  Pallas kernels  18.2 us (14%)
  between operations  14.4 us (11%)
  local copies, waits for them, and re-layouts  12 us (9%)
  other arithmetic  4.24 us (3%)
    ppermute x14, starting transfers between devices, shift(): return lax.ppermute(block, 'chan', chan_shift(k, x))  22 us
    ppermute x14, waiting for transfers between devices, shift(): return lax.ppermute(block, 'chan', chan_shift(k, x))  21.1 us
    ppermute x5, starting transfers between devices, shards(): terms = terms + lax.ppermute(terms, 'rows', rows_perm(f))  18.4 us
    pallas_call x9, Pallas kernels, call(): pl.pallas_call(kernel, out_shape=shapes, in_specs=space, out_specs=[pl.Bl...  18.2 us
    ppermute x5, waiting for transfers between devices, shards(): terms = terms + lax.ppermute(terms, 'rows', rows_perm(f))  7.75 us
    unnamed x16, local copies, waits for them, and re-layouts  6.4 us
    ppermute x1, waiting for transfers between devices, shards(): got = lax.ppermute(send, 'rows', rows_perm(lambda i: i ^ 1))  4.37 us
    convert_element_type x1, other arithmetic, shards(): both = (keep.astype(F32) + got.astype(F32)).astype(BF16).reshape(8, 192, FF)  3.89 us
  transfers between devices with their start and end apart: 26, of which 14 were waited for; matrix products, arithmetic and copies ran while one was open for 4% of the time, Pallas kernels for 5%

profile of v1, /device:TPU:24, one launch (start us, length us, event | category | flops | bytes accessed | tf_op | source)
XLA Modules:
  0.0 131.5 jit_solution(5318280115802591773)
XLA Ops:
  8.4 1.7 %collective-permute-start = (bf16[656,128]{1,0:T(8,128)(2,1)S(1)}, bf16[656,128]{1,0:T(8,128)(2,1)S(1)}, u32[]{:S(2)}, u32[]{:S(2)}) collective-permute-start(bf16[656,128]{1,0:T(8,128)(2,1)S(1)} %shard_map.102.own.refs_2_), channel_id=1, source_target_pairs={{0,8},{8,16},{16,24},{24,32},{32,40},{40,48},{48,56},{56,64},{64,7... | collective-permute-start | bytes 503816 | tf_op jit(solution)/shard_map/ppermute | solution.py:358
  16.3 3.1 %collective-permute-start.2 = (bf16[656,128]{1,0:T(8,128)(2,1)S(1)}, bf16[656,128]{1,0:T(8,128)(2,1)S(1)}, u32[]{:S(2)}, u32[]{:S(2)}) collective-permute-start(bf16[656,128]{1,0:T(8,128)(2,1)S(1)} %shard_map.103.refs_0_.conv), channel_id=1, source_target_pairs={{0,1},{1,0},{2,3},{3,2},{4,5},{5,4},{6,7},{7,6},{8,9},{9,8},{10,11... | collective-permute-start | bytes 503816 | tf_op jit(solution)/shard_map/ppermute | solution.py:395
  21.1 2.2 %collective-permute-start.7 = (bf16[656,128]{1,0:T(8,128)(2,1)S(1)}, bf16[656,128]{1,0:T(8,128)(2,1)S(1)}, u32[]{:S(2)}, u32[]{:S(2)}) collective-permute-start(bf16[656,128]{1,0:T(8,128)(2,1)S(1)} %shard_map.103.refs_0_.conv), channel_id=1, source_target_pairs={{0,2},{1,3},{2,4},{3,5},{4,6},{5,7},{6,0},{7,1},{8,10},{9,11},{10,... | collective-permute-start | bytes 503816 | tf_op jit(solution)/shard_map/ppermute | solution.py:395
  28.3 1.7 %copy-done = bf16[768,1536]{1,0:T(8,128)(2,1)S(1)} copy-done((bf16[768,1536]{1,0:T(8,128)(2,1)S(1)}, bf16[768,1536]{1,0:T(8,128)(2,1)}, u32[]{:S(2)}) %copy-start) | copy-done | bytes 2359320
  31.6 1.9 %shard_map.104 = (bf16[432,1536]{1,0:T(8,128)(2,1)S(1)}, f32[432,768]{1,0:T(8,128)S(1)}, bf16[1536,768]{1,0:T(8,128)(2,1)S(1)}) custom-call(s32[8]{0:T(128)S(1)} %stack.77.blk.refs_0_, bf16[432,1536]{1,0:T(8,128)(2,1)S(1)} %bitcast.39, f32[1,1536]{1,0:T(1,128)S(1)} %reshape.355.scale, bf16[768,1536]{1,0:T(8,128)(2,1)S(1)} %copy-done, ...), custom_call_target="tpu_custom_call" | custom-call | flops 1019215872 | bytes 8388608 | tf_op jit(solution)/shard_map/pallas_call | solution.py:329
  33.6 4.1 %collective-permute-done.4.refs_3_ = bf16[656,128]{1,0:T(8,128)(2,1)S(1)} collective-permute-done((bf16[656,128]{1,0:T(8,128)(2,1)S(1)}, bf16[656,128]{1,0:T(8,128)(2,1)S(1)}, u32[]{:S(2)}, u32[]{:S(2)}) %collective-permute-start.4) | collective-permute-done | bytes 167968 | tf_op jit(solution)/shard_map/ppermute | solution.py:395
  38.3 5.2 %shard_map.105 = (bf16[432,1536]{1,0:T(8,128)(2,1)S(1)}, bf16[432,768]{1,0:T(8,128)(2,1)S(1)}, bf16[432,768]{1,0:T(8,128)(2,1)S(1)}, f32[432,128]{1,0:T(8,128)S(...) custom-call(bf16[656,128]{1,0:T(8,128)(2,1)S(1)} %shard_map.103.refs, ...), custom_call_target="tpu_custom_call" | custom-call | flops 2038431744 | bytes 8388608 | tf_op jit(solution)/shard_map/pallas_call | solution.py:329
  45.5 5.5 %shard_map.109 = (bf16[8,2,2,48,768]{4,3,2,1,0:T(8,128)(2,1)}, bf16[8,2,2,48,768]{4,3,2,1,0:T(8,128)(2,1)}) custom-call(s32[8]{0:T(128)S(1)} %stack.77.blk.refs_0_, s32[2]{0:T(128)S(1)} %pad_add_fusion.refs_1_, bf16[432,1536]{1,0:T(8,128)(2,1)S(1)} %get-tuple-element.34.refs_2_, bf16[432,768]{1,0:T(8,128)(2,1)S(1)} %get-tuple-element.35.refs_3_, ...), custom_call_target="tpu_custom_call" | custom-call | flops 2038431744 | bytes 8388608 | tf_op jit(solution)/shard_map/pallas_call | solution.py:329
  52.0 4.4 %collective-permute-done.18 = bf16[8,2,2,48,768]{4,3,2,1,0:T(8,128)(2,1)S(1)} collective-permute-done((bf16[8,2,2,48,768]{4,3,2,1,0:T(8,128)(2,1)}, bf16[8,2,2,48,768]{4,3,2,1,0:T(8,128)(2,1)S(1)}, u32[]{:S(2)}, u32[]{:S(2)}) %collective-permute-start.18) | collective-permute-done | bytes 2359328 | tf_op jit(solution)/shard_map/ppermute | solution.py:437
  56.4 3.9 %add_convert_fusion = bf16[8,2,2,48,768]{4,3,2,1,0:T(8,128)(2,1)} fusion(bf16[8,2,2,48,768]{4,3,2,1,0:T(8,128)(2,1)S(1)} %collective-permute-done.18, bf16[8,2,2,48,768]{4,3,2,1,0:T(8,128)(2,1)} %get-tuple-element.38), kind=kLoop, calls=%fused_computation.1 | loop fusion | flops 4718592 | bytes 7077888 | tf_op jit(solution)/shard_map/convert_element_type | solution.py:438
  60.3 3.1 %collective-permute-start.12 = (bf16[704,128]{1,0:T(8,128)(2,1)}, bf16[704,128]{1,0:T(8,128)(2,1)S(1)}, u32[]{:S(2)}, u32[]{:S(2)}) collective-permute-start(bf16[704,128]{1,0:T(8,128)(2,1)} %copy-done.6), channel_id=1, source_target_pairs={{0,2},{1,3},{2,4},{3,5},{4,6},{5,7},{6,0},{7,1},{8,10},{9,11},{10,... | collective-permute-start | bytes 540680 | tf_op jit(solution)/shard_map/ppermute | solution.py:395
  65.0 2.5 %collective-permute-start.10 = (bf16[704,128]{1,0:T(8,128)(2,1)S(1)}, bf16[704,128]{1,0:T(8,128)(2,1)S(1)}, u32[]{:S(2)}, u32[]{:S(2)}) collective-permute-start(bf16[704,128]{1,0:T(8,128)(2,1)S(1)} %get-tuple-element.26), channel_id=1, source_target_pairs={{0,6},{1,7},{2,0},{3,1},{4,2},{5,3},{6,4},{7,5},{8,14},{9,15},{10,... | collective-permute-start | bytes 540680 | tf_op jit(solution)/shard_map/ppermute | solution.py:395
  68.1 7.8 %collective-permute-done.12.b = bf16[704,128]{1,0:T(8,128)(2,1)S(1)} collective-permute-done((bf16[704,128]{1,0:T(8,128)(2,1)}, bf16[704,128]{1,0:T(8,128)(2,1)S(1)}, u32[]{:S(2)}, u32[]{:S(2)}) %collective-permute-start.12) | collective-permute-done | bytes 180256 | tf_op jit(solution)/shard_map/ppermute | solution.py:395
  76.0 3.9 %collective-permute-start.9 = (bf16[704,128]{1,0:T(8,128)(2,1)S(1)}, bf16[704,128]{1,0:T(8,128)(2,1)S(1)}, u32[]{:S(2)}, u32[]{:S(2)}) collective-permute-start(bf16[704,128]{1,0:T(8,128)(2,1)S(1)} %get-tuple-element.25), channel_id=1, source_target_pairs={{0,2},{1,3},{2,4},{3,5},{4,6},{5,7},{6,0},{7,1},{8,10},{9,11},{10,... | collective-permute-start | bytes 540680 | tf_op jit(solution)/shard_map/ppermute | solution.py:395
  80.3 2.4 %collective-permute-done.10.c = bf16[704,128]{1,0:T(8,128)(2,1)S(1)} collective-permute-done((bf16[704,128]{1,0:T(8,128)(2,1)S(1)}, bf16[704,128]{1,0:T(8,128)(2,1)S(1)}, u32[]{:S(2)}, u32[]{:S(2)}) %collective-permute-start.10) | collective-permute-done | bytes 180256 | tf_op jit(solution)/shard_map/ppermute | solution.py:395
  82.9 4.3 %collective-permute-done.15.e = bf16[704,128]{1,0:T(8,128)(2,1)S(1)} collective-permute-done((bf16[704,128]{1,0:T(8,128)(2,1)S(1)}, bf16[704,128]{1,0:T(8,128)(2,1)S(1)}, u32[]{:S(2)}, u32[]{:S(2)}) %collective-permute-start.15) | collective-permute-done | bytes 180256 | tf_op jit(solution)/shard_map/ppermute | solution.py:395
  90.2 3.3 %collective-permute-start.21 = (f32[112,128]{1,0:T(8,128)S(1)}, f32[112,128]{1,0:T(8,128)S(1)}, u32[]{:S(2)}, u32[]{:S(2)}) collective-permute-start(f32[112,128]{1,0:T(8,128)S(1)} %add.132), channel_id=1, source_target_pairs={{0,16},{8,24},{16,0},{24,8},{32,48},{40,56},{48,32},{56,40},{64,80... | collective-permute-start | bytes 172040 | tf_op jit(solution)/shard_map/ppermute | solution.py:466
  93.5 2.2 %collective-permute-done.21 = f32[112,128]{1,0:T(8,128)S(1)} collective-permute-done((f32[112,128]{1,0:T(8,128)S(1)}, f32[112,128]{1,0:T(8,128)S(1)}, u32[]{:S(2)}, u32[]{:S(2)}) %collective-permute-start.21) | collective-permute-done | bytes 57376 | tf_op jit(solution)/shard_map/ppermute | solution.py:466
  95.7 2.9 %collective-permute-start.22 = (f32[112,128]{1,0:T(8,128)S(1)}, f32[112,128]{1,0:T(8,128)S(1)}, u32[]{:S(2)}, u32[]{:S(2)}) collective-permute-start(f32[112,128]{1,0:T(8,128)S(1)} %add.133), channel_id=1, source_target_pairs={{0,32},{8,40},{16,48},{24,56},{32,0},{40,8},{48,16},{56,24},{64,96... | collective-permute-start | bytes 172040 | tf_op jit(solution)/shard_map/ppermute | solution.py:466
  98.6 3.5 %collective-permute-done.22 = f32[112,128]{1,0:T(8,128)S(1)} collective-permute-done((f32[112,128]{1,0:T(8,128)S(1)}, f32[112,128]{1,0:T(8,128)S(1)}, u32[]{:S(2)}, u32[]{:S(2)}) %collective-permute-start.22) | collective-permute-done | bytes 57376 | tf_op jit(solution)/shard_map/ppermute | solution.py:466
  102.1 3.2 %collective-permute-start.23 = (f32[112,128]{1,0:T(8,128)S(1)}, f32[112,128]{1,0:T(8,128)S(1)}, u32[]{:S(2)}, u32[]{:S(2)}) collective-permute-start(f32[112,128]{1,0:T(8,128)S(1)} %add.134), channel_id=1, source_target_pairs={{0,64},{8,72},{16,80},{24,88},{32,96},{40,104},{48,112},{56,120},{... | collective-permute-start | bytes 172040 | tf_op jit(solution)/shard_map/ppermute | solution.py:466
  108.8 8.9 %collective-permute-start.24 = (f32[112,128]{1,0:T(8,128)S(1)}, f32[112,128]{1,0:T(8,128)S(1)}, u32[]{:S(2)}, u32[]{:S(2)}) collective-permute-start(f32[112,128]{1,0:T(8,128)S(1)} %add.135), channel_id=1, source_target_pairs={{0,128},{8,136},{16,144},{24,152},{32,160},{40,168},{48,176},{56,1... | collective-permute-start | bytes 172040 | tf_op jit(solution)/shard_map/ppermute | solution.py:466
  118.9 2.1 %shard_map.108 = bf16[3,144,192]{2,1,0:T(8,128)(2,1)} custom-call(bf16[656,128]{1,0:T(8,128)(2,1)S(1)} %collective-permute-done.16.top, bf16[656,128]{1,0:T(8,128)(2,1)S(1)} %shard_map.107.own.refs_0_, bf16[656,128]{1,0:T(8,128)(2,1)S(1)} %collective-permute-done.17.bot, f32[49,256]{1,0:T(8,128)S(1)} %pad_maximum_fusion.k_ref, ...), custom_call_target="tpu_custom_call" | custom-call | flops 8388608 | bytes 1048576 | tf_op jit(solution)/shard_map/pallas_call | solution.py:329
  121.7 2.1 %collective-permute-done.19 = bf16[2,48,768]{2,1,0:T(8,128)(2,1)S(1)} collective-permute-done((bf16[2,48,768]{2,1,0:T(8,128)(2,1)S(1)}, bf16[2,48,768]{2,1,0:T(8,128)(2,1)S(1)}, u32[]{:S(2)}, u32[]{:S(2)}) %collective-permute-start.19) | collective-permute-done | bytes 147488 | tf_op jit(solution)/shard_map/ppermute | solution.py:481
  (87 shorter events, 31.0 us)
Async XLA Ops:
  7.2 110.4 %reduce-scatter.2.cloned.1.call-start = ((), (), s32[]{:S(2)}) async-start(), calls=%async_computation.1 | async-start | bytes 2654208 | tf_op jit(solution)/shard_map/reduce_scatter | solution.py:440
  8.4 6.5 %collective-permute-start = (bf16[656,128]{1,0:T(8,128)(2,1)S(1)}, bf16[656,128]{1,0:T(8,128)(2,1)S(1)}, u32[]{:S(2)}, u32[]{:S(2)}) collective-permute-start(bf16[656,128]{1,0:T(8,128)(2,1)S(1)} %shard_map.102.own.refs_2_), channel_id=1, source_target_pairs={{0,8},{8,16},{16,24},{24,32},{32,40},{40,48},{48,56},{56,64},{64,7... | collective-permute-start | bytes 503816 | tf_op jit(solution)/shard_map/ppermute | solution.py:358
  16.3 8.0 %collective-permute-start.2 = (bf16[656,128]{1,0:T(8,128)(2,1)S(1)}, bf16[656,128]{1,0:T(8,128)(2,1)S(1)}, u32[]{:S(2)}, u32[]{:S(2)}) collective-permute-start(bf16[656,128]{1,0:T(8,128)(2,1)S(1)} %shard_map.103.refs_0_.conv), channel_id=1, source_target_pairs={{0,1},{1,0},{2,3},{3,2},{4,5},{5,4},{6,7},{7,6},{8,9},{9,8},{10,11... | collective-permute-start | bytes 503816 | tf_op jit(solution)/shard_map/ppermute | solution.py:395
  19.4 7.7 %collective-permute-start.3 = (bf16[656,128]{1,0:T(8,128)(2,1)S(1)}, bf16[656,128]{1,0:T(8,128)(2,1)S(1)}, u32[]{:S(2)}, u32[]{:S(2)}) collective-permute-start(bf16[656,128]{1,0:T(8,128)(2,1)S(1)} %shard_map.103.refs_0_.conv), channel_id=1, source_target_pairs={{0,6},{1,7},{2,0},{3,1},{4,2},{5,3},{6,4},{7,5},{8,14},{9,15},{10,... | collective-permute-start | bytes 503816 | tf_op jit(solution)/shard_map/ppermute | solution.py:395
  20.2 13.4 %collective-permute-start.5 = (bf16[656,128]{1,0:T(8,128)(2,1)S(1)}, bf16[656,128]{1,0:T(8,128)(2,1)S(1)}, u32[]{:S(2)}, u32[]{:S(2)}) collective-permute-start(bf16[656,128]{1,0:T(8,128)(2,1)S(1)} %shard_map.103.refs_0_.conv), channel_id=1, source_target_pairs={{0,4},{1,5},{2,6},{3,7},{4,0},{5,1},{6,2},{7,3},{8,12},{9,13},{10,... | collective-permute-start | bytes 503816 | tf_op jit(solution)/shard_map/ppermute | solution.py:395
  21.1 12.5 %collective-permute-start.7 = (bf16[656,128]{1,0:T(8,128)(2,1)S(1)}, bf16[656,128]{1,0:T(8,128)(2,1)S(1)}, u32[]{:S(2)}, u32[]{:S(2)}) collective-permute-start(bf16[656,128]{1,0:T(8,128)(2,1)S(1)} %shard_map.103.refs_0_.conv), channel_id=1, source_target_pairs={{0,2},{1,3},{2,4},{3,5},{4,6},{5,7},{6,0},{7,1},{8,10},{9,11},{10,... | collective-permute-start | bytes 503816 | tf_op jit(solution)/shard_map/ppermute | solution.py:395
  24.3 13.3 %collective-permute-start.4 = (bf16[656,128]{1,0:T(8,128)(2,1)S(1)}, bf16[656,128]{1,0:T(8,128)(2,1)S(1)}, u32[]{:S(2)}, u32[]{:S(2)}) collective-permute-start(bf16[656,128]{1,0:T(8,128)(2,1)S(1)} %collective-permute-done.2.refs_1_), channel_id=1, source_target_pairs={{0,6},{1,7},{2,0},{3,1},{4,2},{5,3},{6,4},{7,5},{8,14},{9,15},{10,... | collective-permute-start | bytes 503816 | tf_op jit(solution)/shard_map/ppermute | solution.py:395
  25.1 12.6 %collective-permute-start.6 = (bf16[656,128]{1,0:T(8,128)(2,1)S(1)}, bf16[656,128]{1,0:T(8,128)(2,1)S(1)}, u32[]{:S(2)}, u32[]{:S(2)}) collective-permute-start(bf16[656,128]{1,0:T(8,128)(2,1)S(1)} %collective-permute-done.2.refs_1_), channel_id=1, source_target_pairs={{0,4},{1,5},{2,6},{3,7},{4,0},{5,1},{6,2},{7,3},{8,12},{9,13},{10,... | collective-permute-start | bytes 503816 | tf_op jit(solution)/shard_map/ppermute | solution.py:395
  27.1 11.1 %collective-permute-start.8 = (bf16[656,128]{1,0:T(8,128)(2,1)S(1)}, bf16[656,128]{1,0:T(8,128)(2,1)S(1)}, u32[]{:S(2)}, u32[]{:S(2)}) collective-permute-start(bf16[656,128]{1,0:T(8,128)(2,1)S(1)} %collective-permute-done.2.refs_1_), channel_id=1, source_target_pairs={{0,2},{1,3},{2,4},{3,5},{4,6},{5,7},{6,0},{7,1},{8,10},{9,11},{10,... | collective-permute-start | bytes 503816 | tf_op jit(solution)/shard_map/ppermute | solution.py:395
  51.0 5.4 %collective-permute-start.18 = (bf16[8,2,2,48,768]{4,3,2,1,0:T(8,128)(2,1)}, bf16[8,2,2,48,768]{4,3,2,1,0:T(8,128)(2,1)S(1)}, u32[]{:S(2)}, u32[]{:S(2)}) collective-permute-start(bf16[8,2,2,48,768]{4,3,2,1,0:T(8,128)(2,1)} %get-tuple-element.39), channel_id=1, source_target_pairs={{0,8},{8,0},{16,24},{24,16},{32,40},{40,32},{48,56},{56,48},{64,72... | collective-permute-start | bytes 7077896 | tf_op jit(solution)/shard_map/ppermute | solution.py:437
  60.3 15.7 %collective-permute-start.12 = (bf16[704,128]{1,0:T(8,128)(2,1)}, bf16[704,128]{1,0:T(8,128)(2,1)S(1)}, u32[]{:S(2)}, u32[]{:S(2)}) collective-permute-start(bf16[704,128]{1,0:T(8,128)(2,1)} %copy-done.6), channel_id=1, source_target_pairs={{0,2},{1,3},{2,4},{3,5},{4,6},{5,7},{6,0},{7,1},{8,10},{9,11},{10,... | collective-permute-start | bytes 540680 | tf_op jit(solution)/shard_map/ppermute | solution.py:395
  63.4 16.5 %collective-permute-start.13 = (bf16[704,128]{1,0:T(8,128)(2,1)}, bf16[704,128]{1,0:T(8,128)(2,1)S(1)}, u32[]{:S(2)}, u32[]{:S(2)}) collective-permute-start(bf16[704,128]{1,0:T(8,128)(2,1)} %copy-done.5), channel_id=1, source_target_pairs={{0,6},{1,7},{2,0},{3,1},{4,2},{5,3},{6,4},{7,5},{8,14},{9,15},{10,... | collective-permute-start | bytes 540680 | tf_op jit(solution)/shard_map/ppermute | solution.py:395
  63.4 16.5 %collective-permute-start.14 = (bf16[704,128]{1,0:T(8,128)(2,1)}, bf16[704,128]{1,0:T(8,128)(2,1)S(1)}, u32[]{:S(2)}, u32[]{:S(2)}) collective-permute-start(bf16[704,128]{1,0:T(8,128)(2,1)} %copy-done.4), channel_id=1, source_target_pairs={{0,4},{1,5},{2,6},{3,7},{4,0},{5,1},{6,2},{7,3},{8,12},{9,13},{10,... | collective-permute-start | bytes 540680 | tf_op jit(solution)/shard_map/ppermute | solution.py:395
  65.0 17.8 %collective-permute-start.10 = (bf16[704,128]{1,0:T(8,128)(2,1)S(1)}, bf16[704,128]{1,0:T(8,128)(2,1)S(1)}, u32[]{:S(2)}, u32[]{:S(2)}) collective-permute-start(bf16[704,128]{1,0:T(8,128)(2,1)S(1)} %get-tuple-element.26), channel_id=1, source_target_pairs={{0,6},{1,7},{2,0},{3,1},{4,2},{5,3},{6,4},{7,5},{8,14},{9,15},{10,... | collective-permute-start | bytes 540680 | tf_op jit(solution)/shard_map/ppermute | solution.py:395
  67.5 15.2 %collective-permute-start.11 = (bf16[704,128]{1,0:T(8,128)(2,1)S(1)}, bf16[704,128]{1,0:T(8,128)(2,1)S(1)}, u32[]{:S(2)}, u32[]{:S(2)}) collective-permute-start(bf16[704,128]{1,0:T(8,128)(2,1)S(1)} %get-tuple-element.27), channel_id=1, source_target_pairs={{0,4},{1,5},{2,6},{3,7},{4,0},{5,1},{6,2},{7,3},{8,12},{9,13},{10,... | collective-permute-start | bytes 540680 | tf_op jit(solution)/shard_map/ppermute | solution.py:395
  76.0 6.9 %collective-permute-start.9 = (bf16[704,128]{1,0:T(8,128)(2,1)S(1)}, bf16[704,128]{1,0:T(8,128)(2,1)S(1)}, u32[]{:S(2)}, u32[]{:S(2)}) collective-permute-start(bf16[704,128]{1,0:T(8,128)(2,1)S(1)} %get-tuple-element.25), channel_id=1, source_target_pairs={{0,2},{1,3},{2,4},{3,5},{4,6},{5,7},{6,0},{7,1},{8,10},{9,11},{10,... | collective-permute-start | bytes 540680 | tf_op jit(solution)/shard_map/ppermute | solution.py:395
  80.2 7.0 %collective-permute-start.15 = (bf16[704,128]{1,0:T(8,128)(2,1)S(1)}, bf16[704,128]{1,0:T(8,128)(2,1)S(1)}, u32[]{:S(2)}, u32[]{:S(2)}) collective-permute-start(bf16[704,128]{1,0:T(8,128)(2,1)S(1)} %shard_map.106), channel_id=1, source_target_pairs={{0,1},{1,0},{2,3},{3,2},{4,5},{5,4},{6,7},{7,6},{8,9},{9,8},{10,11... | collective-permute-start | bytes 540680 | tf_op jit(solution)/shard_map/ppermute | solution.py:395
  90.2 5.5 %collective-permute-start.21 = (f32[112,128]{1,0:T(8,128)S(1)}, f32[112,128]{1,0:T(8,128)S(1)}, u32[]{:S(2)}, u32[]{:S(2)}) collective-permute-start(f32[112,128]{1,0:T(8,128)S(1)} %add.132), channel_id=1, source_target_pairs={{0,16},{8,24},{16,0},{24,8},{32,48},{40,56},{48,32},{56,40},{64,80... | collective-permute-start | bytes 172040 | tf_op jit(solution)/shard_map/ppermute | solution.py:466
  95.7 6.4 %collective-permute-start.22 = (f32[112,128]{1,0:T(8,128)S(1)}, f32[112,128]{1,0:T(8,128)S(1)}, u32[]{:S(2)}, u32[]{:S(2)}) collective-permute-start(f32[112,128]{1,0:T(8,128)S(1)} %add.133), channel_id=1, source_target_pairs={{0,32},{8,40},{16,48},{24,56},{32,0},{40,8},{48,16},{56,24},{64,96... | collective-permute-start | bytes 172040 | tf_op jit(solution)/shard_map/ppermute | solution.py:466
  102.1 6.7 %collective-permute-start.23 = (f32[112,128]{1,0:T(8,128)S(1)}, f32[112,128]{1,0:T(8,128)S(1)}, u32[]{:S(2)}, u32[]{:S(2)}) collective-permute-start(f32[112,128]{1,0:T(8,128)S(1)} %add.134), channel_id=1, source_target_pairs={{0,64},{8,72},{16,80},{24,88},{32,96},{40,104},{48,112},{56,120},{... | collective-permute-start | bytes 172040 | tf_op jit(solution)/shard_map/ppermute | solution.py:466
  105.3 13.5 %collective-permute-start.16 = (bf16[656,128]{1,0:T(8,128)(2,1)S(1)}, bf16[656,128]{1,0:T(8,128)(2,1)S(1)}, u32[]{:S(2)}, u32[]{:S(2)}) collective-permute-start(bf16[656,128]{1,0:T(8,128)(2,1)S(1)} %shard_map.107.own.refs_0_), channel_id=1, source_target_pairs={{0,8},{8,16},{16,24},{24,32},{32,40},{40,48},{48,56},{56,64},{64,7... | collective-permute-start | bytes 503816 | tf_op jit(solution)/shard_map/ppermute | solution.py:358
  106.6 12.3 %collective-permute-start.17 = (bf16[656,128]{1,0:T(8,128)(2,1)S(1)}, bf16[656,128]{1,0:T(8,128)(2,1)S(1)}, u32[]{:S(2)}, u32[]{:S(2)}) collective-permute-start(bf16[656,128]{1,0:T(8,128)(2,1)S(1)} %shard_map.107.own.refs_0_), channel_id=1, source_target_pairs={{8,0},{16,8},{24,16},{32,24},{40,32},{48,40},{56,48},{64,56},{72,6... | collective-permute-start | bytes 503816 | tf_op jit(solution)/shard_map/ppermute | solution.py:359
  108.8 12.3 %collective-permute-start.24 = (f32[112,128]{1,0:T(8,128)S(1)}, f32[112,128]{1,0:T(8,128)S(1)}, u32[]{:S(2)}, u32[]{:S(2)}) collective-permute-start(f32[112,128]{1,0:T(8,128)S(1)} %add.135), channel_id=1, source_target_pairs={{0,128},{8,136},{16,144},{24,152},{32,160},{40,168},{48,176},{56,1... | collective-permute-start | bytes 172040 | tf_op jit(solution)/shard_map/ppermute | solution.py:466
  118.6 5.2 %collective-permute-start.19 = (bf16[2,48,768]{2,1,0:T(8,128)(2,1)S(1)}, bf16[2,48,768]{2,1,0:T(8,128)(2,1)S(1)}, u32[]{:S(2)}, u32[]{:S(2)}) collective-permute-start(bf16[2,48,768]{2,1,0:T(8,128)(2,1)S(1)} %dynamic-slice_bitcast_fusion), channel_id=1, source_target_pairs={{0,16},{8,24},{16,0},{24,8},{32,48},{40,56},{48,32},{56,40},{64,80... | collective-permute-start | bytes 442376 | tf_op jit(solution)/shard_map/ppermute | solution.py:481
  (10 other events, 39.8 us)
Sparse Core Ops, SparseCore 0:
  60.4 47.3 reduce-scatter.1

commit v2 on v1

--- a/solution.py
+++ b/solution.py
@@ -19,6 +19,7 @@
 PACK = 656
 MOM = 656
 PAY = 704
+TERMS = 96
 GRP = 48
 CALL = 1536
 FF = 768
@@ -37,7 +38,27 @@
     return pltpu.CompilerParams(vmem_limit_bytes=mib * 1024 * 1024)
 
 
-def pack_kernel(x_ref, o_ref):
+def my_block():
+    return lax.axis_index("chan")
+
+
+def slot_block(s):
+    me = my_block()
+    return ((me // 2 + s // 2) % 4) * 2 + (me % 2 + s % 2) % 2
+
+
+def my_core():
+    return lax.axis_index("rows") % 2
+
+
+def my_lo():
+    return (lax.axis_index("rows") // 2) % 2
+
+
+def pack_kernel(far, o_ref, x_ref, sem):
+    copy = pltpu.make_async_copy(far, x_ref, sem.at[0])
+    copy.start()
+    copy.wait()
     parts = []
     low = lanes((HALF, 128)) < 64
     for i in range(ROWS):
@@ -99,7 +120,7 @@
     for start in range(0, COLS, 48):
         acc = taps_block(main_pad, k_ref, 0, start, 48, True)
         for i in range(ROWS):
-            cot = cot_ref[i, start : start + 48, :128].astype(F32)
+            cot = cot_ref[i * COLS + start : i * COLS + start + 48, :128].astype(F32)
             o_ref[i, start : start + 48, :128] = (acc[i] + cot).astype(BF16)
     parts = [[] for _ in range(ROWS)]
     for start in range(0, HALF, 24):
@@ -109,18 +130,16 @@
     for i in range(ROWS):
         rem = jnp.concatenate(parts[i], axis=0)
         both = jnp.concatenate([rem[:, :64], swap(rem)[:, :64]], axis=0)
-        cot = cot_ref[i, :, 128:].astype(F32)
+        cot = cot_ref[i * COLS : (i + 1) * COLS, 128:192].astype(F32)
         o_ref[i, :, 128:] = (both + cot).astype(BF16)
 
 
-def terms_kernel(scale, grad, top, own, bot, o_ref, main_pad, rem_pad):
+def kernel_terms(grad, top, own, bot, o_ref, main_pad, rem_pad):
     fill_pads((top, own, bot), main_pad, rem_pad)
+    o_ref[...] = jnp.zeros((TERMS, 128), F32)
     gmain = grad[:PIX, :].astype(F32)
     grem = grad[PIX:PACK, :].astype(F32)
-    for pad, part, width, base, folded in (
-        (main_pad, gmain, COLS, 0, False),
-        (rem_pad, grem, HALF, 56, True),
-    ):
+    for pad, part, width, folded in ((main_pad, gmain, COLS, False), (rem_pad, grem, HALF, True)):
         for b in range(7):
             acc = [jnp.zeros((8, 128), F32)] * 7
             for start in range(0, width, 8):
@@ -130,24 +149,90 @@
                     for a in range(7):
                         acc[a] = acc[a] + g * windows[i + a]
             for a in range(7):
-                total = jnp.sum(acc[a], axis=0, keepdims=True) * scale
-                if folded:
+                total = jnp.sum(acc[a], axis=0, keepdims=True)
+                t = a * 7 + b
+                if not folded:
+                    o_ref[t : t + 1, :] = total
+                else:
                     total = total + swap(total)
-                o_ref[base + a * 7 + b : base + a * 7 + b + 1, :] = total
-    for base in (49, 105):
-        o_ref[base : base + 7, :] = jnp.zeros((7, 128), F32)
-
-
-def first_kernel(blk, cot, scale, w_out, w_in, mixed, activ_grad, w_slot):
-    mixed[...] = (cot[...].astype(F32) * scale[...]).astype(BF16)
+                    if t < 25:
+                        o_ref[64 + t : 65 + t, :64] = total[:, :64]
+                    else:
+                        o_ref[39 + t : 40 + t, 64:] = total[:, 64:]
+
+
+def first_kernel(far_cot, far_scale, far_gain, far_taps, w_out, w_in, mixed, activ_grad, w_slot, gain_slot,
+                 gain_own, taps_out, cot_own, cot, scale, gain, taps, w_here, sems):
+    near = [
+        pltpu.make_async_copy(src, dst, sems.at[n])
+        for n, (src, dst) in enumerate(
+            ((far_scale, scale), (far_cot, cot), (far_gain, gain), (far_taps, taps), (w_out, w_here))
+        )
+    ]
+    late = []
+    for s in range(8):
+        row = pl.multiple_of(slot_block(s) * CH, 64)
+        late.append(
+            pltpu.make_async_copy(
+                w_in.at[pl.ds(row, 128), :], w_slot.at[pl.ds(128 * s, 128), :], sems.at[5 + 2 * s]
+            )
+        )
+        row = pl.multiple_of(slot_block(s) * CH + 128, 64)
+        late.append(
+            pltpu.make_async_copy(
+                w_in.at[pl.ds(row, 64), :],
+                w_slot.at[pl.ds(MAIN + 64 * s, 64), :],
+                sems.at[6 + 2 * s],
+            )
+        )
+    for copy in near + late:
+        copy.start()
+    near[0].wait()
+    near[1].wait()
+    for j in range(12):
+        at = slice(128 * j, 128 * j + 128)
+        mixed[:, at] = (cot[:, at].astype(F32) * scale[j : j + 1, :]).astype(BF16)
+    near[2].wait()
+    near[3].wait()
+    for a in range(7):
+        rows = slice(7 * a, 7 * a + 7)
+        taps_out[rows, :128] = taps[a, :, :128]
+        taps_out[rows, 128:192] = taps[a, :, 128:]
+        taps_out[rows, 192:] = taps[a, :, 128:]
+
+    def unit(index, high):
+        line = gain[pl.ds(index // 2, 1), :]
+        return jnp.where(index % 2 == high, line, swap(line))
+
+    low = lanes((1, 128)) < 64
+    rest = []
+    for s in range(8):
+        u = 3 * slot_block(s)
+        main = jnp.where(low, unit(u, 0), unit(u + 1, 1))
+        gain_slot[:, 128 * s : 128 * s + 128] = main
+        rest.append(unit(u + 2, s % 2))
+        if s == 0:
+            gain_own[0:1, :] = main
+            gain_own[1:2, :] = jnp.where(low, rest[0], swap(rest[0]))
+    for t in range(4):
+        at = MAIN + 128 * t
+        gain_slot[:, at : at + 128] = jnp.where(low, rest[2 * t], rest[2 * t + 1])
+
+    def column(index, high):
+        at = pl.multiple_of((index // 2) * 128, 128)
+        tile = cot[:, pl.ds(at, 128)].astype(F32)
+        return jnp.where(index % 2 == high, tile, swap(tile))
+
+    u = 3 * my_block()
+    low = lanes((PIX, 128)) < 64
+    cot_own[:, :128] = jnp.where(low, column(u, 0), column(u + 1, 1)).astype(BF16)
+    cot_own[:, 128:] = column(u + 2, 0).astype(BF16)
+    near[4].wait()
     activ_grad[...] = lax.dot_general(
-        mixed[...], w_out[...], (((1,), (1,)), ((), ())), preferred_element_type=F32
-    )
-    for s in range(8):
-        row = pl.multiple_of(blk[s] * CH, 64)
-        w_slot[128 * s : 128 * s + 128, :] = w_in[pl.ds(row, 128), :]
-        row = pl.multiple_of(blk[s] * CH + 128, 64)
-        w_slot[MAIN + 64 * s : MAIN + 64 * s + 64, :] = w_in[pl.ds(row, 64), :]
+        mixed[...], w_here[...], (((1,), (1,)), ((), ())), preferred_element_type=F32
+    )
+    for copy in late:
+        copy.wait()
 
 
 def gelu_pair(v):
@@ -167,9 +252,9 @@
 def middle_kernel(*refs):
     slots = refs[:8]
     gain, w_slot, activ_grad = refs[8:11]
-    normed, activ, grad_hidden, mean_ref, rstd_ref = refs[11:16]
-    payloads = refs[16:24]
-    x, first, second = refs[24:]
+    normed, activ, grad_hidden, stats = refs[11:15]
+    payloads = refs[15:23]
+    x, first, second = refs[23:]
     low = lanes((HALF, 128)) < 64
     for s in range(8):
         x[:, 128 * s : 128 * s + 128] = slots[s][:PIX, :].astype(F32)
@@ -182,6 +267,7 @@
             o = odd[i * HALF : (i + 1) * HALF]
             x[i * COLS : i * COLS + HALF, at : at + 128] = jnp.where(low, e, swap(o))
             x[i * COLS + HALF : (i + 1) * COLS, at : at + 128] = jnp.where(low, swap(e), o)
+    low = lanes((GRP, 128)) < 64
     for start in range(0, PIX, GRP):
         rows = slice(start, start + GRP)
         values = x[rows, :]
@@ -192,13 +278,15 @@
         nhat = centred * rstd
         x[rows, :] = nhat
         normed[rows, :] = (nhat * gain[...]).astype(BF16)
-        mean_ref[rows, :] = jnp.broadcast_to(mean, (GRP, 128))
-        rstd_ref[rows, :] = jnp.broadcast_to(rstd, (GRP, 128))
+        stats[rows, :] = jnp.where(
+            low, jnp.broadcast_to(mean, (GRP, 128)), jnp.broadcast_to(rstd, (GRP, 128))
+        )
     for n in range(0, FF, 256):
         hidden = jnp.dot(normed[...], w_slot[:, n : n + 256], preferred_element_type=F32)
         value, slope = gelu_pair(hidden)
         activ[:, n : n + 256] = value.astype(BF16)
         grad_hidden[:, n : n + 256] = (activ_grad[:, n : n + 256] * slope).astype(BF16)
+    low = lanes((HALF, 128)) < 64
     for t in range(4):
         for at, kind in ((256 * t, 0), (MAIN + 128 * t, 1)):
             width = 128 if kind else 256
@@ -245,8 +333,11 @@
         payloads[s][MOM:PAY, :] = moments
 
 
-def sum_kernel(a, b, c, d, o_ref):
-    total = a[...].astype(F32) + b[...].astype(F32) + c[...].astype(F32) + d[...].astype(F32)
+def sum_kernel(*refs):
+    o_ref = refs[-1]
+    total = refs[0][...].astype(F32)
+    for ref in refs[1:-1]:
+        total = total + ref[...].astype(F32)
     o_ref[:MOM, :] = total[:MOM].astype(BF16)
     moments = total[MOM:]
     whole = moments + pltpu.roll(moments, 128 - 16, 1)
@@ -255,7 +346,7 @@
     o_ref[MOM:, :] = jnp.where(low, hi, pltpu.roll(lo, 16, 1)).astype(BF16)
 
 
-def norm_back_kernel(a, b, c, d, e, conv, mean_ref, rstd_ref, gain, o_ref):
+def norm_back_kernel(a, b, c, d, e, conv, stats, gain, top, own, bot, o_ref, terms, main_pad, rem_pad):
     refs = (a, b, c, d, e)
     total = sum(ref[...].astype(F32) for ref in refs[1:]) + a[...].astype(F32)
     moments = total[MOM:]
@@ -266,8 +357,11 @@
         seconds.append(jnp.broadcast_to(whole[:, 32 + g : 33 + g], (GRP, 128)))
     first = jnp.concatenate(firsts)
     second = jnp.concatenate(seconds)
-    mean = mean_ref[...]
-    rstd = rstd_ref[...]
+    both = stats[...]
+    low = lanes((PIX, 128)) < 64
+    other = swap(both)
+    mean = jnp.where(low, both, other)
+    rstd = jnp.where(low, other, both)
     main = rstd * (
         total[:PIX] * gain[0:1, :] - first - (conv[:PIX, :].astype(F32) - mean) * rstd * second
     )
@@ -287,50 +381,97 @@
     rem = rstd * (total[PIX : PIX + REM] * gain[1:2, :] - first - (crem - mean) * rstd * second)
     rem = jnp.concatenate([rem, jnp.zeros((PACK - PIX - REM, 128), F32)])
     o_ref[PIX:PACK, :] = rem.astype(BF16)
-
-
-def weights_kernel(scale, blk, place, normed, grad_hidden, activ, mixed, keep, send):
-    own = place[0] == 0
-
-    def put(z, w, xlo, rows, zero, one):
-        zero, one = zero.astype(BF16), one.astype(BF16)
-        keep[z, w, xlo, rows, :] = jnp.where(own, zero, one)
-        send[z, w, xlo, rows, :] = jnp.where(own, one, zero)
-
-    def product(left, right):
-        return (
-            lax.dot_general(left, right, (((0,), (0,)), ((), ())), preferred_element_type=F32)
-            * scale
-        )
-
-    every = slice(0, 48)
+    kernel_terms(o_ref, top, own, bot, terms, main_pad, rem_pad)
+
+
+def put(own, keep, send, z, xlo, zero, one):
+    zero, one = zero.astype(BF16), one.astype(BF16)
+    keep[z, xlo, :, :] = jnp.where(own, zero, one)
+    send[z, xlo, :, :] = jnp.where(own, one, zero)
+
+
+def product(left, right):
+    return lax.dot_general(left, right, (((0,), (0,)), ((), ())), preferred_element_type=F32)
+
+
+def weights_out_kernel(activ, mixed, keep, send):
+    own = my_core() == 0
     for t in range(4):
         part = product(mixed[:, 384 * t : 384 * t + 384], activ[...])
         for n in range(2):
             p = part[192 * n : 192 * n + 192]
-            put(2 * t + n, 1, 0, every, p[0:48], p[48:96])
-            put(2 * t + n, 1, 1, every, p[96:144], p[144:192])
+            put(own, keep, send, 2 * t + n, 0, p[0:48], p[48:96])
+            put(own, keep, send, 2 * t + n, 1, p[96:144], p[144:192])
+
+
+def weights_in_kernel(normed, grad_hidden, keep, send):
+    own = my_core() == 0
     for t in range(4):
         part = product(normed[:, 256 * t : 256 * t + 256], grad_hidden[...])
         rest = product(normed[:, MAIN + 128 * t : MAIN + 128 * t + 128], grad_hidden[...])
         for n in range(2):
             p = part[128 * n : 128 * n + 128]
             q = rest[64 * n : 64 * n + 64]
-            z = blk[2 * t + n]
-            put(z, 0, 0, every, p[0:48], p[48:96])
-            put(z, 0, 1, every, jnp.concatenate([p[96:128], q[0:16]]), q[16:64])
-
-
-def call(kernel, outs, args, scratch=(), mib=32, smem=0, flops=0, moved=0):
-    space = [pl.BlockSpec(memory_space=pltpu.SMEM)] * smem
-    space += [pl.BlockSpec(memory_space=pltpu.VMEM)] * (len(args) - smem)
+            z = slot_block(2 * t + n)
+            put(own, keep, send, z, 0, p[0:48], p[48:96])
+            put(own, keep, send, z, 1, jnp.concatenate([p[96:128], q[0:16]]), q[16:64])
+
+
+def join_kernel(keep_in, got_in, keep_out, got_out, far, here, sems):
+    copies = []
+    for z in range(8):
+        for w, (keep, got) in enumerate(((keep_in, got_in), (keep_out, got_out))):
+            here[z, w] = (keep[z].astype(F32) + got[z].astype(F32)).astype(BF16)
+        copies.append(pltpu.make_async_copy(here.at[z], far.at[z], sems.at[z]))
+        copies[-1].start()
+    for copy in copies:
+        copy.wait()
+
+
+def pass_kernel(terms, got, *refs):
+    refs[len(refs) // 2][...] = terms[...] + got[...]
+    for n in range(len(refs) // 2):
+        refs[len(refs) // 2 + 1 + n][...] = refs[n][...]
+
+
+def away_kernel(far, terms, other, o_ref, held, sems):
+    copies = []
+    for w in range(2):
+        rows = pl.ds(48 * w, 48)
+        copies.append(pltpu.make_async_copy(far.at[w, 1 - my_lo()], o_ref.at[rows], sems.at[w]))
+        copies.append(pltpu.make_async_copy(far.at[w, my_lo()], held.at[rows], sems.at[2 + w]))
+    for copy in copies:
+        copy.start()
+    total = (terms[...] + other[...]).astype(BF16)
+    for j in range(6):
+        o_ref[96:112, 128 * j : 128 * j + 128] = total[16 * j : 16 * j + 16]
+    for copy in copies:
+        copy.wait()
+
+
+def last_kernel(scale, held, away, got, grad_in, grad_out, grad_kernel):
+    for w, ref in enumerate((grad_in, grad_out)):
+        rows = slice(48 * w, 48 * w + 48)
+        ref[...] = (held[rows, :].astype(F32) + got[rows, :].astype(F32)) * scale
+    both = (away[96:112, :].astype(F32) + got[96:112, :].astype(F32)) * scale
+    lines = jnp.concatenate([both[:, 128 * j : 128 * j + 128] for j in range(6)], axis=0)
+    rest = jnp.concatenate([lines[64:89], swap(lines[64:96])[:24]], axis=0)
+    for a in range(7):
+        grad_kernel[a, :, :128] = lines[7 * a : 7 * a + 7]
+        grad_kernel[a, :, 128:] = rest[7 * a : 7 * a + 7, :64]
+
+
+def call(kernel, outs, args, scratch=(), mib=16, far=(), far_out=False, flops=0, moved=0):
+    near = pl.BlockSpec(memory_space=pltpu.VMEM)
+    args = [pltpu.with_memory_space_constraint(a, pltpu.HBM) if n in far else a for n, a in enumerate(args)]
+    hbm = pl.BlockSpec(memory_space=pltpu.HBM)
     single = not isinstance(outs, (list, tuple))
     shapes = [outs] if single else list(outs)
     result = pl.pallas_call(
         kernel,
         out_shape=shapes,
-        in_specs=space,
-        out_specs=[pl.BlockSpec(memory_space=pltpu.VMEM)] * len(shapes),
+        in_specs=[hbm if n in far else near for n in range(len(args))],
+        out_specs=[hbm if far_out else near] * len(shapes),
         scratch_shapes=list(scratch),
         compiler_params=limit(mib),
         cost_estimate=pl.CostEstimate(flops=flops, bytes_accessed=moved, transcendentals=0),
@@ -362,30 +503,47 @@
 
 def shards(feature, kernel, ln_gain, layer_scale, w_in, w_out, cotangent):
     scale = 1.0 / math.sqrt(32 * PIX)
-    me = lax.axis_index("chan")
-    row = lax.axis_index("rows")
-    my_y, my_x = me // 2, me % 2
     slots = [(k, x) for k in range(4) for x in range(2)]
-    blk = jnp.stack([((my_y + k) % 4) * 2 + (my_x ^ x) for k, x in slots]).astype(jnp.int32)
-    place = jnp.stack([row % 2, (row // 2) % 2]).astype(jnp.int32)
-
-    packed = call(pack_kernel, shape((PACK, 128), BF16), [feature])
+
+    packed = call(
+        pack_kernel,
+        shape((PACK, 128), BF16),
+        [feature],
+        [pltpu.VMEM((ROWS, COLS, CH), BF16), pltpu.SemaphoreType.DMA((1,))],
+        far=(0,),
+    )
     above, below = halos(packed)
-    taps = kernel.reshape(49, CH)
-    taps = jnp.concatenate([taps[:, :128], taps[:, 128:], taps[:, 128:]], axis=1)
-    cot = cotangent.reshape(PIX, CALL)
-    mixed, activ_grad, w_slot = call(
+    mixed, activ_grad, w_slot, gain_slot, gain_own, taps, cot_own = call(
         first_kernel,
-        [shape((PIX, CALL), BF16), shape((PIX, FF), F32), shape((CALL, FF), BF16)],
-        [blk, cot, layer_scale.reshape(1, CALL), w_out, w_in],
-        smem=1,
+        [
+            shape((PIX, CALL), BF16),
+            shape((PIX, FF), F32),
+            shape((CALL, FF), BF16),
+            shape((1, CALL), F32),
+            shape((2, 128), F32),
+            shape((49, 256), F32),
+            shape((PIX, 256), BF16),
+        ],
+        [
+            cotangent.reshape(PIX, CALL),
+            layer_scale.reshape(12, 128),
+            ln_gain.reshape(12, 128),
+            kernel,
+            w_out,
+            w_in,
+        ],
+        [
+            pltpu.VMEM((PIX, CALL), BF16),
+            pltpu.VMEM((12, 128), F32),
+            pltpu.VMEM((12, 128), F32),
+            pltpu.VMEM((7, 7, CH), F32),
+            pltpu.VMEM((FF, CALL), BF16),
+            pltpu.SemaphoreType.DMA((21,)),
+        ],
+        far=range(6),
         flops=2 * PIX * CALL * FF,
         moved=8 << 20,
     )
-    gains = ln_gain.reshape(8, CH)[blk]
-    gain_slot = jnp.concatenate([gains[:, :128].reshape(1, -1), gains[:, 128:].reshape(1, -1)], axis=1)
-    gain_own = jnp.stack([gains[0, :128], jnp.concatenate([gains[0, 128:], gains[0, 128:]])])
-    cot_own = lax.dynamic_slice_in_dim(cotangent, me * CH, CH, 2)
 
     conv = call(
         conv_kernel, shape((PACK, 128), BF16), [above, packed, below, taps], pads(), flops=1 << 23, moved=1 << 20
@@ -396,10 +554,11 @@
 
     partner = shift(conv, 0, 1)
     gathered = {(0, 0): conv, (0, 1): partner}
-    for k in (1, 3, 2):
+    for k in (2, 1, 3):
         gathered[(4 - k) % 4, 0] = shift(conv, k, 0)
-    for k in (1, 3, 2):
+    for k in (1, 3):
         gathered[(4 - k) % 4, 1] = shift(partner, k, 0)
+    gathered[2, 1] = shift(gathered[2, 0], 0, 1)
 
     outs = call(
         middle_kernel,
@@ -408,64 +567,75 @@
             shape((PIX, FF), BF16),
             shape((PIX, FF), BF16),
             shape((PIX, 128), F32),
-            shape((PIX, 128), F32),
         ]
         + [shape((PAY, 128), BF16)] * 8,
         [gathered[s] for s in slots] + [gain_slot, w_slot, activ_grad],
         [pltpu.VMEM((PIX, CALL), F32), pltpu.VMEM((PIX, 128), F32), pltpu.VMEM((PIX, 128), F32)],
-        mib=40,
+        mib=16,
         flops=4 * PIX * CALL * FF,
         moved=8 << 20,
     )
-    normed, activ, grad_hidden, mean, rstd = outs[:5]
-    payload = dict(zip(slots, outs[5:]))
-
-    other = [shift(payload[k, 1], k, 0) for k in (1, 3, 2)]
-    mine = [shift(payload[k, 0], k, 0) for k in (1, 3, 2)]
+    normed, activ, grad_hidden, stats = outs[:4]
+    payload = dict(zip(slots, outs[4:]))
+
+    across = shift(payload[2, 1], 0, 1)
+    other = [shift(payload[k, 1], k, 0) for k in (1, 3)]
+    far_sum = call(sum_kernel, shape((PAY, 128), BF16), [payload[2, 0], across], moved=1 << 20)
+    mine = [shift(far_sum, 2, 0)] + [shift(payload[k, 0], k, 0) for k in (1, 3)]
     other_sum = call(sum_kernel, shape((PAY, 128), BF16), [payload[0, 1]] + other, moved=1 << 20)
     crossed = shift(other_sum, 0, 1)
 
-    keep, send = call(
-        lambda *refs: weights_kernel(scale, *refs),
-        [shape((8, 2, 2, 48, FF), BF16)] * 2,
-        [blk, place, normed, grad_hidden, activ, mixed],
-        smem=2,
-        mib=48,
-        flops=4 * PIX * CALL * FF,
+    pairs = [shape((8, 2, 48, FF), BF16)] * 2
+    core = rows_perm(lambda i: i ^ 1)
+    keep_out, send_out = call(
+        weights_out_kernel, pairs, [activ, mixed], flops=2 * PIX * CALL * FF, moved=8 << 20
+    )
+    got_out = lax.ppermute(send_out, "rows", core)
+    keep_in, send_in = call(
+        weights_in_kernel,
+        pairs,
+        [normed, grad_hidden],
+        flops=2 * PIX * CALL * FF,
         moved=8 << 20,
     )
-    got = lax.ppermute(send, "rows", rows_perm(lambda i: i ^ 1))
-    both = (keep.astype(F32) + got.astype(F32)).astype(BF16).reshape(8, 192, FF)
+    got_in = lax.ppermute(send_in, "rows", core)
+    joined = call(
+        join_kernel,
+        shape((8, 2, 2, 48, FF), BF16),
+        [keep_in, got_in, keep_out, got_out],
+        [pltpu.VMEM((8, 2, 2, 48, FF), BF16), pltpu.SemaphoreType.DMA((8,))],
+        far_out=True,
+        moved=8 << 20,
+    ).reshape(8, 192, FF)
     z_groups = [[z * 4 + q for z in range(8)] for q in range(4)]
     z_sum = lax.psum_scatter(
-        both, "rows", scatter_dimension=0, axis_index_groups=z_groups, tiled=True
+        joined, "rows", scatter_dimension=0, axis_index_groups=z_groups, tiled=True
     ).reshape(2, 2, 48, FF)
 
-    grad_conv = call(
+    grad_conv, terms = call(
         norm_back_kernel,
-        shape((PACK, 128), BF16),
-        [payload[0, 0]] + mine + [crossed, conv, mean, rstd, gain_own],
-        moved=2 << 20,
-    )
-    grad_above, grad_below = halos(grad_conv)
-    terms = call(
-        lambda *refs: terms_kernel(scale, *refs),
-        shape((112, 128), F32),
-        [grad_conv, above, packed, below],
+        [shape((PACK, 128), BF16), shape((TERMS, 128), F32)],
+        [payload[0, 0]] + mine + [crossed, conv, stats, gain_own, above, packed, below],
         pads(),
         flops=1 << 23,
-        moved=1 << 20,
-    )
-    for f in (
-        lambda i: i ^ 1,
-        lambda i: i ^ 2,
-        lambda i: i ^ 4,
-        lambda i: i ^ 8,
-        lambda i: i ^ 16,
-    ):
-        terms = terms + lax.ppermute(terms, "rows", rows_perm(f))
-    grad_kernel = jnp.concatenate([terms[:49], terms[56:105, :64]], axis=1).reshape(7, 7, CH)
-
+        moved=2 << 20,
+    )
+
+    def partner_terms(terms, f):
+        return lax.ppermute(terms, "rows", rows_perm(f))
+
+    def step(terms, f, *rest):
+        return call(
+            pass_kernel,
+            [shape((TERMS, 128), F32)] + [shape((PACK, 128), BF16)] * len(rest),
+            [terms, partner_terms(terms, f)] + list(rest),
+            moved=1 << 20,
+        )
+
+    terms, grad_conv = step(terms, lambda i: i ^ 1, grad_conv)
+    grad_above, grad_below = halos(grad_conv)
+    terms, grad_above, grad_below = step(terms, lambda i: i ^ 4, grad_above, grad_below)
+    terms = terms + partner_terms(terms, lambda i: i ^ 8)
     grad_feature = call(
         back_kernel,
         shape((ROWS, COLS, CH), BF16),
@@ -474,12 +644,22 @@
         flops=1 << 23,
         moved=1 << 20,
     )
-
-    my_lo = place[1]
-    away = lax.dynamic_index_in_dim(z_sum, 1 - my_lo, 1, keepdims=False)
-    held = lax.dynamic_index_in_dim(z_sum, my_lo, 1, keepdims=False)
-    final = held.astype(F32) + lax.ppermute(away, "rows", rows_perm(lambda i: i ^ 2)).astype(F32)
-    return grad_feature, final[0], final[1].T, grad_kernel
+    away, held = call(
+        away_kernel,
+        [shape((112, FF), BF16), shape((96, FF), BF16)],
+        [z_sum, terms, partner_terms(terms, lambda i: i ^ 16)],
+        [pltpu.SemaphoreType.DMA((4,))],
+        far=(0,),
+        moved=1 << 20,
+    )
+    got = lax.ppermute(away, "rows", rows_perm(lambda i: i ^ 2))
+    grad_in, grad_out, grad_kernel = call(
+        lambda *refs: last_kernel(scale, *refs),
+        [shape((48, FF), F32), shape((48, FF), F32), shape((7, 7, CH), F32)],
+        [held, away, got],
+        moved=1 << 20,
+    )
+    return grad_feature, grad_in, grad_out.T, grad_kernel
 
 
 def solution(mesh):

time: 132 us -> 119 us (0.902)
  the two profiles are of different devices: /device:TPU:24 before, /device:TPU:8 now
where the time goes in v2:
time: 119 us; the launch traced here: 118 us
  starting transfers between devices  49.4 us (42%)
  waiting for transfers between devices  32.6 us (27%)
  Pallas kernels  22.3 us (19%)
  between operations  14.2 us (12%)
    ppermute x14, starting transfers between devices, shift(): return lax.ppermute(block, 'chan', chan_shift(k, x))  24.1 us
    pallas_call x15, Pallas kernels, call(): pl.pallas_call(kernel, out_shape=shapes, in_specs=[hbm if n in far else n...  22.3 us
    ppermute x4, starting transfers between devices, partner_terms(): return lax.ppermute(terms, 'rows', rows_perm(f))  15.9 us
    ppermute x14, waiting for transfers between devices, shift(): return lax.ppermute(block, 'chan', chan_shift(k, x))  13.9 us
    ppermute x4, waiting for transfers between devices, partner_terms(): return lax.ppermute(terms, 'rows', rows_perm(f))  12.8 us
    ppermute x2, starting transfers between devices, halos(): above = lax.ppermute(block, 'rows', [(i, i + 1) for i in range(31)])  6.08 us
    ppermute x1, waiting for transfers between devices, shards(): got = lax.ppermute(away, 'rows', rows_perm(lambda i: i ^ 2))  3.34 us
    ppermute x2, starting transfers between devices, halos(): below = lax.ppermute(block, 'rows', [(i + 1, i) for i in range(31)])  2.58 us
  transfers between devices with their start and end apart: 26, of which 15 were waited for; matrix products, arithmetic and copies ran while one was open for 0% of the time, Pallas kernels for 8%

profile of v2, /device:TPU:8, one launch (start us, length us, event | category | flops | bytes accessed | tf_op | source)
XLA Modules:
  0.0 118.5 jit_solution(16797666655566949050)
XLA Ops:
  9.6 3.0 %collective-permute-start = (bf16[656,128]{1,0:T(8,128)(2,1)S(1)}, bf16[656,128]{1,0:T(8,128)(2,1)S(1)}, u32[]{:S(2)}, u32[]{:S(2)}) collective-permute-start(bf16[656,128]{1,0:T(8,128)(2,1)S(1)} %shard_map.102.own), channel_id=1, source_target_pairs={{0,8},{8,16},{16,24},{24,32},{32,40},{40,48},{48,56},{56,64},{64,7... | collective-permute-start | bytes 503816 | tf_op jit(solution)/shard_map/ppermute | solution.py:499
  12.6 3.6 %shard_map.103 = (bf16[432,1536]{1,0:T(8,128)(2,1)S(1)}, f32[432,768]{1,0:T(8,128)S(1)}, bf16[1536,768]{1,0:T(8,128)(2,1)S(1)}, f32[1,1536]{1,0:T(1,128)S(1)}, f...) custom-call(bf16[432,1536]{1,0:T(8,128)(2,1)} %bitcast.6, f32[12,128]{1,0:T(8,128)} %bitcast.8, ...), custom_call_target="tpu_custom_call" | custom-call | flops 1019215872 | bytes 8388608 | tf_op jit(solution)/shard_map/pallas_call | solution.py:470
  17.6 2.4 %collective-permute-start.5 = (bf16[656,128]{1,0:T(8,128)(2,1)S(1)}, bf16[656,128]{1,0:T(8,128)(2,1)S(1)}, u32[]{:S(2)}, u32[]{:S(2)}) collective-permute-start(bf16[656,128]{1,0:T(8,128)(2,1)S(1)} %shard_map.104.refs_0_.conv), channel_id=1, source_target_pairs={{0,4},{1,5},{2,6},{3,7},{4,0},{5,1},{6,2},{7,3},{8,12},{9,13},{10,... | collective-permute-start | bytes 503816 | tf_op jit(solution)/shard_map/ppermute | solution.py:553
  20.0 3.0 %collective-permute-start.2 = (bf16[656,128]{1,0:T(8,128)(2,1)S(1)}, bf16[656,128]{1,0:T(8,128)(2,1)S(1)}, u32[]{:S(2)}, u32[]{:S(2)}) collective-permute-start(bf16[656,128]{1,0:T(8,128)(2,1)S(1)} %shard_map.104.refs_0_.conv), channel_id=1, source_target_pairs={{0,1},{1,0},{2,3},{3,2},{4,5},{5,4},{6,7},{7,6},{8,9},{9,8},{10,11... | collective-permute-start | bytes 503816 | tf_op jit(solution)/shard_map/ppermute | solution.py:553
  23.0 2.0 %collective-permute-start.3 = (bf16[656,128]{1,0:T(8,128)(2,1)S(1)}, bf16[656,128]{1,0:T(8,128)(2,1)S(1)}, u32[]{:S(2)}, u32[]{:S(2)}) collective-permute-start(bf16[656,128]{1,0:T(8,128)(2,1)S(1)} %shard_map.104.refs_0_.conv), channel_id=1, source_target_pairs={{0,6},{1,7},{2,0},{3,1},{4,2},{5,3},{6,4},{7,5},{8,14},{9,15},{10,... | collective-permute-start | bytes 503816 | tf_op jit(solution)/shard_map/ppermute | solution.py:553
  26.3 3.1 %collective-permute-start.6 = (bf16[656,128]{1,0:T(8,128)(2,1)S(1)}, bf16[656,128]{1,0:T(8,128)(2,1)S(1)}, u32[]{:S(2)}, u32[]{:S(2)}) collective-permute-start(bf16[656,128]{1,0:T(8,128)(2,1)S(1)} %collective-permute-done.5.refs_4_), channel_id=1, source_target_pairs={{0,1},{1,0},{2,3},{3,2},{4,5},{5,4},{6,7},{7,6},{8,9},{9,8},{10,11... | collective-permute-start | bytes 503816 | tf_op jit(solution)/shard_map/ppermute | solution.py:553
  31.4 2.8 %collective-permute-done.6.refs_5_ = bf16[656,128]{1,0:T(8,128)(2,1)S(1)} collective-permute-done((bf16[656,128]{1,0:T(8,128)(2,1)S(1)}, bf16[656,128]{1,0:T(8,128)(2,1)S(1)}, u32[]{:S(2)}, u32[]{:S(2)}) %collective-permute-start.6) | collective-permute-done | bytes 167968 | tf_op jit(solution)/shard_map/ppermute | solution.py:553
  36.9 5.1 %shard_map.105 = (bf16[432,1536]{1,0:T(8,128)(2,1)S(1)}, bf16[432,768]{1,0:T(8,128)(2,1)S(1)}, bf16[432,768]{1,0:T(8,128)(2,1)S(1)}, f32[432,128]{1,0:T(8,128)S(...) custom-call(bf16[656,128]{1,0:T(8,128)(2,1)S(1)} %shard_map.104.refs, ...), custom_call_target="tpu_custom_call" | custom-call | flops 2038431744 | bytes 8388608 | tf_op jit(solution)/shard_map/pallas_call | solution.py:470
  50.5 2.0 %collective-permute-start.13 = (bf16[704,128]{1,0:T(8,128)(2,1)S(1)}, bf16[704,128]{1,0:T(8,128)(2,1)S(1)}, u32[]{:S(2)}, u32[]{:S(2)}) collective-permute-start(bf16[704,128]{1,0:T(8,128)(2,1)S(1)} %get-tuple-element.49), channel_id=1, source_target_pairs={{0,2},{1,3},{2,4},{3,5},{4,6},{5,7},{6,0},{7,1},{8,10},{9,11},{10,... | collective-permute-start | bytes 540680 | tf_op jit(solution)/shard_map/ppermute | solution.py:553
  53.1 2.3 %collective-permute-start.11 = (bf16[704,128]{1,0:T(8,128)(2,1)S(1)}, bf16[704,128]{1,0:T(8,128)(2,1)S(1)}, u32[]{:S(2)}, u32[]{:S(2)}) collective-permute-start(bf16[704,128]{1,0:T(8,128)(2,1)S(1)} %get-tuple-element.46), channel_id=1, source_target_pairs={{0,2},{1,3},{2,4},{3,5},{4,6},{5,7},{6,0},{7,1},{8,10},{9,11},{10,... | collective-permute-start | bytes 540680 | tf_op jit(solution)/shard_map/ppermute | solution.py:553
  56.3 1.7 %collective-permute-done.9.refs_1_ = bf16[704,128]{1,0:T(8,128)(2,1)S(1)} collective-permute-done((bf16[704,128]{1,0:T(8,128)(2,1)S(1)}, bf16[704,128]{1,0:T(8,128)(2,1)S(1)}, u32[]{:S(2)}, u32[]{:S(2)}) %collective-permute-start.9) | collective-permute-done | bytes 180256 | tf_op jit(solution)/shard_map/ppermute | solution.py:553
  58.3 2.2 %collective-permute-start.10 = (bf16[704,128]{1,0:T(8,128)(2,1)S(1)}, bf16[704,128]{1,0:T(8,128)(2,1)S(1)}, u32[]{:S(2)}, u32[]{:S(2)}) collective-permute-start(bf16[704,128]{1,0:T(8,128)(2,1)S(1)} %shard_map.106), channel_id=1, source_target_pairs={{0,4},{1,5},{2,6},{3,7},{4,0},{5,1},{6,2},{7,3},{8,12},{9,13},{10,... | collective-permute-start | bytes 540680 | tf_op jit(solution)/shard_map/ppermute | solution.py:553
  61.1 2.6 %collective-permute-start.15 = (bf16[704,128]{1,0:T(8,128)(2,1)S(1)}, bf16[704,128]{1,0:T(8,128)(2,1)S(1)}, u32[]{:S(2)}, u32[]{:S(2)}) collective-permute-start(bf16[704,128]{1,0:T(8,128)(2,1)S(1)} %shard_map.107), channel_id=1, source_target_pairs={{0,1},{1,0},{2,3},{3,2},{4,5},{5,4},{6,7},{7,6},{8,9},{9,8},{10,11... | collective-permute-start | bytes 540680 | tf_op jit(solution)/shard_map/ppermute | solution.py:553
  63.8 5.0 %collective-permute-done.10.b = bf16[704,128]{1,0:T(8,128)(2,1)S(1)} collective-permute-done((bf16[704,128]{1,0:T(8,128)(2,1)S(1)}, bf16[704,128]{1,0:T(8,128)(2,1)S(1)}, u32[]{:S(2)}, u32[]{:S(2)}) %collective-permute-start.10) | collective-permute-done | bytes 180256 | tf_op jit(solution)/shard_map/ppermute | solution.py:553
  68.9 2.3 %shard_map.108 = (bf16[656,128]{1,0:T(8,128)(2,1)S(1)}, f32[96,128]{1,0:T(8,128)S(1)}) custom-call(bf16[704,128]{1,0:T(8,128)(2,1)S(1)} %get-tuple-element.43.a, bf16[704,128]{1,0:T(8,128)(2,1)S(1)} %collective-permute-done.10.b, bf16[704,128]{1,0:T(8,128)(2,1)S(1)} %collective-permute-done.11.c, bf16[704,128]{1,0:T(8,128)(2,1)S(1)} %collective-permute-done.12.d, ...), custom_call_target="tpu_custom_call" | custom-call | flops 8388608 | bytes 2097152 | tf_op jit(solution)/shard_map/pallas_call | solution.py:470
  73.8 3.0 %collective-permute-start.18 = (bf16[656,128]{1,0:T(8,128)(2,1)S(1)}, bf16[656,128]{1,0:T(8,128)(2,1)S(1)}, u32[]{:S(2)}, u32[]{:S(2)}) collective-permute-start(bf16[656,128]{1,0:T(8,128)(2,1)S(1)} %get-tuple-element.56.own), channel_id=1, source_target_pairs={{0,8},{8,16},{16,24},{24,32},{32,40},{40,48},{48,56},{56,64},{64,7... | collective-permute-start | bytes 503816 | tf_op jit(solution)/shard_map/ppermute | solution.py:499
  76.9 2.2 %collective-permute-start.17 = (f32[96,128]{1,0:T(8,128)S(1)}, f32[96,128]{1,0:T(8,128)S(1)}, u32[]{:S(2)}, u32[]{:S(2)}) collective-permute-start(f32[96,128]{1,0:T(8,128)S(1)} %get-tuple-element.55.terms), channel_id=1, source_target_pairs={{0,32},{8,40},{16,48},{24,56},{32,0},{40,8},{48,16},{56,24},{64,96... | collective-permute-start | bytes 147464 | tf_op jit(solution)/shard_map/ppermute | solution.py:625
  79.1 6.3 %collective-permute-done.17.got = f32[96,128]{1,0:T(8,128)S(1)} collective-permute-done((f32[96,128]{1,0:T(8,128)S(1)}, f32[96,128]{1,0:T(8,128)S(1)}, u32[]{:S(2)}, u32[]{:S(2)}) %collective-permute-start.17) | collective-permute-done | bytes 49184 | tf_op jit(solution)/shard_map/ppermute | solution.py:625
  85.4 3.8 %collective-permute-start.22 = (f32[96,128]{1,0:T(8,128)S(1)}, f32[96,128]{1,0:T(8,128)S(1)}, u32[]{:S(2)}, u32[]{:S(2)}) collective-permute-start(f32[96,128]{1,0:T(8,128)S(1)} %get-tuple-element.68), channel_id=1, source_target_pairs={{0,64},{8,72},{16,80},{24,88},{32,96},{40,104},{48,112},{56,120},{... | collective-permute-start | bytes 147464 | tf_op jit(solution)/shard_map/ppermute | solution.py:625
  89.2 3.3 %collective-permute-done.22 = f32[96,128]{1,0:T(8,128)S(1)} collective-permute-done((f32[96,128]{1,0:T(8,128)S(1)}, f32[96,128]{1,0:T(8,128)S(1)}, u32[]{:S(2)}, u32[]{:S(2)}) %collective-permute-start.22) | collective-permute-done | bytes 49184 | tf_op jit(solution)/shard_map/ppermute | solution.py:625
  92.5 9.8 %collective-permute-start.23 = (f32[96,128]{1,0:T(8,128)S(1)}, f32[96,128]{1,0:T(8,128)S(1)}, u32[]{:S(2)}, u32[]{:S(2)}) collective-permute-start(f32[96,128]{1,0:T(8,128)S(1)} %add.5.terms), channel_id=1, source_target_pairs={{0,128},{8,136},{16,144},{24,152},{32,160},{40,168},{48,176},{56,1... | collective-permute-start | bytes 147464 | tf_op jit(solution)/shard_map/ppermute | solution.py:625
  102.3 2.1 %collective-permute-done.23.other = f32[96,128]{1,0:T(8,128)S(1)} collective-permute-done((f32[96,128]{1,0:T(8,128)S(1)}, f32[96,128]{1,0:T(8,128)S(1)}, u32[]{:S(2)}, u32[]{:S(2)}) %collective-permute-start.23) | collective-permute-done | bytes 49184 | tf_op jit(solution)/shard_map/ppermute | solution.py:625
  105.5 2.1 %shard_map.111 = bf16[3,144,192]{2,1,0:T(8,128)(2,1)} custom-call(bf16[656,128]{1,0:T(8,128)(2,1)S(1)} %get-tuple-element.57.top, bf16[656,128]{1,0:T(8,128)(2,1)S(1)} %get-tuple-element.56.own, bf16[656,128]{1,0:T(8,128)(2,1)S(1)} %get-tuple-element.58.bot, f32[49,256]{1,0:T(8,128)S(1)} %get-tuple-element.39.k_ref, ...), custom_call_target="tpu_custom_call" | custom-call | flops 8388608 | bytes 1048576 | tf_op jit(solution)/shard_map/pallas_call | solution.py:470
  107.6 3.3 %collective-permute-done.24.refs_2_ = bf16[112,768]{1,0:T(8,128)(2,1)S(1)} collective-permute-done((bf16[112,768]{1,0:T(8,128)(2,1)S(1)}, bf16[112,768]{1,0:T(8,128)(2,1)S(1)}, u32[]{:S(2)}, u32[]{:S(2)}) %collective-permute-start.24) | collective-permute-done | bytes 172064 | tf_op jit(solution)/shard_map/ppermute | solution.py:655
  (45 shorter events, 25.1 us)
Async XLA Ops:
  7.2 97.2 %reduce-scatter.2.cloned.1.call-start = ((), (), s32[]{:S(2)}) async-start(), calls=%async_computation.1 | async-start | bytes 2654208 | tf_op jit(solution)/shard_map/reduce_scatter | solution.py:611
  8.3 7.9 %collective-permute-start.1 = (bf16[656,128]{1,0:T(8,128)(2,1)S(1)}, bf16[656,128]{1,0:T(8,128)(2,1)S(1)}, u32[]{:S(2)}, u32[]{:S(2)}) collective-permute-start(bf16[656,128]{1,0:T(8,128)(2,1)S(1)} %shard_map.102.own), channel_id=1, source_target_pairs={{8,0},{16,8},{24,16},{32,24},{40,32},{48,40},{56,48},{64,56},{72,6... | collective-permute-start | bytes 503816 | tf_op jit(solution)/shard_map/ppermute | solution.py:500
  9.6 6.6 %collective-permute-start = (bf16[656,128]{1,0:T(8,128)(2,1)S(1)}, bf16[656,128]{1,0:T(8,128)(2,1)S(1)}, u32[]{:S(2)}, u32[]{:S(2)}) collective-permute-start(bf16[656,128]{1,0:T(8,128)(2,1)S(1)} %shard_map.102.own), channel_id=1, source_target_pairs={{0,8},{8,16},{16,24},{24,32},{32,40},{40,48},{48,56},{56,64},{64,7... | collective-permute-start | bytes 503816 | tf_op jit(solution)/shard_map/ppermute | solution.py:499
  17.6 8.6 %collective-permute-start.5 = (bf16[656,128]{1,0:T(8,128)(2,1)S(1)}, bf16[656,128]{1,0:T(8,128)(2,1)S(1)}, u32[]{:S(2)}, u32[]{:S(2)}) collective-permute-start(bf16[656,128]{1,0:T(8,128)(2,1)S(1)} %shard_map.104.refs_0_.conv), channel_id=1, source_target_pairs={{0,4},{1,5},{2,6},{3,7},{4,0},{5,1},{6,2},{7,3},{8,12},{9,13},{10,... | collective-permute-start | bytes 503816 | tf_op jit(solution)/shard_map/ppermute | solution.py:553
  20.0 9.4 %collective-permute-start.2 = (bf16[656,128]{1,0:T(8,128)(2,1)S(1)}, bf16[656,128]{1,0:T(8,128)(2,1)S(1)}, u32[]{:S(2)}, u32[]{:S(2)}) collective-permute-start(bf16[656,128]{1,0:T(8,128)(2,1)S(1)} %shard_map.104.refs_0_.conv), channel_id=1, source_target_pairs={{0,1},{1,0},{2,3},{3,2},{4,5},{5,4},{6,7},{7,6},{8,9},{9,8},{10,11... | collective-permute-start | bytes 503816 | tf_op jit(solution)/shard_map/ppermute | solution.py:553
  23.0 8.4 %collective-permute-start.7 = (bf16[656,128]{1,0:T(8,128)(2,1)S(1)}, bf16[656,128]{1,0:T(8,128)(2,1)S(1)}, u32[]{:S(2)}, u32[]{:S(2)}) collective-permute-start(bf16[656,128]{1,0:T(8,128)(2,1)S(1)} %shard_map.104.refs_0_.conv), channel_id=1, source_target_pairs={{0,2},{1,3},{2,4},{3,5},{4,6},{5,7},{6,0},{7,1},{8,10},{9,11},{10,... | collective-permute-start | bytes 503816 | tf_op jit(solution)/shard_map/ppermute | solution.py:553
  23.0 8.4 %collective-permute-start.3 = (bf16[656,128]{1,0:T(8,128)(2,1)S(1)}, bf16[656,128]{1,0:T(8,128)(2,1)S(1)}, u32[]{:S(2)}, u32[]{:S(2)}) collective-permute-start(bf16[656,128]{1,0:T(8,128)(2,1)S(1)} %shard_map.104.refs_0_.conv), channel_id=1, source_target_pairs={{0,6},{1,7},{2,0},{3,1},{4,2},{5,3},{6,4},{7,5},{8,14},{9,15},{10,... | collective-permute-start | bytes 503816 | tf_op jit(solution)/shard_map/ppermute | solution.py:553
  26.3 7.9 %collective-permute-start.6 = (bf16[656,128]{1,0:T(8,128)(2,1)S(1)}, bf16[656,128]{1,0:T(8,128)(2,1)S(1)}, u32[]{:S(2)}, u32[]{:S(2)}) collective-permute-start(bf16[656,128]{1,0:T(8,128)(2,1)S(1)} %collective-permute-done.5.refs_4_), channel_id=1, source_target_pairs={{0,1},{1,0},{2,3},{3,2},{4,5},{5,4},{6,7},{7,6},{8,9},{9,8},{10,11... | collective-permute-start | bytes 503816 | tf_op jit(solution)/shard_map/ppermute | solution.py:553
  29.4 6.2 %collective-permute-start.8 = (bf16[656,128]{1,0:T(8,128)(2,1)S(1)}, bf16[656,128]{1,0:T(8,128)(2,1)S(1)}, u32[]{:S(2)}, u32[]{:S(2)}) collective-permute-start(bf16[656,128]{1,0:T(8,128)(2,1)S(1)} %collective-permute-done.2.refs_1_), channel_id=1, source_target_pairs={{0,2},{1,3},{2,4},{3,5},{4,6},{5,7},{6,0},{7,1},{8,10},{9,11},{10,... | collective-permute-start | bytes 503816 | tf_op jit(solution)/shard_map/ppermute | solution.py:553
  31.0 5.9 %collective-permute-start.4 = (bf16[656,128]{1,0:T(8,128)(2,1)S(1)}, bf16[656,128]{1,0:T(8,128)(2,1)S(1)}, u32[]{:S(2)}, u32[]{:S(2)}) collective-permute-start(bf16[656,128]{1,0:T(8,128)(2,1)S(1)} %collective-permute-done.2.refs_1_), channel_id=1, source_target_pairs={{0,6},{1,7},{2,0},{3,1},{4,2},{5,3},{6,4},{7,5},{8,14},{9,15},{10,... | collective-permute-start | bytes 503816 | tf_op jit(solution)/shard_map/ppermute | solution.py:553
  45.0 3.1 %collective-permute-start.20 = (bf16[8,2,48,768]{3,2,1,0:T(8,128)(2,1)S(1)}, bf16[8,2,48,768]{3,2,1,0:T(8,128)(2,1)S(1)}, u32[]{:S(2)}, u32[]{:S(2)}) collective-permute-start(bf16[8,2,48,768]{3,2,1,0:T(8,128)(2,1)S(1)} %get-tuple-element.63), channel_id=1, source_target_pairs={{0,8},{8,0},{16,24},{24,16},{32,40},{40,32},{48,56},{56,48},{64,72... | collective-permute-start | bytes 3538952 | tf_op jit(solution)/shard_map/ppermute | solution.py:601
  49.7 8.4 %collective-permute-start.9 = (bf16[704,128]{1,0:T(8,128)(2,1)S(1)}, bf16[704,128]{1,0:T(8,128)(2,1)S(1)}, u32[]{:S(2)}, u32[]{:S(2)}) collective-permute-start(bf16[704,128]{1,0:T(8,128)(2,1)S(1)} %get-tuple-element.45), channel_id=1, source_target_pairs={{0,1},{1,0},{2,3},{3,2},{4,5},{5,4},{6,7},{7,6},{8,9},{9,8},{10,11... | collective-permute-start | bytes 540680 | tf_op jit(solution)/shard_map/ppermute | solution.py:553
  50.5 10.0 %collective-permute-start.13 = (bf16[704,128]{1,0:T(8,128)(2,1)S(1)}, bf16[704,128]{1,0:T(8,128)(2,1)S(1)}, u32[]{:S(2)}, u32[]{:S(2)}) collective-permute-start(bf16[704,128]{1,0:T(8,128)(2,1)S(1)} %get-tuple-element.49), channel_id=1, source_target_pairs={{0,2},{1,3},{2,4},{3,5},{4,6},{5,7},{6,0},{7,1},{8,10},{9,11},{10,... | collective-permute-start | bytes 540680 | tf_op jit(solution)/shard_map/ppermute | solution.py:553
  52.5 8.3 %collective-permute-start.14 = (bf16[704,128]{1,0:T(8,128)(2,1)S(1)}, bf16[704,128]{1,0:T(8,128)(2,1)S(1)}, u32[]{:S(2)}, u32[]{:S(2)}) collective-permute-start(bf16[704,128]{1,0:T(8,128)(2,1)S(1)} %get-tuple-element.50), channel_id=1, source_target_pairs={{0,6},{1,7},{2,0},{3,1},{4,2},{5,3},{6,4},{7,5},{8,14},{9,15},{10,... | collective-permute-start | bytes 540680 | tf_op jit(solution)/shard_map/ppermute | solution.py:553
  53.1 10.6 %collective-permute-start.11 = (bf16[704,128]{1,0:T(8,128)(2,1)S(1)}, bf16[704,128]{1,0:T(8,128)(2,1)S(1)}, u32[]{:S(2)}, u32[]{:S(2)}) collective-permute-start(bf16[704,128]{1,0:T(8,128)(2,1)S(1)} %get-tuple-element.46), channel_id=1, source_target_pairs={{0,2},{1,3},{2,4},{3,5},{4,6},{5,7},{6,0},{7,1},{8,10},{9,11},{10,... | collective-permute-start | bytes 540680 | tf_op jit(solution)/shard_map/ppermute | solution.py:553
  55.5 8.4 %collective-permute-start.12 = (bf16[704,128]{1,0:T(8,128)(2,1)S(1)}, bf16[704,128]{1,0:T(8,128)(2,1)S(1)}, u32[]{:S(2)}, u32[]{:S(2)}) collective-permute-start(bf16[704,128]{1,0:T(8,128)(2,1)S(1)} %get-tuple-element.47), channel_id=1, source_target_pairs={{0,6},{1,7},{2,0},{3,1},{4,2},{5,3},{6,4},{7,5},{8,14},{9,15},{10,... | collective-permute-start | bytes 540680 | tf_op jit(solution)/shard_map/ppermute | solution.py:553
  58.3 10.6 %collective-permute-start.10 = (bf16[704,128]{1,0:T(8,128)(2,1)S(1)}, bf16[704,128]{1,0:T(8,128)(2,1)S(1)}, u32[]{:S(2)}, u32[]{:S(2)}) collective-permute-start(bf16[704,128]{1,0:T(8,128)(2,1)S(1)} %shard_map.106), channel_id=1, source_target_pairs={{0,4},{1,5},{2,6},{3,7},{4,0},{5,1},{6,2},{7,3},{8,12},{9,13},{10,... | collective-permute-start | bytes 540680 | tf_op jit(solution)/shard_map/ppermute | solution.py:553
  61.1 7.8 %collective-permute-start.15 = (bf16[704,128]{1,0:T(8,128)(2,1)S(1)}, bf16[704,128]{1,0:T(8,128)(2,1)S(1)}, u32[]{:S(2)}, u32[]{:S(2)}) collective-permute-start(bf16[704,128]{1,0:T(8,128)(2,1)S(1)} %shard_map.107), channel_id=1, source_target_pairs={{0,1},{1,0},{2,3},{3,2},{4,5},{5,4},{6,7},{7,6},{8,9},{9,8},{10,11... | collective-permute-start | bytes 540680 | tf_op jit(solution)/shard_map/ppermute | solution.py:553
  72.5 12.8 %collective-permute-start.19 = (bf16[656,128]{1,0:T(8,128)(2,1)S(1)}, bf16[656,128]{1,0:T(8,128)(2,1)S(1)}, u32[]{:S(2)}, u32[]{:S(2)}) collective-permute-start(bf16[656,128]{1,0:T(8,128)(2,1)S(1)} %get-tuple-element.56.own), channel_id=1, source_target_pairs={{8,0},{16,8},{24,16},{32,24},{40,32},{48,40},{56,48},{64,56},{72,6... | collective-permute-start | bytes 503816 | tf_op jit(solution)/shard_map/ppermute | solution.py:500
  73.8 11.5 %collective-permute-start.18 = (bf16[656,128]{1,0:T(8,128)(2,1)S(1)}, bf16[656,128]{1,0:T(8,128)(2,1)S(1)}, u32[]{:S(2)}, u32[]{:S(2)}) collective-permute-start(bf16[656,128]{1,0:T(8,128)(2,1)S(1)} %get-tuple-element.56.own), channel_id=1, source_target_pairs={{0,8},{8,16},{16,24},{24,32},{32,40},{40,48},{48,56},{56,64},{64,7... | collective-permute-start | bytes 503816 | tf_op jit(solution)/shard_map/ppermute | solution.py:499
  76.9 8.5 %collective-permute-start.17 = (f32[96,128]{1,0:T(8,128)S(1)}, f32[96,128]{1,0:T(8,128)S(1)}, u32[]{:S(2)}, u32[]{:S(2)}) collective-permute-start(f32[96,128]{1,0:T(8,128)S(1)} %get-tuple-element.55.terms), channel_id=1, source_target_pairs={{0,32},{8,40},{16,48},{24,56},{32,0},{40,8},{48,16},{56,24},{64,96... | collective-permute-start | bytes 147464 | tf_op jit(solution)/shard_map/ppermute | solution.py:625
  85.4 7.1 %collective-permute-start.22 = (f32[96,128]{1,0:T(8,128)S(1)}, f32[96,128]{1,0:T(8,128)S(1)}, u32[]{:S(2)}, u32[]{:S(2)}) collective-permute-start(f32[96,128]{1,0:T(8,128)S(1)} %get-tuple-element.68), channel_id=1, source_target_pairs={{0,64},{8,72},{16,80},{24,88},{32,96},{40,104},{48,112},{56,120},{... | collective-permute-start | bytes 147464 | tf_op jit(solution)/shard_map/ppermute | solution.py:625
  92.5 11.9 %collective-permute-start.23 = (f32[96,128]{1,0:T(8,128)S(1)}, f32[96,128]{1,0:T(8,128)S(1)}, u32[]{:S(2)}, u32[]{:S(2)}) collective-permute-start(f32[96,128]{1,0:T(8,128)S(1)} %add.5.terms), channel_id=1, source_target_pairs={{0,128},{8,136},{16,144},{24,152},{32,160},{40,168},{48,176},{56,1... | collective-permute-start | bytes 147464 | tf_op jit(solution)/shard_map/ppermute | solution.py:625
  105.4 5.5 %collective-permute-start.24 = (bf16[112,768]{1,0:T(8,128)(2,1)S(1)}, bf16[112,768]{1,0:T(8,128)(2,1)S(1)}, u32[]{:S(2)}, u32[]{:S(2)}) collective-permute-start(bf16[112,768]{1,0:T(8,128)(2,1)S(1)} %get-tuple-element.70.refs_1_), channel_id=1, source_target_pairs={{0,16},{8,24},{16,0},{24,8},{32,48},{40,56},{48,32},{56,40},{64,80... | collective-permute-start | bytes 516104 | tf_op jit(solution)/shard_map/ppermute | solution.py:655
  (2 other events, 4.2 us)
Sparse Core Ops, SparseCore 0:
  49.8 49.7 reduce-scatter.1

commit v3 on v2

--- a/solution.py
+++ b/solution.py
@@ -20,6 +20,7 @@
 MOM = 656
 PAY = 704
 TERMS = 96
+WEIGHTY = 1 << 35
 GRP = 48
 CALL = 1536
 FF = 768
@@ -49,6 +50,11 @@
 
 def my_core():
     return lax.axis_index("rows") % 2
+
+
+def other_neighbour():
+    pairs = [(i, i + 1) for i in range(1, 31, 2)]
+    return pairs + [(b, a) for a, b in pairs]
 
 
 def my_lo():
@@ -72,9 +78,19 @@
 
 def fill_pads(blocks, main_pad, rem_pad):
     low = lanes((8, 128)) < 64
-    for n, block in enumerate(blocks):
-        main = block[:PIX, :].astype(F32)
-        rem = block[PIX:PACK, :].astype(F32)
+    odd = my_core() == 1
+    core, own, other = blocks
+
+    def either(a, b, rows):
+        return jnp.where(odd, a[rows, :].astype(F32), b[rows, :].astype(F32))
+
+    whole, tail = slice(0, PIX), slice(PIX, PACK)
+    parts = (
+        (either(core, other, whole), either(core, other, tail)),
+        (own[whole, :].astype(F32), own[tail, :].astype(F32)),
+        (either(other, core, whole), either(other, core, tail)),
+    )
+    for n, (main, rem) in enumerate(parts):
         for i in range(ROWS):
             r = n * ROWS + i
             main_pad[r, 0:8, :] = jnp.zeros((8, 128), F32)
@@ -333,10 +349,9 @@
         payloads[s][MOM:PAY, :] = moments
 
 
-def sum_kernel(*refs):
-    o_ref = refs[-1]
+def sum_payloads(refs, o_ref):
     total = refs[0][...].astype(F32)
-    for ref in refs[1:-1]:
+    for ref in refs[1:]:
         total = total + ref[...].astype(F32)
     o_ref[:MOM, :] = total[:MOM].astype(BF16)
     moments = total[MOM:]
@@ -346,7 +361,14 @@
     o_ref[MOM:, :] = jnp.where(low, hi, pltpu.roll(lo, 16, 1)).astype(BF16)
 
 
-def norm_back_kernel(a, b, c, d, e, conv, stats, gain, top, own, bot, o_ref, terms, main_pad, rem_pad):
+def middle_sums_kernel(far, across, other, one, three, own_one, own_three, *outs):
+    sum_payloads((other, one, three), outs[0])
+    sum_payloads((far, across), outs[1])
+    outs[2][...] = own_one[...]
+    outs[3][...] = own_three[...]
+
+
+def norm_back_kernel(a, b, c, d, e, conv, stats, gain, top, own, bot, o_ref, both_ref, terms, main_pad, rem_pad):
     refs = (a, b, c, d, e)
     total = sum(ref[...].astype(F32) for ref in refs[1:]) + a[...].astype(F32)
     moments = total[MOM:]
@@ -382,6 +404,8 @@
     rem = jnp.concatenate([rem, jnp.zeros((PACK - PIX - REM, 128), F32)])
     o_ref[PIX:PACK, :] = rem.astype(BF16)
     kernel_terms(o_ref, top, own, bot, terms, main_pad, rem_pad)
+    both_ref[:PACK, :] = o_ref[...]
+    both_ref[PACK:, :] = terms[...].astype(BF16)
 
 
 def put(own, keep, send, z, xlo, zero, one):
@@ -417,61 +441,135 @@
             put(own, keep, send, z, 1, jnp.concatenate([p[96:128], q[0:16]]), q[16:64])
 
 
-def join_kernel(keep_in, got_in, keep_out, got_out, far, here, sems):
-    copies = []
+HALVES = ((0, 3, 4, 7), (1, 2, 5, 6))
+PAIRS = (((0, 1), (2, 3)), ((0, 3), (1, 2)))
+
+
+def kind_of(z):
+    return 0 if z in HALVES[0] else 1
+
+
+def pair_of(z):
+    kind = kind_of(z)
+    return next(q for q in range(2) if HALVES[kind].index(z) in PAIRS[kind][q])
+
+
+def second_partner(z):
+    return (z + (1 if z % 2 else -1)) % 8
+
+
+def third_partner(z):
+    half = HALVES[kind_of(z)]
+    pair = [half[place] for place in PAIRS[kind_of(z)][pair_of(z)]]
+    return pair[1 - pair.index(z)]
+
+
+def by_z(table):
+    z = lax.axis_index("rows") // 4
+    value = 0
+    for n, entry in enumerate(table):
+        value = jnp.where(z == n, entry, value)
+    return value
+
+
+def added(a, b):
+    return (a.astype(F32) + b.astype(F32)).astype(BF16)
+
+
+def half_blocks(n):
+    mine = by_z([HALVES[kind_of(z)][n] for z in range(8)])
+    theirs = by_z([HALVES[1 - kind_of(z)][n] for z in range(8)])
+    return mine, theirs
+
+
+def join_half_kernel(keep, got, keep_next, send_next):
+    for n in range(4):
+        mine, theirs = half_blocks(n)
+        keep_next[n] = added(keep[mine], got[mine])
+        send_next[n] = added(keep[theirs], got[theirs])
+
+
+def join_out_kernel(keep, got, keep_next, send_next):
+    lo = my_lo()
     for z in range(8):
-        for w, (keep, got) in enumerate(((keep_in, got_in), (keep_out, got_out))):
-            here[z, w] = (keep[z].astype(F32) + got[z].astype(F32)).astype(BF16)
-        copies.append(pltpu.make_async_copy(here.at[z], far.at[z], sems.at[z]))
-        copies[-1].start()
-    for copy in copies:
-        copy.wait()
-
-
-def pass_kernel(terms, got, *refs):
-    refs[len(refs) // 2][...] = terms[...] + got[...]
-    for n in range(len(refs) // 2):
-        refs[len(refs) // 2 + 1 + n][...] = refs[n][...]
-
-
-def away_kernel(far, terms, other, o_ref, held, sems):
-    copies = []
-    for w in range(2):
-        rows = pl.ds(48 * w, 48)
-        copies.append(pltpu.make_async_copy(far.at[w, 1 - my_lo()], o_ref.at[rows], sems.at[w]))
-        copies.append(pltpu.make_async_copy(far.at[w, my_lo()], held.at[rows], sems.at[2 + w]))
-    for copy in copies:
-        copy.start()
-    total = (terms[...] + other[...]).astype(BF16)
+        keep_next[z] = added(keep[z, lo], got[z, lo])
+        send_next[z] = added(keep[z, 1 - lo], got[z, 1 - lo])
+
+
+def join_lo_kernel(keep, got, keep_next, send_next):
+    lo = my_lo()
+    for n in range(4):
+        keep_next[n] = added(keep[n, lo], got[n, lo])
+        send_next[n] = added(keep[n, 1 - lo], got[n, 1 - lo])
+
+
+def put_terms(o_ref, at, total):
     for j in range(6):
-        o_ref[96:112, 128 * j : 128 * j + 128] = total[16 * j : 16 * j + 16]
-    for copy in copies:
-        copy.wait()
-
-
-def last_kernel(scale, held, away, got, grad_in, grad_out, grad_kernel):
+        o_ref[at : at + 16, 128 * j : 128 * j + 128] = total[16 * j : 16 * j + 16]
+
+
+def take_terms(ref, at):
+    return jnp.concatenate(
+        [ref[at : at + 16, 128 * j : 128 * j + 128].astype(F32) for j in range(6)], axis=0
+    )
+
+
+def join_pair_kernel(keep_in, got_in, keep_out, got_out, keep_next, send_next):
+    for n in range(2):
+        mine = by_z([PAIRS[kind_of(z)][pair_of(z)][n] for z in range(8)])
+        theirs = by_z([PAIRS[kind_of(z)][1 - pair_of(z)][n] for z in range(8)])
+        for w, (keep, other) in enumerate(((keep_in, got_in), (keep_out, got_out))):
+            rows = slice(96 * n + 48 * w, 96 * n + 48 * w + 48)
+            keep_next[rows, :] = added(keep[mine], other[mine])
+            send_next[rows, :] = added(keep[theirs], other[theirs])
+
+
+def join_one_kernel(keep, other, terms, got, keep_next, send_next):
+    second = by_z([PAIRS[kind_of(z)][pair_of(z)].index(HALVES[kind_of(z)].index(z)) for z in range(8)])
+    mine = pl.multiple_of(96 * second, 32)
+    theirs = pl.multiple_of(96 - 96 * second, 32)
+    keep_next[...] = added(keep[pl.ds(mine, 96), :], other[pl.ds(mine, 96), :])
+    send_next[:96, :] = added(keep[pl.ds(theirs, 96), :], other[pl.ds(theirs, 96), :])
+    put_terms(send_next, 96, (terms[...] + got[...]).astype(BF16))
+
+
+def pass_kernel(terms, got, block, o_ref, block_ref):
+    o_ref[...] = terms[...] + got[...]
+    block_ref[...] = block[...]
+
+
+def open_kernel(sent, got, o_ref):
+    o_ref[...] = sent[PACK:, :].astype(F32) + got[PACK:, :].astype(F32)
+
+
+def last_kernel(scale, keep, sent, got, grad_in, grad_out, grad_kernel):
     for w, ref in enumerate((grad_in, grad_out)):
         rows = slice(48 * w, 48 * w + 48)
-        ref[...] = (held[rows, :].astype(F32) + got[rows, :].astype(F32)) * scale
-    both = (away[96:112, :].astype(F32) + got[96:112, :].astype(F32)) * scale
-    lines = jnp.concatenate([both[:, 128 * j : 128 * j + 128] for j in range(6)], axis=0)
+        ref[...] = (keep[rows, :].astype(F32) + got[rows, :].astype(F32)) * scale
+    lines = (take_terms(sent, 96) + take_terms(got, 96)) * scale
     rest = jnp.concatenate([lines[64:89], swap(lines[64:96])[:24]], axis=0)
     for a in range(7):
         grad_kernel[a, :, :128] = lines[7 * a : 7 * a + 7]
         grad_kernel[a, :, 128:] = rest[7 * a : 7 * a + 7, :64]
 
 
-def call(kernel, outs, args, scratch=(), mib=16, far=(), far_out=False, flops=0, moved=0):
+def call(kernel, outs, args, scratch=(), mib=16, far=(), after=(), flops=0, moved=0):
+    count = len(args)
+    args = list(args) + list(after)
+
+    def body(*refs):
+        kernel(*refs[:count], *refs[len(args) :])
+
     near = pl.BlockSpec(memory_space=pltpu.VMEM)
     args = [pltpu.with_memory_space_constraint(a, pltpu.HBM) if n in far else a for n, a in enumerate(args)]
     hbm = pl.BlockSpec(memory_space=pltpu.HBM)
     single = not isinstance(outs, (list, tuple))
     shapes = [outs] if single else list(outs)
     result = pl.pallas_call(
-        kernel,
+        body,
         out_shape=shapes,
         in_specs=[hbm if n in far else near for n in range(len(args))],
-        out_specs=[hbm if far_out else near] * len(shapes),
+        out_specs=[near] * len(shapes),
         scratch_shapes=list(scratch),
         compiler_params=limit(mib),
         cost_estimate=pl.CostEstimate(flops=flops, bytes_accessed=moved, transcendentals=0),
@@ -495,10 +593,8 @@
     return [(i, ((i // 2 + k) % 4) * 2 + ((i % 2) ^ x)) for i in range(8)]
 
 
-def halos(block):
-    above = lax.ppermute(block, "rows", [(i, i + 1) for i in range(31)])
-    below = lax.ppermute(block, "rows", [(i + 1, i) for i in range(31)])
-    return above, below
+def other_side(block):
+    return lax.ppermute(block, "rows", other_neighbour())
 
 
 def shards(feature, kernel, ln_gain, layer_scale, w_in, w_out, cotangent):
@@ -512,7 +608,8 @@
         [pltpu.VMEM((ROWS, COLS, CH), BF16), pltpu.SemaphoreType.DMA((1,))],
         far=(0,),
     )
-    above, below = halos(packed)
+    core = rows_perm(lambda i: i ^ 1)
+    above, below = lax.ppermute(packed, "rows", core), other_side(packed)
     mixed, activ_grad, w_slot, gain_slot, gain_own, taps, cot_own = call(
         first_kernel,
         [
@@ -580,83 +677,98 @@
 
     across = shift(payload[2, 1], 0, 1)
     other = [shift(payload[k, 1], k, 0) for k in (1, 3)]
-    far_sum = call(sum_kernel, shape((PAY, 128), BF16), [payload[2, 0], across], moved=1 << 20)
-    mine = [shift(far_sum, 2, 0)] + [shift(payload[k, 0], k, 0) for k in (1, 3)]
-    other_sum = call(sum_kernel, shape((PAY, 128), BF16), [payload[0, 1]] + other, moved=1 << 20)
-    crossed = shift(other_sum, 0, 1)
-
     pairs = [shape((8, 2, 48, FF), BF16)] * 2
-    core = rows_perm(lambda i: i ^ 1)
     keep_out, send_out = call(
         weights_out_kernel, pairs, [activ, mixed], flops=2 * PIX * CALL * FF, moved=8 << 20
     )
     got_out = lax.ppermute(send_out, "rows", core)
     keep_in, send_in = call(
-        weights_in_kernel,
-        pairs,
-        [normed, grad_hidden],
-        flops=2 * PIX * CALL * FF,
-        moved=8 << 20,
+        weights_in_kernel, pairs, [normed, grad_hidden], flops=2 * PIX * CALL * FF, moved=8 << 20
     )
     got_in = lax.ppermute(send_in, "rows", core)
-    joined = call(
-        join_kernel,
-        shape((8, 2, 2, 48, FF), BF16),
-        [keep_in, got_in, keep_out, got_out],
-        [pltpu.VMEM((8, 2, 2, 48, FF), BF16), pltpu.SemaphoreType.DMA((8,))],
-        far_out=True,
-        moved=8 << 20,
-    ).reshape(8, 192, FF)
-    z_groups = [[z * 4 + q for z in range(8)] for q in range(4)]
-    z_sum = lax.psum_scatter(
-        joined, "rows", scatter_dimension=0, axis_index_groups=z_groups, tiled=True
-    ).reshape(2, 2, 48, FF)
-
-    grad_conv, terms = call(
+    other_sum, far_sum, own_one, own_three = call(
+        middle_sums_kernel,
+        [shape((PAY, 128), BF16)] * 4,
+        [payload[2, 0], across, payload[0, 1]] + other + [payload[1, 0], payload[3, 0]],
+        after=[send_out, send_in],
+        moved=1 << 20,
+    )
+    crossed = shift(other_sum, 0, 1)
+    mine = [shift(far_sum, 2, 0), shift(own_one, 1, 0), shift(own_three, 3, 0)]
+
+    def move(block, f):
+        return lax.ppermute(block, "rows", rows_perm(f))
+
+    def blocks(*dims):
+        return shape(dims + (48, FF), BF16)
+
+    def to_z(f):
+        return lambda i: 4 * f(i // 4) + i % 4
+
+    def to_lo(i):
+        return i ^ 2
+
+    def exchange(joiner, keep, got, dims, f, moved, after):
+        keep, send = call(joiner, [blocks(*dims)] * 2, [keep, got], after=[after], moved=moved)
+        return keep, move(send, f)
+
+    def first(z):
+        return z ^ 1
+
+    keep_out, got_out = exchange(join_out_kernel, keep_out, got_out, (8,), to_lo, 4 << 20, other_sum)
+    keep_in, got_in = exchange(join_half_kernel, keep_in, got_in, (4, 2), to_z(first), 4 << 20, far_sum)
+    grad_conv, sent, terms = call(
         norm_back_kernel,
-        [shape((PACK, 128), BF16), shape((TERMS, 128), F32)],
+        [shape((PACK, 128), BF16), shape((PACK + TERMS, 128), BF16), shape((TERMS, 128), F32)],
         [payload[0, 0]] + mine + [crossed, conv, stats, gain_own, above, packed, below],
         pads(),
-        flops=1 << 23,
+        flops=WEIGHTY,
         moved=2 << 20,
     )
 
     def partner_terms(terms, f):
         return lax.ppermute(terms, "rows", rows_perm(f))
 
-    def step(terms, f, *rest):
-        return call(
-            pass_kernel,
-            [shape((TERMS, 128), F32)] + [shape((PACK, 128), BF16)] * len(rest),
-            [terms, partner_terms(terms, f)] + list(rest),
-            moved=1 << 20,
-        )
-
-    terms, grad_conv = step(terms, lambda i: i ^ 1, grad_conv)
-    grad_above, grad_below = halos(grad_conv)
-    terms, grad_above, grad_below = step(terms, lambda i: i ^ 4, grad_above, grad_below)
-    terms = terms + partner_terms(terms, lambda i: i ^ 8)
+    grad_side = other_side(grad_conv)
+    grad_core = lax.ppermute(sent, "rows", core)
+    terms = call(open_kernel, shape((TERMS, 128), F32), [sent, grad_core])
+    terms = terms + partner_terms(terms, to_lo)
+    keep_out, got_out = exchange(join_half_kernel, keep_out, got_out, (4,), to_z(first), 2 << 20, terms)
+    keep_in, got_in = exchange(join_lo_kernel, keep_in, got_in, (4,), to_lo, 2 << 20, terms)
+    terms, grad_side = call(
+        pass_kernel,
+        [shape((TERMS, 128), F32), shape((PACK, 128), BF16)],
+        [terms, partner_terms(terms, to_z(first)), grad_side],
+        moved=1 << 20,
+    )
+    keep, send = call(
+        join_pair_kernel,
+        [shape((192, FF), BF16), shape((192, FF), BF16)],
+        [keep_in, got_in, keep_out, got_out],
+        after=[terms],
+        moved=2 << 20,
+    )
+    got = move(send, to_z(second_partner))
+
     grad_feature = call(
         back_kernel,
         shape((ROWS, COLS, CH), BF16),
-        [grad_above, grad_conv, grad_below, taps, cot_own],
+        [grad_core, grad_conv, grad_side, taps, cot_own],
         pads(),
         flops=1 << 23,
         moved=1 << 20,
     )
-    away, held = call(
-        away_kernel,
-        [shape((112, FF), BF16), shape((96, FF), BF16)],
-        [z_sum, terms, partner_terms(terms, lambda i: i ^ 16)],
-        [pltpu.SemaphoreType.DMA((4,))],
-        far=(0,),
+    keep, sent = call(
+        join_one_kernel,
+        [shape((96, FF), BF16), shape((112, FF), BF16)],
+        [keep, got, terms, partner_terms(terms, to_z(second_partner))],
         moved=1 << 20,
     )
-    got = lax.ppermute(away, "rows", rows_perm(lambda i: i ^ 2))
+    got = move(sent, to_z(third_partner))
     grad_in, grad_out, grad_kernel = call(
         lambda *refs: last_kernel(scale, *refs),
         [shape((48, FF), F32), shape((48, FF), F32), shape((7, 7, CH), F32)],
-        [held, away, got],
+        [keep, sent, got],
         moved=1 << 20,
     )
     return grad_feature, grad_in, grad_out.T, grad_kernel

time: 119 us -> 111 us (0.933)
  between operations: 14.2 us -> 0.79 us
  waiting for transfers between devices: 32.6 us -> 40.4 us
  starting transfers between devices: 49.4 us -> 47.3 us
  Pallas kernels: 22.3 us -> 21 us
    ppermute x5 -> x10, starting transfers between devices: 8.76 us -> 22.5 us  [the longest x6 18.2 us: move(): return lax.ppermute(block, 'rows', rows_perm(f))]
    ppermute x4 -> x3, starting transfers between devices: 15.9 us -> 3.05 us  [partner_terms(): return lax.ppermute(terms, 'rows', rows_perm(f))]
    ppermute x4 -> x3, waiting for transfers between devices: 12.8 us -> 17.9 us  [partner_terms(): return lax.ppermute(terms, 'rows', rows_perm(f))]
    ppermute x5 -> x10, waiting for transfers between devices: 3.35 us -> 7.67 us  [the longest x6 6.23 us: move(): return lax.ppermute(block, 'rows', rows_perm(f))]
    ppermute x14, starting transfers between devices: 24.1 us -> 21.1 us  [shift(): return lax.ppermute(block, 'chan', chan_shift(k, x))]
    ppermute x1, waiting for transfers between devices: 1.69 us -> 0.01 us  [shards(): got_in = lax.ppermute(send_in, 'rows', core)]
    pallas_call x15 -> x18, Pallas kernels: 22.3 us -> 21 us  [call(): pl.pallas_call(body, out_shape=shapes, in_specs=[hbm if n in far else nea...]
  transfers between devices with their start and end apart: 26 -> 29, of which waited for: 15 -> 13; matrix products, arithmetic and copies ran while one was open for 0% -> 0% of each run, Pallas kernels for 8% -> 10%
where the time goes in v3:
time: 111 us; the launch traced here: 110 us
  starting transfers between devices  47.3 us (43%)
  waiting for transfers between devices  40.4 us (36%)
  Pallas kernels  21 us (19%)
    ppermute x14, starting transfers between devices, shift(): return lax.ppermute(block, 'chan', chan_shift(k, x))  21.1 us
    pallas_call x18, Pallas kernels, call(): pl.pallas_call(body, out_shape=shapes, in_specs=[hbm if n in far else nea...  21 us
    ppermute x6, starting transfers between devices, move(): return lax.ppermute(block, 'rows', rows_perm(f))  18.2 us
    ppermute x3, waiting for transfers between devices, partner_terms(): return lax.ppermute(terms, 'rows', rows_perm(f))  17.9 us
    ppermute x14, waiting for transfers between devices, shift(): return lax.ppermute(block, 'chan', chan_shift(k, x))  14.8 us
    ppermute x6, waiting for transfers between devices, move(): return lax.ppermute(block, 'rows', rows_perm(f))  6.23 us
    ppermute x3, starting transfers between devices, partner_terms(): return lax.ppermute(terms, 'rows', rows_perm(f))  3.05 us
    ppermute x1, starting transfers between devices, shards(): above, below = (lax.ppermute(packed, 'rows', core), other_side(packed))  2.93 us
  transfers between devices with their start and end apart: 29, of which 13 were waited for; matrix products, arithmetic and copies ran while one was open for 0% of the time, Pallas kernels for 10%

profile of v3, /device:TPU:8, one launch (start us, length us, event | category | flops | bytes accessed | tf_op | source)
XLA Modules:
  0.0 109.5 jit_solution(4912971750759304689)
XLA Ops:
  2.4 2.9 %collective-permute-start = (bf16[656,128]{1,0:T(8,128)(2,1)S(1)}, bf16[656,128]{1,0:T(8,128)(2,1)S(1)}, u32[]{:S(2)}, u32[]{:S(2)}) collective-permute-start(bf16[656,128]{1,0:T(8,128)(2,1)S(1)} %shard_map.102.refs_1_.refs_9_), channel_id=1, source_target_pairs={{0,8},{8,0},{16,24},{24,16},{32,40},{40,32},{48,56},{56,48},{64,72... | collective-permute-start | bytes 503816 | tf_op jit(solution)/shard_map/ppermute | solution.py:612
  5.3 3.5 %shard_map.103 = (bf16[432,1536]{1,0:T(8,128)(2,1)S(1)}, f32[432,768]{1,0:T(8,128)S(1)}, bf16[1536,768]{1,0:T(8,128)(2,1)S(1)}, f32[1,1536]{1,0:T(1,128)S(1)}, f...) custom-call(bf16[432,1536]{1,0:T(8,128)(2,1)} %bitcast.4, f32[12,128]{1,0:T(8,128)} %bitcast.5, ...), custom_call_target="tpu_custom_call" | custom-call | flops 1019215872 | bytes 8388608 | tf_op jit(solution)/shard_map/pallas_call | solution.py:568
  10.4 2.4 %collective-permute-start.5 = (bf16[656,128]{1,0:T(8,128)(2,1)S(1)}, bf16[656,128]{1,0:T(8,128)(2,1)S(1)}, u32[]{:S(2)}, u32[]{:S(2)}) collective-permute-start(bf16[656,128]{1,0:T(8,128)(2,1)S(1)} %shard_map.104.refs_0_.refs_5_), channel_id=1, source_target_pairs={{0,4},{1,5},{2,6},{3,7},{4,0},{5,1},{6,2},{7,3},{8,12},{9,13},{10,... | collective-permute-start | bytes 503816 | tf_op jit(solution)/shard_map/ppermute | solution.py:650
  12.8 2.7 %collective-permute-start.2 = (bf16[656,128]{1,0:T(8,128)(2,1)S(1)}, bf16[656,128]{1,0:T(8,128)(2,1)S(1)}, u32[]{:S(2)}, u32[]{:S(2)}) collective-permute-start(bf16[656,128]{1,0:T(8,128)(2,1)S(1)} %shard_map.104.refs_0_.refs_5_), channel_id=1, source_target_pairs={{0,1},{1,0},{2,3},{3,2},{4,5},{5,4},{6,7},{7,6},{8,9},{9,8},{10,11... | collective-permute-start | bytes 503816 | tf_op jit(solution)/shard_map/ppermute | solution.py:650
  15.5 2.0 %collective-permute-start.3 = (bf16[656,128]{1,0:T(8,128)(2,1)S(1)}, bf16[656,128]{1,0:T(8,128)(2,1)S(1)}, u32[]{:S(2)}, u32[]{:S(2)}) collective-permute-start(bf16[656,128]{1,0:T(8,128)(2,1)S(1)} %shard_map.104.refs_0_.refs_5_), channel_id=1, source_target_pairs={{0,6},{1,7},{2,0},{3,1},{4,2},{5,3},{6,4},{7,5},{8,14},{9,15},{10,... | collective-permute-start | bytes 503816 | tf_op jit(solution)/shard_map/ppermute | solution.py:650
  18.7 3.2 %collective-permute-start.6 = (bf16[656,128]{1,0:T(8,128)(2,1)S(1)}, bf16[656,128]{1,0:T(8,128)(2,1)S(1)}, u32[]{:S(2)}, u32[]{:S(2)}) collective-permute-start(bf16[656,128]{1,0:T(8,128)(2,1)S(1)} %collective-permute-done.5.refs_4_), channel_id=1, source_target_pairs={{0,1},{1,0},{2,3},{3,2},{4,5},{5,4},{6,7},{7,6},{8,9},{9,8},{10,11... | collective-permute-start | bytes 503816 | tf_op jit(solution)/shard_map/ppermute | solution.py:650
  21.9 1.6 %collective-permute-start.8 = (bf16[656,128]{1,0:T(8,128)(2,1)S(1)}, bf16[656,128]{1,0:T(8,128)(2,1)S(1)}, u32[]{:S(2)}, u32[]{:S(2)}) collective-permute-start(bf16[656,128]{1,0:T(8,128)(2,1)S(1)} %collective-permute-done.2.refs_1_), channel_id=1, source_target_pairs={{0,2},{1,3},{2,4},{3,5},{4,6},{5,7},{6,0},{7,1},{8,10},{9,11},{10,... | collective-permute-start | bytes 503816 | tf_op jit(solution)/shard_map/ppermute | solution.py:650
  23.9 2.1 %collective-permute-done.6.refs_5_ = bf16[656,128]{1,0:T(8,128)(2,1)S(1)} collective-permute-done((bf16[656,128]{1,0:T(8,128)(2,1)S(1)}, bf16[656,128]{1,0:T(8,128)(2,1)S(1)}, u32[]{:S(2)}, u32[]{:S(2)}) %collective-permute-start.6) | collective-permute-done | bytes 167968 | tf_op jit(solution)/shard_map/ppermute | solution.py:650
  28.8 5.3 %shard_map.105 = (bf16[432,1536]{1,0:T(8,128)(2,1)S(1)}, bf16[432,768]{1,0:T(8,128)(2,1)S(1)}, bf16[432,768]{1,0:T(8,128)(2,1)S(1)}, f32[432,128]{1,0:T(8,128)S(...) custom-call(bf16[656,128]{1,0:T(8,128)(2,1)S(1)} %shard_map.104.refs, ...), custom_call_target="tpu_custom_call" | custom-call | flops 2038431744 | bytes 8388608 | tf_op jit(solution)/shard_map/pallas_call | solution.py:568
  40.5 5.3 %collective-permute-done.9.refs_1_ = bf16[704,128]{1,0:T(8,128)(2,1)S(1)} collective-permute-done((bf16[704,128]{1,0:T(8,128)(2,1)S(1)}, bf16[704,128]{1,0:T(8,128)(2,1)S(1)}, u32[]{:S(2)}, u32[]{:S(2)}) %collective-permute-start.9) | collective-permute-done | bytes 180256 | tf_op jit(solution)/shard_map/ppermute | solution.py:650
  47.4 1.8 %collective-permute-start.13 = (bf16[704,128]{1,0:T(8,128)(2,1)S(1)}, bf16[704,128]{1,0:T(8,128)(2,1)S(1)}, u32[]{:S(2)}, u32[]{:S(2)}) collective-permute-start(bf16[704,128]{1,0:T(8,128)(2,1)S(1)} %get-tuple-element.69), channel_id=1, source_target_pairs={{0,2},{1,3},{2,4},{3,5},{4,6},{5,7},{6,0},{7,1},{8,10},{9,11},{10,... | collective-permute-start | bytes 540680 | tf_op jit(solution)/shard_map/ppermute | solution.py:650
  49.5 2.7 %collective-permute-start.12 = (bf16[704,128]{1,0:T(8,128)(2,1)S(1)}, bf16[704,128]{1,0:T(8,128)(2,1)S(1)}, u32[]{:S(2)}, u32[]{:S(2)}) collective-permute-start(bf16[704,128]{1,0:T(8,128)(2,1)S(1)} %get-tuple-element.68.refs_2_), channel_id=1, source_target_pairs={{0,4},{1,5},{2,6},{3,7},{4,0},{5,1},{6,2},{7,3},{8,12},{9,13},{10,... | collective-permute-start | bytes 540680 | tf_op jit(solution)/shard_map/ppermute | solution.py:650
  53.6 1.9 %collective-permute-start.24 = (bf16[8,48,768]{2,1,0:T(8,128)(2,1)S(1)}, bf16[8,48,768]{2,1,0:T(8,128)(2,1)S(1)}, u32[]{:S(2)}, u32[]{:S(2)}) collective-permute-start(bf16[8,48,768]{2,1,0:T(8,128)(2,1)S(1)} %get-tuple-element.85), channel_id=1, source_target_pairs={{0,16},{8,24},{16,0},{24,8},{32,48},{40,56},{48,32},{56,40},{64,80... | collective-permute-start | bytes 1769480 | tf_op jit(solution)/shard_map/ppermute | solution.py:700
  56.1 3.0 %collective-permute-start.21 = (bf16[4,2,48,768]{3,2,1,0:T(8,128)(2,1)S(1)}, bf16[4,2,48,768]{3,2,1,0:T(8,128)(2,1)S(1)}, u32[]{:S(2)}, u32[]{:S(2)}) collective-permute-start(bf16[4,2,48,768]{3,2,1,0:T(8,128)(2,1)S(1)} %get-tuple-element.80), channel_id=1, source_target_pairs={{0,32},{8,40},{16,48},{24,56},{32,0},{40,8},{48,16},{56,24},{64,96... | collective-permute-start | bytes 1769480 | tf_op jit(solution)/shard_map/ppermute | solution.py:700
  59.1 2.0 %collective-permute-done.15.refs_4_ = bf16[704,128]{1,0:T(8,128)(2,1)S(1)} collective-permute-done((bf16[704,128]{1,0:T(8,128)(2,1)S(1)}, bf16[704,128]{1,0:T(8,128)(2,1)S(1)}, u32[]{:S(2)}, u32[]{:S(2)}) %collective-permute-start.15) | collective-permute-done | bytes 180256 | tf_op jit(solution)/shard_map/ppermute | solution.py:650
  61.0 2.4 %shard_map.109 = (bf16[656,128]{1,0:T(8,128)(2,1)S(1)}, bf16[752,128]{1,0:T(8,128)(2,1)S(1)}, f32[96,128]{1,0:T(8,128)}) custom-call(bf16[704,128]{1,0:T(8,128)(2,1)S(1)} %get-tuple-element.54.refs_0_, bf16[704,128]{1,0:T(8,128)(2,1)S(1)} %collective-permute-done.12.refs_1_, bf16[704,128]{1,0:T(8,128)(2,1)S(1)} %collective-permute-done.13.refs_2_, ...), custom_call_target="tpu_custom_call" | custom-call | flops 34359738368 | bytes 2097152 | tf_op jit(solution)/shard_map/pallas_call | solution.py:568
  66.3 4.8 %collective-permute-done.17 = f32[96,128]{1,0:T(8,128)S(1)} collective-permute-done((f32[96,128]{1,0:T(8,128)S(1)}, f32[96,128]{1,0:T(8,128)S(1)}, u32[]{:S(2)}, u32[]{:S(2)}) %collective-permute-start.17) | collective-permute-done | bytes 49184 | tf_op jit(solution)/shard_map/ppermute | solution.py:730
  71.3 2.0 %collective-permute-start.25 = (bf16[4,48,768]{2,1,0:T(8,128)(2,1)S(1)}, bf16[4,48,768]{2,1,0:T(8,128)(2,1)S(1)}, u32[]{:S(2)}, u32[]{:S(2)}) collective-permute-start(bf16[4,48,768]{2,1,0:T(8,128)(2,1)S(1)} %get-tuple-element.87), channel_id=1, source_target_pairs={{0,32},{8,40},{16,48},{24,56},{32,0},{40,8},{48,16},{56,24},{64,96... | collective-permute-start | bytes 884744 | tf_op jit(solution)/shard_map/ppermute | solution.py:700
  77.0 5.3 %collective-permute-done.18.refs_1_ = f32[96,128]{1,0:T(8,128)S(1)} collective-permute-done((f32[96,128]{1,0:T(8,128)S(1)}, f32[96,128]{1,0:T(8,128)S(1)}, u32[]{:S(2)}, u32[]{:S(2)}) %collective-permute-start.18) | collective-permute-done | bytes 49184 | tf_op jit(solution)/shard_map/ppermute | solution.py:730
  82.5 5.6 %collective-permute-start.26 = (bf16[192,768]{1,0:T(8,128)(2,1)S(1)}, bf16[192,768]{1,0:T(8,128)(2,1)S(1)}, u32[]{:S(2)}, u32[]{:S(2)}) collective-permute-start(bf16[192,768]{1,0:T(8,128)(2,1)S(1)} %get-tuple-element.90), channel_id=1, source_target_pairs={{0,224},{8,232},{16,240},{24,248},{32,64},{40,72},{48,80},{56,88},... | collective-permute-start | bytes 884744 | tf_op jit(solution)/shard_map/ppermute | solution.py:700
  88.2 7.8 %collective-permute-done.27.refs_3_ = f32[96,128]{1,0:T(8,128)S(1)} collective-permute-done((f32[96,128]{1,0:T(8,128)S(1)}, f32[96,128]{1,0:T(8,128)S(1)}, u32[]{:S(2)}, u32[]{:S(2)}) %collective-permute-start.27) | collective-permute-done | bytes 49184 | tf_op jit(solution)/shard_map/ppermute | solution.py:730
  96.1 4.3 %collective-permute-start.28 = (bf16[112,768]{1,0:T(8,128)(2,1)S(1)}, bf16[112,768]{1,0:T(8,128)(2,1)S(1)}, u32[]{:S(2)}, u32[]{:S(2)}) collective-permute-start(bf16[112,768]{1,0:T(8,128)(2,1)S(1)} %get-tuple-element.92.refs_1_), channel_id=1, source_target_pairs={{0,96},{8,104},{16,112},{24,120},{32,192},{40,200},{48,208},{56,21... | collective-permute-start | bytes 516104 | tf_op jit(solution)/shard_map/ppermute | solution.py:700
  100.4 2.1 %shard_map.112 = bf16[3,144,192]{2,1,0:T(8,128)(2,1)} custom-call(bf16[752,128]{1,0:T(8,128)(2,1)S(1)} %collective-permute-done.16.refs_1_.refs_0_, bf16[656,128]{1,0:T(8,128)(2,1)S(1)} %get-tuple-element.75.refs_1_, bf16[656,128]{1,0:T(8,128)(2,1)S(1)} %get-tuple-element.76.refs_2_, f32[49,256]{1,0:T(8,128)S(1)} %get-tuple-element.50.refs_3_, ...), custom_call_target="tpu_custom_call" | custom-call | flops 8388608 | bytes 1048576 | tf_op jit(solution)/shard_map/pallas_call | solution.py:568
  102.5 6.2 %collective-permute-done.28.refs_2_ = bf16[112,768]{1,0:T(8,128)(2,1)S(1)} collective-permute-done((bf16[112,768]{1,0:T(8,128)(2,1)S(1)}, bf16[112,768]{1,0:T(8,128)(2,1)S(1)}, u32[]{:S(2)}, u32[]{:S(2)}) %collective-permute-start.28) | collective-permute-done | bytes 172064 | tf_op jit(solution)/shard_map/ppermute | solution.py:700
  (53 shorter events, 25.8 us)
Async XLA Ops:
  1.7 7.2 %collective-permute-start.1 = (bf16[656,128]{1,0:T(8,128)(2,1)S(1)}, bf16[656,128]{1,0:T(8,128)(2,1)S(1)}, u32[]{:S(2)}, u32[]{:S(2)}) collective-permute-start(bf16[656,128]{1,0:T(8,128)(2,1)S(1)} %shard_map.102.refs_1_.refs_9_), channel_id=1, source_target_pairs={{8,16},{24,32},{40,48},{56,64},{72,80},{88,96},{104,112},{120,128}... | collective-permute-start | bytes 503816 | tf_op jit(solution)/shard_map/ppermute | solution.py:597
  2.4 6.5 %collective-permute-start = (bf16[656,128]{1,0:T(8,128)(2,1)S(1)}, bf16[656,128]{1,0:T(8,128)(2,1)S(1)}, u32[]{:S(2)}, u32[]{:S(2)}) collective-permute-start(bf16[656,128]{1,0:T(8,128)(2,1)S(1)} %shard_map.102.refs_1_.refs_9_), channel_id=1, source_target_pairs={{0,8},{8,0},{16,24},{24,16},{32,40},{40,32},{48,56},{56,48},{64,72... | collective-permute-start | bytes 503816 | tf_op jit(solution)/shard_map/ppermute | solution.py:612
  10.4 8.3 %collective-permute-start.5 = (bf16[656,128]{1,0:T(8,128)(2,1)S(1)}, bf16[656,128]{1,0:T(8,128)(2,1)S(1)}, u32[]{:S(2)}, u32[]{:S(2)}) collective-permute-start(bf16[656,128]{1,0:T(8,128)(2,1)S(1)} %shard_map.104.refs_0_.refs_5_), channel_id=1, source_target_pairs={{0,4},{1,5},{2,6},{3,7},{4,0},{5,1},{6,2},{7,3},{8,12},{9,13},{10,... | collective-permute-start | bytes 503816 | tf_op jit(solution)/shard_map/ppermute | solution.py:650
  12.8 9.1 %collective-permute-start.2 = (bf16[656,128]{1,0:T(8,128)(2,1)S(1)}, bf16[656,128]{1,0:T(8,128)(2,1)S(1)}, u32[]{:S(2)}, u32[]{:S(2)}) collective-permute-start(bf16[656,128]{1,0:T(8,128)(2,1)S(1)} %shard_map.104.refs_0_.refs_5_), channel_id=1, source_target_pairs={{0,1},{1,0},{2,3},{3,2},{4,5},{5,4},{6,7},{7,6},{8,9},{9,8},{10,11... | collective-permute-start | bytes 503816 | tf_op jit(solution)/shard_map/ppermute | solution.py:650
  15.5 8.4 %collective-permute-start.7 = (bf16[656,128]{1,0:T(8,128)(2,1)S(1)}, bf16[656,128]{1,0:T(8,128)(2,1)S(1)}, u32[]{:S(2)}, u32[]{:S(2)}) collective-permute-start(bf16[656,128]{1,0:T(8,128)(2,1)S(1)} %shard_map.104.refs_0_.refs_5_), channel_id=1, source_target_pairs={{0,2},{1,3},{2,4},{3,5},{4,6},{5,7},{6,0},{7,1},{8,10},{9,11},{10,... | collective-permute-start | bytes 503816 | tf_op jit(solution)/shard_map/ppermute | solution.py:650
  15.5 8.4 %collective-permute-start.3 = (bf16[656,128]{1,0:T(8,128)(2,1)S(1)}, bf16[656,128]{1,0:T(8,128)(2,1)S(1)}, u32[]{:S(2)}, u32[]{:S(2)}) collective-permute-start(bf16[656,128]{1,0:T(8,128)(2,1)S(1)} %shard_map.104.refs_0_.refs_5_), channel_id=1, source_target_pairs={{0,6},{1,7},{2,0},{3,1},{4,2},{5,3},{6,4},{7,5},{8,14},{9,15},{10,... | collective-permute-start | bytes 503816 | tf_op jit(solution)/shard_map/ppermute | solution.py:650
  18.7 7.3 %collective-permute-start.6 = (bf16[656,128]{1,0:T(8,128)(2,1)S(1)}, bf16[656,128]{1,0:T(8,128)(2,1)S(1)}, u32[]{:S(2)}, u32[]{:S(2)}) collective-permute-start(bf16[656,128]{1,0:T(8,128)(2,1)S(1)} %collective-permute-done.5.refs_4_), channel_id=1, source_target_pairs={{0,1},{1,0},{2,3},{3,2},{4,5},{5,4},{6,7},{7,6},{8,9},{9,8},{10,11... | collective-permute-start | bytes 503816 | tf_op jit(solution)/shard_map/ppermute | solution.py:650
  35.5 16.6 %collective-permute-start.23 = (bf16[8,2,48,768]{3,2,1,0:T(8,128)(2,1)S(1)}, bf16[8,2,48,768]{3,2,1,0:T(8,128)(2,1)S(1)}, u32[]{:S(2)}, u32[]{:S(2)}) collective-permute-start(bf16[8,2,48,768]{3,2,1,0:T(8,128)(2,1)S(1)} %get-tuple-element.64.refs_7_), channel_id=1, source_target_pairs={{0,8},{8,0},{16,24},{24,16},{32,40},{40,32},{48,56},{56,48},{64,72... | collective-permute-start | bytes 3538952 | tf_op jit(solution)/shard_map/ppermute | solution.py:684
  37.1 16.5 %collective-permute-start.20 = (bf16[8,2,48,768]{3,2,1,0:T(8,128)(2,1)S(1)}, bf16[8,2,48,768]{3,2,1,0:T(8,128)(2,1)S(1)}, u32[]{:S(2)}, u32[]{:S(2)}) collective-permute-start(bf16[8,2,48,768]{3,2,1,0:T(8,128)(2,1)S(1)} %get-tuple-element.67.refs_8_), channel_id=1, source_target_pairs={{0,8},{8,0},{16,24},{24,16},{32,40},{40,32},{48,56},{56,48},{64,72... | collective-permute-start | bytes 3538952 | tf_op jit(solution)/shard_map/ppermute | solution.py:688
  37.7 8.1 %collective-permute-start.9 = (bf16[704,128]{1,0:T(8,128)(2,1)S(1)}, bf16[704,128]{1,0:T(8,128)(2,1)S(1)}, u32[]{:S(2)}, u32[]{:S(2)}) collective-permute-start(bf16[704,128]{1,0:T(8,128)(2,1)S(1)} %get-tuple-element.56), channel_id=1, source_target_pairs={{0,1},{1,0},{2,3},{3,2},{4,5},{5,4},{6,7},{7,6},{8,9},{9,8},{10,11... | collective-permute-start | bytes 540680 | tf_op jit(solution)/shard_map/ppermute | solution.py:650
  38.5 7.3 %collective-permute-start.10 = (bf16[704,128]{1,0:T(8,128)(2,1)S(1)}, bf16[704,128]{1,0:T(8,128)(2,1)S(1)}, u32[]{:S(2)}, u32[]{:S(2)}) collective-permute-start(bf16[704,128]{1,0:T(8,128)(2,1)S(1)} %get-tuple-element.58), channel_id=1, source_target_pairs={{0,2},{1,3},{2,4},{3,5},{4,6},{5,7},{6,0},{7,1},{8,10},{9,11},{10,... | collective-permute-start | bytes 540680 | tf_op jit(solution)/shard_map/ppermute | solution.py:650
  39.7 7.3 %collective-permute-start.11 = (bf16[704,128]{1,0:T(8,128)(2,1)S(1)}, bf16[704,128]{1,0:T(8,128)(2,1)S(1)}, u32[]{:S(2)}, u32[]{:S(2)}) collective-permute-start(bf16[704,128]{1,0:T(8,128)(2,1)S(1)} %get-tuple-element.59), channel_id=1, source_target_pairs={{0,6},{1,7},{2,0},{3,1},{4,2},{5,3},{6,4},{7,5},{8,14},{9,15},{10,... | collective-permute-start | bytes 540680 | tf_op jit(solution)/shard_map/ppermute | solution.py:650
  47.4 8.7 %collective-permute-start.13 = (bf16[704,128]{1,0:T(8,128)(2,1)S(1)}, bf16[704,128]{1,0:T(8,128)(2,1)S(1)}, u32[]{:S(2)}, u32[]{:S(2)}) collective-permute-start(bf16[704,128]{1,0:T(8,128)(2,1)S(1)} %get-tuple-element.69), channel_id=1, source_target_pairs={{0,2},{1,3},{2,4},{3,5},{4,6},{5,7},{6,0},{7,1},{8,10},{9,11},{10,... | collective-permute-start | bytes 540680 | tf_op jit(solution)/shard_map/ppermute | solution.py:650
  49.2 9.9 %collective-permute-start.14 = (bf16[704,128]{1,0:T(8,128)(2,1)S(1)}, bf16[704,128]{1,0:T(8,128)(2,1)S(1)}, u32[]{:S(2)}, u32[]{:S(2)}) collective-permute-start(bf16[704,128]{1,0:T(8,128)(2,1)S(1)} %get-tuple-element.70), channel_id=1, source_target_pairs={{0,6},{1,7},{2,0},{3,1},{4,2},{5,3},{6,4},{7,5},{8,14},{9,15},{10,... | collective-permute-start | bytes 540680 | tf_op jit(solution)/shard_map/ppermute | solution.py:650
  49.5 9.6 %collective-permute-start.12 = (bf16[704,128]{1,0:T(8,128)(2,1)S(1)}, bf16[704,128]{1,0:T(8,128)(2,1)S(1)}, u32[]{:S(2)}, u32[]{:S(2)}) collective-permute-start(bf16[704,128]{1,0:T(8,128)(2,1)S(1)} %get-tuple-element.68.refs_2_), channel_id=1, source_target_pairs={{0,4},{1,5},{2,6},{3,7},{4,0},{5,1},{6,2},{7,3},{8,12},{9,13},{10,... | collective-permute-start | bytes 540680 | tf_op jit(solution)/shard_map/ppermute | solution.py:650
  52.1 8.9 %collective-permute-start.15 = (bf16[704,128]{1,0:T(8,128)(2,1)S(1)}, bf16[704,128]{1,0:T(8,128)(2,1)S(1)}, u32[]{:S(2)}, u32[]{:S(2)}) collective-permute-start(bf16[704,128]{1,0:T(8,128)(2,1)S(1)} %get-tuple-element.71.refs_2_), channel_id=1, source_target_pairs={{0,1},{1,0},{2,3},{3,2},{4,5},{5,4},{6,7},{7,6},{8,9},{9,8},{10,11... | collective-permute-start | bytes 540680 | tf_op jit(solution)/shard_map/ppermute | solution.py:650
  53.6 17.5 %collective-permute-start.24 = (bf16[8,48,768]{2,1,0:T(8,128)(2,1)S(1)}, bf16[8,48,768]{2,1,0:T(8,128)(2,1)S(1)}, u32[]{:S(2)}, u32[]{:S(2)}) collective-permute-start(bf16[8,48,768]{2,1,0:T(8,128)(2,1)S(1)} %get-tuple-element.85), channel_id=1, source_target_pairs={{0,16},{8,24},{16,0},{24,8},{32,48},{40,56},{48,32},{56,40},{64,80... | collective-permute-start | bytes 1769480 | tf_op jit(solution)/shard_map/ppermute | solution.py:700
  56.1 17.2 %collective-permute-start.21 = (bf16[4,2,48,768]{3,2,1,0:T(8,128)(2,1)S(1)}, bf16[4,2,48,768]{3,2,1,0:T(8,128)(2,1)S(1)}, u32[]{:S(2)}, u32[]{:S(2)}) collective-permute-start(bf16[4,2,48,768]{3,2,1,0:T(8,128)(2,1)S(1)} %get-tuple-element.80), channel_id=1, source_target_pairs={{0,32},{8,40},{16,48},{24,56},{32,0},{40,8},{48,16},{56,24},{64,96... | collective-permute-start | bytes 1769480 | tf_op jit(solution)/shard_map/ppermute | solution.py:700
  71.3 11.0 %collective-permute-start.25 = (bf16[4,48,768]{2,1,0:T(8,128)(2,1)S(1)}, bf16[4,48,768]{2,1,0:T(8,128)(2,1)S(1)}, u32[]{:S(2)}, u32[]{:S(2)}) collective-permute-start(bf16[4,48,768]{2,1,0:T(8,128)(2,1)S(1)} %get-tuple-element.87), channel_id=1, source_target_pairs={{0,32},{8,40},{16,48},{24,56},{32,0},{40,8},{48,16},{56,24},{64,96... | collective-permute-start | bytes 884744 | tf_op jit(solution)/shard_map/ppermute | solution.py:700
  73.4 8.9 %collective-permute-start.22 = (bf16[4,48,768]{2,1,0:T(8,128)(2,1)S(1)}, bf16[4,48,768]{2,1,0:T(8,128)(2,1)S(1)}, u32[]{:S(2)}, u32[]{:S(2)}) collective-permute-start(bf16[4,48,768]{2,1,0:T(8,128)(2,1)S(1)} %get-tuple-element.82), channel_id=1, source_target_pairs={{0,16},{8,24},{16,0},{24,8},{32,48},{40,56},{48,32},{56,40},{64,80... | collective-permute-start | bytes 884744 | tf_op jit(solution)/shard_map/ppermute | solution.py:700
  75.4 6.8 %collective-permute-start.18 = (f32[96,128]{1,0:T(8,128)S(1)}, f32[96,128]{1,0:T(8,128)S(1)}, u32[]{:S(2)}, u32[]{:S(2)}) collective-permute-start(f32[96,128]{1,0:T(8,128)S(1)} %add.3.refs_0_.refs_2_), channel_id=1, source_target_pairs={{0,32},{8,40},{16,48},{24,56},{32,0},{40,8},{48,16},{56,24},{64,96... | collective-permute-start | bytes 147464 | tf_op jit(solution)/shard_map/ppermute | solution.py:730
  82.5 13.5 %collective-permute-start.26 = (bf16[192,768]{1,0:T(8,128)(2,1)S(1)}, bf16[192,768]{1,0:T(8,128)(2,1)S(1)}, u32[]{:S(2)}, u32[]{:S(2)}) collective-permute-start(bf16[192,768]{1,0:T(8,128)(2,1)S(1)} %get-tuple-element.90), channel_id=1, source_target_pairs={{0,224},{8,232},{16,240},{24,248},{32,64},{40,72},{48,80},{56,88},... | collective-permute-start | bytes 884744 | tf_op jit(solution)/shard_map/ppermute | solution.py:700
  88.1 7.9 %collective-permute-start.27 = (f32[96,128]{1,0:T(8,128)S(1)}, f32[96,128]{1,0:T(8,128)S(1)}, u32[]{:S(2)}, u32[]{:S(2)}) collective-permute-start(f32[96,128]{1,0:T(8,128)S(1)} %get-tuple-element.88.refs_4_.refs_2_), channel_id=1, source_target_pairs={{0,224},{8,232},{16,240},{24,248},{32,64},{40,72},{48,80},{56,88},... | collective-permute-start | bytes 147464 | tf_op jit(solution)/shard_map/ppermute | solution.py:730
  96.1 12.7 %collective-permute-start.28 = (bf16[112,768]{1,0:T(8,128)(2,1)S(1)}, bf16[112,768]{1,0:T(8,128)(2,1)S(1)}, u32[]{:S(2)}, u32[]{:S(2)}) collective-permute-start(bf16[112,768]{1,0:T(8,128)(2,1)S(1)} %get-tuple-element.92.refs_1_), channel_id=1, source_target_pairs={{0,96},{8,104},{16,112},{24,120},{32,192},{40,200},{48,208},{56,21... | collective-permute-start | bytes 516104 | tf_op jit(solution)/shard_map/ppermute | solution.py:700
  (5 other events, 20.6 us)

commit v4 on v3

--- a/solution.py
+++ b/solution.py
@@ -20,7 +20,12 @@
 MOM = 656
 PAY = 704
 TERMS = 96
-WEIGHTY = 1 << 35
+COST_BACK = 1 << 35
+COST_OUT = 1 << 30
+COST_PASS = 1 << 20
+COST_FAR = 1 << 20
+COST_IN = 1 << 30
+COST_SUMS = 1 << 20
 GRP = 48
 CALL = 1536
 FF = 768
@@ -269,8 +274,9 @@
     slots = refs[:8]
     gain, w_slot, activ_grad = refs[8:11]
     normed, activ, grad_hidden, stats = refs[11:15]
-    payloads = refs[15:23]
-    x, first, second = refs[23:]
+    payloads = list(refs[15:19]) + [refs[19].at[x] for x in range(2)] + [refs[20].at[x] for x in range(2)]
+    payloads = [payloads[n] for n in (0, 1, 4, 5, 2, 3, 6, 7)]
+    x, first, second = refs[21:]
     low = lanes((HALF, 128)) < 64
     for s in range(8):
         x[:, 128 * s : 128 * s + 128] = slots[s][:PIX, :].astype(F32)
@@ -361,16 +367,16 @@
     o_ref[MOM:, :] = jnp.where(low, hi, pltpu.roll(lo, 16, 1)).astype(BF16)
 
 
-def middle_sums_kernel(far, across, other, one, three, own_one, own_three, *outs):
-    sum_payloads((other, one, three), outs[0])
-    sum_payloads((far, across), outs[1])
-    outs[2][...] = own_one[...]
-    outs[3][...] = own_three[...]
+def far_sum_kernel(far, across, o_ref):
+    sum_payloads((far, across), o_ref)
+
+
+def other_sum_kernel(other, one, three, o_ref):
+    sum_payloads((other, one.at[1], three.at[1]), o_ref)
 
 
 def norm_back_kernel(a, b, c, d, e, conv, stats, gain, top, own, bot, o_ref, both_ref, terms, main_pad, rem_pad):
-    refs = (a, b, c, d, e)
-    total = sum(ref[...].astype(F32) for ref in refs[1:]) + a[...].astype(F32)
+    total = a[...].astype(F32) + (b[...].astype(F32) + c[0].astype(F32)) + (d[0].astype(F32) + e[...].astype(F32))
     moments = total[MOM:]
     whole = moments + pltpu.roll(moments, 128 - 16, 1)
     firsts, seconds = [], []
@@ -496,9 +502,22 @@
         send_next[z] = added(keep[z, 1 - lo], got[z, 1 - lo])
 
 
+def pair_blocks(n):
+    mine = by_z([PAIRS[kind_of(z)][pair_of(z)][n] for z in range(8)])
+    theirs = by_z([PAIRS[kind_of(z)][1 - pair_of(z)][n] for z in range(8)])
+    return mine, theirs
+
+
+def join_pair_kernel(keep, got, keep_next, send_next):
+    for n in range(2):
+        mine, theirs = pair_blocks(n)
+        keep_next[n] = added(keep[mine], got[mine])
+        send_next[n] = added(keep[theirs], got[theirs])
+
+
 def join_lo_kernel(keep, got, keep_next, send_next):
     lo = my_lo()
-    for n in range(4):
+    for n in range(2):
         keep_next[n] = added(keep[n, lo], got[n, lo])
         send_next[n] = added(keep[n, 1 - lo], got[n, 1 - lo])
 
@@ -514,22 +533,12 @@
     )
 
 
-def join_pair_kernel(keep_in, got_in, keep_out, got_out, keep_next, send_next):
-    for n in range(2):
-        mine = by_z([PAIRS[kind_of(z)][pair_of(z)][n] for z in range(8)])
-        theirs = by_z([PAIRS[kind_of(z)][1 - pair_of(z)][n] for z in range(8)])
-        for w, (keep, other) in enumerate(((keep_in, got_in), (keep_out, got_out))):
-            rows = slice(96 * n + 48 * w, 96 * n + 48 * w + 48)
-            keep_next[rows, :] = added(keep[mine], other[mine])
-            send_next[rows, :] = added(keep[theirs], other[theirs])
-
-
-def join_one_kernel(keep, other, terms, got, keep_next, send_next):
+def join_one_kernel(keep_in, got_in, keep_out, got_out, terms, got, keep_next, send_next):
     second = by_z([PAIRS[kind_of(z)][pair_of(z)].index(HALVES[kind_of(z)].index(z)) for z in range(8)])
-    mine = pl.multiple_of(96 * second, 32)
-    theirs = pl.multiple_of(96 - 96 * second, 32)
-    keep_next[...] = added(keep[pl.ds(mine, 96), :], other[pl.ds(mine, 96), :])
-    send_next[:96, :] = added(keep[pl.ds(theirs, 96), :], other[pl.ds(theirs, 96), :])
+    for w, (keep, other) in enumerate(((keep_in, got_in), (keep_out, got_out))):
+        rows = slice(48 * w, 48 * w + 48)
+        keep_next[rows, :] = added(keep[second], other[second])
+        send_next[rows, :] = added(keep[1 - second], other[1 - second])
     put_terms(send_next, 96, (terms[...] + got[...]).astype(BF16))
 
 
@@ -665,7 +674,8 @@
             shape((PIX, FF), BF16),
             shape((PIX, 128), F32),
         ]
-        + [shape((PAY, 128), BF16)] * 8,
+        + [shape((PAY, 128), BF16)] * 4
+        + [shape((2, PAY, 128), BF16)] * 2,
         [gathered[s] for s in slots] + [gain_slot, w_slot, activ_grad],
         [pltpu.VMEM((PIX, CALL), F32), pltpu.VMEM((PIX, 128), F32), pltpu.VMEM((PIX, 128), F32)],
         mib=16,
@@ -673,29 +683,32 @@
         moved=8 << 20,
     )
     normed, activ, grad_hidden, stats = outs[:4]
-    payload = dict(zip(slots, outs[4:]))
+    payload = dict(zip(((0, 0), (0, 1), (2, 0), (2, 1), 1, 3), outs[4:]))
 
     across = shift(payload[2, 1], 0, 1)
-    other = [shift(payload[k, 1], k, 0) for k in (1, 3)]
+    far_sum = call(
+        far_sum_kernel, shape((PAY, 128), BF16), [payload[2, 0], across], flops=COST_FAR, moved=1 << 20
+    )
+    beside = [shift(payload[k], k, 0) for k in (1, 3)]
+    other_sum = call(
+        other_sum_kernel,
+        shape((PAY, 128), BF16),
+        [payload[0, 1]] + beside,
+        flops=COST_SUMS,
+        moved=1 << 20,
+    )
+    crossed = shift(other_sum, 0, 1)
+    mine = [shift(far_sum, 2, 0)] + beside
+
     pairs = [shape((8, 2, 48, FF), BF16)] * 2
     keep_out, send_out = call(
-        weights_out_kernel, pairs, [activ, mixed], flops=2 * PIX * CALL * FF, moved=8 << 20
+        weights_out_kernel, pairs, [activ, mixed], flops=COST_OUT, moved=8 << 20
     )
     got_out = lax.ppermute(send_out, "rows", core)
     keep_in, send_in = call(
-        weights_in_kernel, pairs, [normed, grad_hidden], flops=2 * PIX * CALL * FF, moved=8 << 20
+        weights_in_kernel, pairs, [normed, grad_hidden], after=[other_sum, far_sum], flops=COST_IN, moved=8 << 20
     )
     got_in = lax.ppermute(send_in, "rows", core)
-    other_sum, far_sum, own_one, own_three = call(
-        middle_sums_kernel,
-        [shape((PAY, 128), BF16)] * 4,
-        [payload[2, 0], across, payload[0, 1]] + other + [payload[1, 0], payload[3, 0]],
-        after=[send_out, send_in],
-        moved=1 << 20,
-    )
-    crossed = shift(other_sum, 0, 1)
-    mine = [shift(far_sum, 2, 0), shift(own_one, 1, 0), shift(own_three, 3, 0)]
-
     def move(block, f):
         return lax.ppermute(block, "rows", rows_perm(f))
 
@@ -708,21 +721,21 @@
     def to_lo(i):
         return i ^ 2
 
-    def exchange(joiner, keep, got, dims, f, moved, after):
-        keep, send = call(joiner, [blocks(*dims)] * 2, [keep, got], after=[after], moved=moved)
+    def exchange(joiner, keep, got, dims, f, moved, after=()):
+        keep, send = call(joiner, [blocks(*dims)] * 2, [keep, got], after=after, moved=moved)
         return keep, move(send, f)
 
     def first(z):
         return z ^ 1
 
-    keep_out, got_out = exchange(join_out_kernel, keep_out, got_out, (8,), to_lo, 4 << 20, other_sum)
-    keep_in, got_in = exchange(join_half_kernel, keep_in, got_in, (4, 2), to_z(first), 4 << 20, far_sum)
+    keep_out, got_out = exchange(join_out_kernel, keep_out, got_out, (8,), to_lo, 4 << 20, [other_sum])
+    keep_in, got_in = exchange(join_half_kernel, keep_in, got_in, (4, 2), to_z(first), 4 << 20, [other_sum])
     grad_conv, sent, terms = call(
         norm_back_kernel,
         [shape((PACK, 128), BF16), shape((PACK + TERMS, 128), BF16), shape((TERMS, 128), F32)],
         [payload[0, 0]] + mine + [crossed, conv, stats, gain_own, above, packed, below],
         pads(),
-        flops=WEIGHTY,
+        flops=COST_BACK,
         moved=2 << 20,
     )
 
@@ -733,22 +746,23 @@
     grad_core = lax.ppermute(sent, "rows", core)
     terms = call(open_kernel, shape((TERMS, 128), F32), [sent, grad_core])
     terms = terms + partner_terms(terms, to_lo)
-    keep_out, got_out = exchange(join_half_kernel, keep_out, got_out, (4,), to_z(first), 2 << 20, terms)
-    keep_in, got_in = exchange(join_lo_kernel, keep_in, got_in, (4,), to_lo, 2 << 20, terms)
+    keep_out, got_out = exchange(
+        join_half_kernel, keep_out, got_out, (4,), to_z(first), 2 << 20, [terms]
+    )
+    keep_in, got_in = exchange(
+        join_pair_kernel, keep_in, got_in, (2, 2), to_z(second_partner), 2 << 20, [terms]
+    )
     terms, grad_side = call(
         pass_kernel,
         [shape((TERMS, 128), F32), shape((PACK, 128), BF16)],
         [terms, partner_terms(terms, to_z(first)), grad_side],
+        flops=COST_PASS,
         moved=1 << 20,
     )
-    keep, send = call(
-        join_pair_kernel,
-        [shape((192, FF), BF16), shape((192, FF), BF16)],
-        [keep_in, got_in, keep_out, got_out],
-        after=[terms],
-        moved=2 << 20,
-    )
-    got = move(send, to_z(second_partner))
+    keep_out, got_out = exchange(
+        join_pair_kernel, keep_out, got_out, (2,), to_z(second_partner), 1 << 20, [terms]
+    )
+    keep_in, got_in = exchange(join_lo_kernel, keep_in, got_in, (2,), to_lo, 1 << 20, [terms])
 
     grad_feature = call(
         back_kernel,
@@ -761,7 +775,7 @@
     keep, sent = call(
         join_one_kernel,
         [shape((96, FF), BF16), shape((112, FF), BF16)],
-        [keep, got, terms, partner_terms(terms, to_z(second_partner))],
+        [keep_in, got_in, keep_out, got_out, terms, partner_terms(terms, to_z(second_partner))],
         moved=1 << 20,
     )
     got = move(sent, to_z(third_partner))

time: 111 us -> 106 us (0.955)
  waiting for transfers between devices: 40.4 us -> 33.6 us
  starting transfers between devices: 47.3 us -> 49.5 us
    ppermute x3, starting transfers between devices: 3.05 us -> 7.14 us  [partner_terms(): return lax.ppermute(terms, 'rows', rows_perm(f))]
    ppermute x3, waiting for transfers between devices: 17.9 us -> 15.1 us  [partner_terms(): return lax.ppermute(terms, 'rows', rows_perm(f))]
    ppermute x14 -> x12, waiting for transfers between devices: 14.8 us -> 12.5 us  [shift(): return lax.ppermute(block, 'chan', chan_shift(k, x))]
    ppermute x6 -> x7, waiting for transfers between devices: 6.23 us -> 4.54 us  [move(): return lax.ppermute(block, 'rows', rows_perm(f))]
    ppermute x14 -> x12, starting transfers between devices: 21.1 us -> 20.4 us  [shift(): return lax.ppermute(block, 'chan', chan_shift(k, x))]
    ppermute x6 -> x7, starting transfers between devices: 18.2 us -> 17.5 us  [move(): return lax.ppermute(block, 'rows', rows_perm(f))]
    pallas_call x18 -> x20, Pallas kernels: 21 us -> 21 us  [call(): pl.pallas_call(body, out_shape=shapes, in_specs=[hbm if n in far else nea...]
  transfers between devices with their start and end apart: 29 -> 28, of which waited for: 13 -> 11; matrix products, arithmetic and copies ran while one was open for 0% -> 0% of each run, Pallas kernels for 10% -> 12%
where the time goes in v4:
time: 106 us; the launch traced here: 105 us
  starting transfers between devices  49.5 us (47%)
  waiting for transfers between devices  33.6 us (32%)
  Pallas kernels  21 us (20%)
    pallas_call x20, Pallas kernels, call(): pl.pallas_call(body, out_shape=shapes, in_specs=[hbm if n in far else nea...  21 us
    ppermute x12, starting transfers between devices, shift(): return lax.ppermute(block, 'chan', chan_shift(k, x))  20.4 us
    ppermute x7, starting transfers between devices, move(): return lax.ppermute(block, 'rows', rows_perm(f))  17.5 us
    ppermute x3, waiting for transfers between devices, partner_terms(): return lax.ppermute(terms, 'rows', rows_perm(f))  15.1 us
    ppermute x12, waiting for transfers between devices, shift(): return lax.ppermute(block, 'chan', chan_shift(k, x))  12.5 us
    ppermute x3, starting transfers between devices, partner_terms(): return lax.ppermute(terms, 'rows', rows_perm(f))  7.14 us
    ppermute x7, waiting for transfers between devices, move(): return lax.ppermute(block, 'rows', rows_perm(f))  4.54 us
    ppermute x1, starting transfers between devices, shards(): above, below = (lax.ppermute(packed, 'rows', core), other_side(packed))  2.93 us
  transfers between devices with their start and end apart: 28, of which 11 were waited for; matrix products, arithmetic and copies ran while one was open for 0% of the time, Pallas kernels for 12%

profile of v4, /device:TPU:8, one launch (start us, length us, event | category | flops | bytes accessed | tf_op | source)
XLA Modules:
  0.0 104.9 jit_solution(15240633933471328341)
XLA Ops:
  2.4 2.9 %collective-permute-start = (bf16[656,128]{1,0:T(8,128)(2,1)S(1)}, bf16[656,128]{1,0:T(8,128)(2,1)S(1)}, u32[]{:S(2)}, u32[]{:S(2)}) collective-permute-start(bf16[656,128]{1,0:T(8,128)(2,1)S(1)} %shard_map.102.refs_1_.refs_9_), channel_id=1, source_target_pairs={{0,8},{8,0},{16,24},{24,16},{32,40},{40,32},{48,56},{56,48},{64,72... | collective-permute-start | bytes 503816 | tf_op jit(solution)/shard_map/ppermute | solution.py:621
  5.3 3.5 %shard_map.103 = (bf16[432,1536]{1,0:T(8,128)(2,1)S(1)}, f32[432,768]{1,0:T(8,128)S(1)}, bf16[1536,768]{1,0:T(8,128)(2,1)S(1)}, f32[1,1536]{1,0:T(1,128)S(1)}, f...) custom-call(bf16[432,1536]{1,0:T(8,128)(2,1)} %bitcast.4, f32[12,128]{1,0:T(8,128)} %bitcast.5, ...), custom_call_target="tpu_custom_call" | custom-call | flops 1019215872 | bytes 8388608 | tf_op jit(solution)/shard_map/pallas_call | solution.py:577
  10.4 2.4 %collective-permute-start.5 = (bf16[656,128]{1,0:T(8,128)(2,1)S(1)}, bf16[656,128]{1,0:T(8,128)(2,1)S(1)}, u32[]{:S(2)}, u32[]{:S(2)}) collective-permute-start(bf16[656,128]{1,0:T(8,128)(2,1)S(1)} %shard_map.104.refs_0_.refs_5_), channel_id=1, source_target_pairs={{0,4},{1,5},{2,6},{3,7},{4,0},{5,1},{6,2},{7,3},{8,12},{9,13},{10,... | collective-permute-start | bytes 503816 | tf_op jit(solution)/shard_map/ppermute | solution.py:659
  12.8 2.7 %collective-permute-start.2 = (bf16[656,128]{1,0:T(8,128)(2,1)S(1)}, bf16[656,128]{1,0:T(8,128)(2,1)S(1)}, u32[]{:S(2)}, u32[]{:S(2)}) collective-permute-start(bf16[656,128]{1,0:T(8,128)(2,1)S(1)} %shard_map.104.refs_0_.refs_5_), channel_id=1, source_target_pairs={{0,1},{1,0},{2,3},{3,2},{4,5},{5,4},{6,7},{7,6},{8,9},{9,8},{10,11... | collective-permute-start | bytes 503816 | tf_op jit(solution)/shard_map/ppermute | solution.py:659
  15.5 2.0 %collective-permute-start.3 = (bf16[656,128]{1,0:T(8,128)(2,1)S(1)}, bf16[656,128]{1,0:T(8,128)(2,1)S(1)}, u32[]{:S(2)}, u32[]{:S(2)}) collective-permute-start(bf16[656,128]{1,0:T(8,128)(2,1)S(1)} %shard_map.104.refs_0_.refs_5_), channel_id=1, source_target_pairs={{0,6},{1,7},{2,0},{3,1},{4,2},{5,3},{6,4},{7,5},{8,14},{9,15},{10,... | collective-permute-start | bytes 503816 | tf_op jit(solution)/shard_map/ppermute | solution.py:659
  18.7 3.2 %collective-permute-start.6 = (bf16[656,128]{1,0:T(8,128)(2,1)S(1)}, bf16[656,128]{1,0:T(8,128)(2,1)S(1)}, u32[]{:S(2)}, u32[]{:S(2)}) collective-permute-start(bf16[656,128]{1,0:T(8,128)(2,1)S(1)} %collective-permute-done.5.refs_4_), channel_id=1, source_target_pairs={{0,1},{1,0},{2,3},{3,2},{4,5},{5,4},{6,7},{7,6},{8,9},{9,8},{10,11... | collective-permute-start | bytes 503816 | tf_op jit(solution)/shard_map/ppermute | solution.py:659
  23.9 2.1 %collective-permute-done.6.refs_5_ = bf16[656,128]{1,0:T(8,128)(2,1)S(1)} collective-permute-done((bf16[656,128]{1,0:T(8,128)(2,1)S(1)}, bf16[656,128]{1,0:T(8,128)(2,1)S(1)}, u32[]{:S(2)}, u32[]{:S(2)}) %collective-permute-start.6) | collective-permute-done | bytes 167968 | tf_op jit(solution)/shard_map/ppermute | solution.py:659
  28.8 5.1 %shard_map.105 = (bf16[432,1536]{1,0:T(8,128)(2,1)S(1)}, bf16[432,768]{1,0:T(8,128)(2,1)S(1)}, bf16[432,768]{1,0:T(8,128)(2,1)S(1)}, f32[432,128]{1,0:T(8,128)S(...) custom-call(bf16[656,128]{1,0:T(8,128)(2,1)S(1)} %shard_map.104.refs, ...), custom_call_target="tpu_custom_call" | custom-call | flops 2038431744 | bytes 8388608 | tf_op jit(solution)/shard_map/pallas_call | solution.py:577
  38.3 4.7 %collective-permute-done.9.refs_1_ = bf16[704,128]{1,0:T(8,128)(2,1)S(1)} collective-permute-done((bf16[704,128]{1,0:T(8,128)(2,1)S(1)}, bf16[704,128]{1,0:T(8,128)(2,1)S(1)}, u32[]{:S(2)}, u32[]{:S(2)}) %collective-permute-start.9) | collective-permute-done | bytes 180256 | tf_op jit(solution)/shard_map/ppermute | solution.py:659
  45.1 2.4 %collective-permute-start.10 = (bf16[704,128]{1,0:T(8,128)(2,1)S(1)}, bf16[704,128]{1,0:T(8,128)(2,1)S(1)}, u32[]{:S(2)}, u32[]{:S(2)}) collective-permute-start(bf16[704,128]{1,0:T(8,128)(2,1)S(1)} %shard_map.106.refs_3_), channel_id=1, source_target_pairs={{0,4},{1,5},{2,6},{3,7},{4,0},{5,1},{6,2},{7,3},{8,12},{9,13},{10,... | collective-permute-start | bytes 540680 | tf_op jit(solution)/shard_map/ppermute | solution.py:659
  47.5 2.8 %collective-permute-start.13 = (bf16[704,128]{1,0:T(8,128)(2,1)S(1)}, bf16[704,128]{1,0:T(8,128)(2,1)S(1)}, u32[]{:S(2)}, u32[]{:S(2)}) collective-permute-start(bf16[704,128]{1,0:T(8,128)(2,1)S(1)} %shard_map.107.refs_2_), channel_id=1, source_target_pairs={{0,1},{1,0},{2,3},{3,2},{4,5},{5,4},{6,7},{7,6},{8,9},{9,8},{10,11... | collective-permute-start | bytes 540680 | tf_op jit(solution)/shard_map/ppermute | solution.py:659
  51.8 2.8 %collective-permute-start.19 = (bf16[4,2,48,768]{3,2,1,0:T(8,128)(2,1)S(1)}, bf16[4,2,48,768]{3,2,1,0:T(8,128)(2,1)S(1)}, u32[]{:S(2)}, u32[]{:S(2)}) collective-permute-start(bf16[4,2,48,768]{3,2,1,0:T(8,128)(2,1)S(1)} %get-tuple-element.67), channel_id=1, source_target_pairs={{0,32},{8,40},{16,48},{24,56},{32,0},{40,8},{48,16},{56,24},{64,96... | collective-permute-start | bytes 1769480 | tf_op jit(solution)/shard_map/ppermute | solution.py:713
  56.4 2.4 %shard_map.108 = (bf16[656,128]{1,0:T(8,128)(2,1)S(1)}, bf16[752,128]{1,0:T(8,128)(2,1)S(1)}, f32[96,128]{1,0:T(8,128)}) custom-call(bf16[704,128]{1,0:T(8,128)(2,1)S(1)} %get-tuple-element.50.refs_0_, bf16[704,128]{1,0:T(8,128)(2,1)S(1)} %collective-permute-done.10.refs_1_, bf16[2,704,128]{2,1,0:T(8,128)(2,1)S(1)} %collective-permute-done.11.refs_1_.refs_2_, ...), custom_call_target="tpu_custom_call" | custom-call | flops 34359738368 | bytes 2097152 | tf_op jit(solution)/shard_map/pallas_call | solution.py:577
  61.9 7.3 %collective-permute-done.15 = f32[96,128]{1,0:T(8,128)S(1)} collective-permute-done((f32[96,128]{1,0:T(8,128)S(1)}, f32[96,128]{1,0:T(8,128)S(1)}, u32[]{:S(2)}, u32[]{:S(2)}) %collective-permute-start.15) | collective-permute-done | bytes 49184 | tf_op jit(solution)/shard_map/ppermute | solution.py:743
  69.4 2.3 %collective-permute-start.24 = (bf16[4,48,768]{2,1,0:T(8,128)(2,1)S(1)}, bf16[4,48,768]{2,1,0:T(8,128)(2,1)S(1)}, u32[]{:S(2)}, u32[]{:S(2)}) collective-permute-start(bf16[4,48,768]{2,1,0:T(8,128)(2,1)S(1)} %get-tuple-element.80), channel_id=1, source_target_pairs={{0,32},{8,40},{16,48},{24,56},{32,0},{40,8},{48,16},{56,24},{64,96... | collective-permute-start | bytes 884744 | tf_op jit(solution)/shard_map/ppermute | solution.py:713
  71.9 5.0 %collective-permute-start.20 = (bf16[2,2,48,768]{3,2,1,0:T(8,128)(2,1)S(1)}, bf16[2,2,48,768]{3,2,1,0:T(8,128)(2,1)S(1)}, u32[]{:S(2)}, u32[]{:S(2)}) collective-permute-start(bf16[2,2,48,768]{3,2,1,0:T(8,128)(2,1)S(1)} %get-tuple-element.69), channel_id=1, source_target_pairs={{0,224},{8,232},{16,240},{24,248},{32,64},{40,72},{48,80},{56,88},... | collective-permute-start | bytes 884744 | tf_op jit(solution)/shard_map/ppermute | solution.py:713
  77.6 3.6 %collective-permute-start.16 = (f32[96,128]{1,0:T(8,128)S(1)}, f32[96,128]{1,0:T(8,128)S(1)}, u32[]{:S(2)}, u32[]{:S(2)}) collective-permute-start(f32[96,128]{1,0:T(8,128)S(1)} %add.3.refs_0_.refs_2_), channel_id=1, source_target_pairs={{0,32},{8,40},{16,48},{24,56},{32,0},{40,8},{48,16},{56,24},{64,96... | collective-permute-start | bytes 147464 | tf_op jit(solution)/shard_map/ppermute | solution.py:743
  81.2 4.3 %collective-permute-done.16.refs_1_ = f32[96,128]{1,0:T(8,128)S(1)} collective-permute-done((f32[96,128]{1,0:T(8,128)S(1)}, f32[96,128]{1,0:T(8,128)S(1)}, u32[]{:S(2)}, u32[]{:S(2)}) %collective-permute-start.16) | collective-permute-done | bytes 49184 | tf_op jit(solution)/shard_map/ppermute | solution.py:743
  85.6 2.3 %collective-permute-start.25 = (bf16[2,48,768]{2,1,0:T(8,128)(2,1)S(1)}, bf16[2,48,768]{2,1,0:T(8,128)(2,1)S(1)}, u32[]{:S(2)}, u32[]{:S(2)}) collective-permute-start(bf16[2,48,768]{2,1,0:T(8,128)(2,1)S(1)} %get-tuple-element.82), channel_id=1, source_target_pairs={{0,224},{8,232},{16,240},{24,248},{32,64},{40,72},{48,80},{56,88},... | collective-permute-start | bytes 442376 | tf_op jit(solution)/shard_map/ppermute | solution.py:713
  89.5 1.8 %collective-permute-start.26 = (f32[96,128]{1,0:T(8,128)S(1)}, f32[96,128]{1,0:T(8,128)S(1)}, u32[]{:S(2)}, u32[]{:S(2)}) collective-permute-start(f32[96,128]{1,0:T(8,128)S(1)} %get-tuple-element.70.refs_2_.refs_4_), channel_id=1, source_target_pairs={{0,224},{8,232},{16,240},{24,248},{32,64},{40,72},{48,80},{56,88},... | collective-permute-start | bytes 147464 | tf_op jit(solution)/shard_map/ppermute | solution.py:743
  91.3 3.5 %collective-permute-done.26.refs_5_ = f32[96,128]{1,0:T(8,128)S(1)} collective-permute-done((f32[96,128]{1,0:T(8,128)S(1)}, f32[96,128]{1,0:T(8,128)S(1)}, u32[]{:S(2)}, u32[]{:S(2)}) %collective-permute-start.26) | collective-permute-done | bytes 49184 | tf_op jit(solution)/shard_map/ppermute | solution.py:743
  94.9 2.5 %collective-permute-start.27 = (bf16[112,768]{1,0:T(8,128)(2,1)S(1)}, bf16[112,768]{1,0:T(8,128)(2,1)S(1)}, u32[]{:S(2)}, u32[]{:S(2)}) collective-permute-start(bf16[112,768]{1,0:T(8,128)(2,1)S(1)} %get-tuple-element.84.refs_1_), channel_id=1, source_target_pairs={{0,96},{8,104},{16,112},{24,120},{32,192},{40,200},{48,208},{56,21... | collective-permute-start | bytes 516104 | tf_op jit(solution)/shard_map/ppermute | solution.py:713
  97.5 2.1 %shard_map.111 = bf16[3,144,192]{2,1,0:T(8,128)(2,1)} custom-call(bf16[752,128]{1,0:T(8,128)(2,1)S(1)} %collective-permute-done.14.refs_1_.refs_0_, bf16[656,128]{1,0:T(8,128)(2,1)S(1)} %get-tuple-element.59.refs_1_, bf16[656,128]{1,0:T(8,128)(2,1)S(1)} %get-tuple-element.60.refs_2_, f32[49,256]{1,0:T(8,128)S(1)} %get-tuple-element.46.refs_3_, ...), custom_call_target="tpu_custom_call" | custom-call | flops 8388608 | bytes 1048576 | tf_op jit(solution)/shard_map/pallas_call | solution.py:577
  99.6 4.5 %collective-permute-done.27.refs_2_ = bf16[112,768]{1,0:T(8,128)(2,1)S(1)} collective-permute-done((bf16[112,768]{1,0:T(8,128)(2,1)S(1)}, bf16[112,768]{1,0:T(8,128)(2,1)S(1)}, u32[]{:S(2)}, u32[]{:S(2)}) %collective-permute-start.27) | collective-permute-done | bytes 172064 | tf_op jit(solution)/shard_map/ppermute | solution.py:713
  (53 shorter events, 25.6 us)
Async XLA Ops:
  1.7 7.2 %collective-permute-start.1 = (bf16[656,128]{1,0:T(8,128)(2,1)S(1)}, bf16[656,128]{1,0:T(8,128)(2,1)S(1)}, u32[]{:S(2)}, u32[]{:S(2)}) collective-permute-start(bf16[656,128]{1,0:T(8,128)(2,1)S(1)} %shard_map.102.refs_1_.refs_9_), channel_id=1, source_target_pairs={{8,16},{24,32},{40,48},{56,64},{72,80},{88,96},{104,112},{120,128}... | collective-permute-start | bytes 503816 | tf_op jit(solution)/shard_map/ppermute | solution.py:606
  2.4 6.5 %collective-permute-start = (bf16[656,128]{1,0:T(8,128)(2,1)S(1)}, bf16[656,128]{1,0:T(8,128)(2,1)S(1)}, u32[]{:S(2)}, u32[]{:S(2)}) collective-permute-start(bf16[656,128]{1,0:T(8,128)(2,1)S(1)} %shard_map.102.refs_1_.refs_9_), channel_id=1, source_target_pairs={{0,8},{8,0},{16,24},{24,16},{32,40},{40,32},{48,56},{56,48},{64,72... | collective-permute-start | bytes 503816 | tf_op jit(solution)/shard_map/ppermute | solution.py:621
  10.4 8.3 %collective-permute-start.5 = (bf16[656,128]{1,0:T(8,128)(2,1)S(1)}, bf16[656,128]{1,0:T(8,128)(2,1)S(1)}, u32[]{:S(2)}, u32[]{:S(2)}) collective-permute-start(bf16[656,128]{1,0:T(8,128)(2,1)S(1)} %shard_map.104.refs_0_.refs_5_), channel_id=1, source_target_pairs={{0,4},{1,5},{2,6},{3,7},{4,0},{5,1},{6,2},{7,3},{8,12},{9,13},{10,... | collective-permute-start | bytes 503816 | tf_op jit(solution)/shard_map/ppermute | solution.py:659
  12.8 9.1 %collective-permute-start.2 = (bf16[656,128]{1,0:T(8,128)(2,1)S(1)}, bf16[656,128]{1,0:T(8,128)(2,1)S(1)}, u32[]{:S(2)}, u32[]{:S(2)}) collective-permute-start(bf16[656,128]{1,0:T(8,128)(2,1)S(1)} %shard_map.104.refs_0_.refs_5_), channel_id=1, source_target_pairs={{0,1},{1,0},{2,3},{3,2},{4,5},{5,4},{6,7},{7,6},{8,9},{9,8},{10,11... | collective-permute-start | bytes 503816 | tf_op jit(solution)/shard_map/ppermute | solution.py:659
  15.5 8.4 %collective-permute-start.7 = (bf16[656,128]{1,0:T(8,128)(2,1)S(1)}, bf16[656,128]{1,0:T(8,128)(2,1)S(1)}, u32[]{:S(2)}, u32[]{:S(2)}) collective-permute-start(bf16[656,128]{1,0:T(8,128)(2,1)S(1)} %shard_map.104.refs_0_.refs_5_), channel_id=1, source_target_pairs={{0,2},{1,3},{2,4},{3,5},{4,6},{5,7},{6,0},{7,1},{8,10},{9,11},{10,... | collective-permute-start | bytes 503816 | tf_op jit(solution)/shard_map/ppermute | solution.py:659
  15.5 8.4 %collective-permute-start.3 = (bf16[656,128]{1,0:T(8,128)(2,1)S(1)}, bf16[656,128]{1,0:T(8,128)(2,1)S(1)}, u32[]{:S(2)}, u32[]{:S(2)}) collective-permute-start(bf16[656,128]{1,0:T(8,128)(2,1)S(1)} %shard_map.104.refs_0_.refs_5_), channel_id=1, source_target_pairs={{0,6},{1,7},{2,0},{3,1},{4,2},{5,3},{6,4},{7,5},{8,14},{9,15},{10,... | collective-permute-start | bytes 503816 | tf_op jit(solution)/shard_map/ppermute | solution.py:659
  18.7 7.3 %collective-permute-start.6 = (bf16[656,128]{1,0:T(8,128)(2,1)S(1)}, bf16[656,128]{1,0:T(8,128)(2,1)S(1)}, u32[]{:S(2)}, u32[]{:S(2)}) collective-permute-start(bf16[656,128]{1,0:T(8,128)(2,1)S(1)} %collective-permute-done.5.refs_4_), channel_id=1, source_target_pairs={{0,1},{1,0},{2,3},{3,2},{4,5},{5,4},{6,7},{7,6},{8,9},{9,8},{10,11... | collective-permute-start | bytes 503816 | tf_op jit(solution)/shard_map/ppermute | solution.py:659
  21.9 5.4 %collective-permute-start.8 = (bf16[656,128]{1,0:T(8,128)(2,1)S(1)}, bf16[656,128]{1,0:T(8,128)(2,1)S(1)}, u32[]{:S(2)}, u32[]{:S(2)}) collective-permute-start(bf16[656,128]{1,0:T(8,128)(2,1)S(1)} %collective-permute-done.2.refs_1_), channel_id=1, source_target_pairs={{0,2},{1,3},{2,4},{3,5},{4,6},{5,7},{6,0},{7,1},{8,10},{9,11},{10,... | collective-permute-start | bytes 503816 | tf_op jit(solution)/shard_map/ppermute | solution.py:659
  34.0 9.3 %collective-permute-start.11 = (bf16[2,704,128]{2,1,0:T(8,128)(2,1)S(1)}, bf16[2,704,128]{2,1,0:T(8,128)(2,1)S(1)}, u32[]{:S(2)}, u32[]{:S(2)}) collective-permute-start(bf16[2,704,128]{2,1,0:T(8,128)(2,1)S(1)} %get-tuple-element.53), channel_id=1, source_target_pairs={{0,2},{1,3},{2,4},{3,5},{4,6},{5,7},{6,0},{7,1},{8,10},{9,11},{10,... | collective-permute-start | bytes 1081352 | tf_op jit(solution)/shard_map/ppermute | solution.py:659
  35.3 8.0 %collective-permute-start.12 = (bf16[2,704,128]{2,1,0:T(8,128)(2,1)S(1)}, bf16[2,704,128]{2,1,0:T(8,128)(2,1)S(1)}, u32[]{:S(2)}, u32[]{:S(2)}) collective-permute-start(bf16[2,704,128]{2,1,0:T(8,128)(2,1)S(1)} %get-tuple-element.54), channel_id=1, source_target_pairs={{0,6},{1,7},{2,0},{3,1},{4,2},{5,3},{6,4},{7,5},{8,14},{9,15},{10,... | collective-permute-start | bytes 1081352 | tf_op jit(solution)/shard_map/ppermute | solution.py:659
  36.1 7.0 %collective-permute-start.9 = (bf16[704,128]{1,0:T(8,128)(2,1)S(1)}, bf16[704,128]{1,0:T(8,128)(2,1)S(1)}, u32[]{:S(2)}, u32[]{:S(2)}) collective-permute-start(bf16[704,128]{1,0:T(8,128)(2,1)S(1)} %get-tuple-element.52), channel_id=1, source_target_pairs={{0,1},{1,0},{2,3},{3,2},{4,5},{5,4},{6,7},{7,6},{8,9},{9,8},{10,11... | collective-permute-start | bytes 540680 | tf_op jit(solution)/shard_map/ppermute | solution.py:659
  38.2 12.0 %collective-permute-start.22 = (bf16[8,2,48,768]{3,2,1,0:T(8,128)(2,1)S(1)}, bf16[8,2,48,768]{3,2,1,0:T(8,128)(2,1)S(1)}, u32[]{:S(2)}, u32[]{:S(2)}) collective-permute-start(bf16[8,2,48,768]{3,2,1,0:T(8,128)(2,1)S(1)} %get-tuple-element.76), channel_id=1, source_target_pairs={{0,8},{8,0},{16,24},{24,16},{32,40},{40,32},{48,56},{56,48},{64,72... | collective-permute-start | bytes 3538952 | tf_op jit(solution)/shard_map/ppermute | solution.py:707
  45.0 6.6 %collective-permute-start.18 = (bf16[8,2,48,768]{3,2,1,0:T(8,128)(2,1)S(1)}, bf16[8,2,48,768]{3,2,1,0:T(8,128)(2,1)S(1)}, u32[]{:S(2)}, u32[]{:S(2)}) collective-permute-start(bf16[8,2,48,768]{3,2,1,0:T(8,128)(2,1)S(1)} %get-tuple-element.65), channel_id=1, source_target_pairs={{0,8},{8,0},{16,24},{24,16},{32,40},{40,32},{48,56},{56,48},{64,72... | collective-permute-start | bytes 3538952 | tf_op jit(solution)/shard_map/ppermute | solution.py:711
  45.1 9.5 %collective-permute-start.10 = (bf16[704,128]{1,0:T(8,128)(2,1)S(1)}, bf16[704,128]{1,0:T(8,128)(2,1)S(1)}, u32[]{:S(2)}, u32[]{:S(2)}) collective-permute-start(bf16[704,128]{1,0:T(8,128)(2,1)S(1)} %shard_map.106.refs_3_), channel_id=1, source_target_pairs={{0,4},{1,5},{2,6},{3,7},{4,0},{5,1},{6,2},{7,3},{8,12},{9,13},{10,... | collective-permute-start | bytes 540680 | tf_op jit(solution)/shard_map/ppermute | solution.py:659
  47.5 8.9 %collective-permute-start.13 = (bf16[704,128]{1,0:T(8,128)(2,1)S(1)}, bf16[704,128]{1,0:T(8,128)(2,1)S(1)}, u32[]{:S(2)}, u32[]{:S(2)}) collective-permute-start(bf16[704,128]{1,0:T(8,128)(2,1)S(1)} %shard_map.107.refs_2_), channel_id=1, source_target_pairs={{0,1},{1,0},{2,3},{3,2},{4,5},{5,4},{6,7},{7,6},{8,9},{9,8},{10,11... | collective-permute-start | bytes 540680 | tf_op jit(solution)/shard_map/ppermute | solution.py:659
  50.6 18.7 %collective-permute-start.23 = (bf16[8,48,768]{2,1,0:T(8,128)(2,1)S(1)}, bf16[8,48,768]{2,1,0:T(8,128)(2,1)S(1)}, u32[]{:S(2)}, u32[]{:S(2)}) collective-permute-start(bf16[8,48,768]{2,1,0:T(8,128)(2,1)S(1)} %get-tuple-element.78), channel_id=1, source_target_pairs={{0,16},{8,24},{16,0},{24,8},{32,48},{40,56},{48,32},{56,40},{64,80... | collective-permute-start | bytes 1769480 | tf_op jit(solution)/shard_map/ppermute | solution.py:713
  51.8 19.9 %collective-permute-start.19 = (bf16[4,2,48,768]{3,2,1,0:T(8,128)(2,1)S(1)}, bf16[4,2,48,768]{3,2,1,0:T(8,128)(2,1)S(1)}, u32[]{:S(2)}, u32[]{:S(2)}) collective-permute-start(bf16[4,2,48,768]{3,2,1,0:T(8,128)(2,1)S(1)} %get-tuple-element.67), channel_id=1, source_target_pairs={{0,32},{8,40},{16,48},{24,56},{32,0},{40,8},{48,16},{56,24},{64,96... | collective-permute-start | bytes 1769480 | tf_op jit(solution)/shard_map/ppermute | solution.py:713
  60.2 9.0 %collective-permute-start.15 = (f32[96,128]{1,0:T(8,128)S(1)}, f32[96,128]{1,0:T(8,128)S(1)}, u32[]{:S(2)}, u32[]{:S(2)}) collective-permute-start(f32[96,128]{1,0:T(8,128)S(1)} %shard_map.109), channel_id=1, source_target_pairs={{0,16},{8,24},{16,0},{24,8},{32,48},{40,56},{48,32},{56,40},{64,80... | collective-permute-start | bytes 147464 | tf_op jit(solution)/shard_map/ppermute | solution.py:743
  69.4 16.1 %collective-permute-start.24 = (bf16[4,48,768]{2,1,0:T(8,128)(2,1)S(1)}, bf16[4,48,768]{2,1,0:T(8,128)(2,1)S(1)}, u32[]{:S(2)}, u32[]{:S(2)}) collective-permute-start(bf16[4,48,768]{2,1,0:T(8,128)(2,1)S(1)} %get-tuple-element.80), channel_id=1, source_target_pairs={{0,32},{8,40},{16,48},{24,56},{32,0},{40,8},{48,16},{56,24},{64,96... | collective-permute-start | bytes 884744 | tf_op jit(solution)/shard_map/ppermute | solution.py:713
  71.9 16.1 %collective-permute-start.20 = (bf16[2,2,48,768]{3,2,1,0:T(8,128)(2,1)S(1)}, bf16[2,2,48,768]{3,2,1,0:T(8,128)(2,1)S(1)}, u32[]{:S(2)}, u32[]{:S(2)}) collective-permute-start(bf16[2,2,48,768]{3,2,1,0:T(8,128)(2,1)S(1)} %get-tuple-element.69), channel_id=1, source_target_pairs={{0,224},{8,232},{16,240},{24,248},{32,64},{40,72},{48,80},{56,88},... | collective-permute-start | bytes 884744 | tf_op jit(solution)/shard_map/ppermute | solution.py:713
  77.6 7.9 %collective-permute-start.16 = (f32[96,128]{1,0:T(8,128)S(1)}, f32[96,128]{1,0:T(8,128)S(1)}, u32[]{:S(2)}, u32[]{:S(2)}) collective-permute-start(f32[96,128]{1,0:T(8,128)S(1)} %add.3.refs_0_.refs_2_), channel_id=1, source_target_pairs={{0,32},{8,40},{16,48},{24,56},{32,0},{40,8},{48,16},{56,24},{64,96... | collective-permute-start | bytes 147464 | tf_op jit(solution)/shard_map/ppermute | solution.py:743
  85.6 9.2 %collective-permute-start.25 = (bf16[2,48,768]{2,1,0:T(8,128)(2,1)S(1)}, bf16[2,48,768]{2,1,0:T(8,128)(2,1)S(1)}, u32[]{:S(2)}, u32[]{:S(2)}) collective-permute-start(bf16[2,48,768]{2,1,0:T(8,128)(2,1)S(1)} %get-tuple-element.82), channel_id=1, source_target_pairs={{0,224},{8,232},{16,240},{24,248},{32,64},{40,72},{48,80},{56,88},... | collective-permute-start | bytes 442376 | tf_op jit(solution)/shard_map/ppermute | solution.py:713
  88.0 6.8 %collective-permute-start.21 = (bf16[2,48,768]{2,1,0:T(8,128)(2,1)S(1)}, bf16[2,48,768]{2,1,0:T(8,128)(2,1)S(1)}, u32[]{:S(2)}, u32[]{:S(2)}) collective-permute-start(bf16[2,48,768]{2,1,0:T(8,128)(2,1)S(1)} %get-tuple-element.72), channel_id=1, source_target_pairs={{0,16},{8,24},{16,0},{24,8},{32,48},{40,56},{48,32},{56,40},{64,80... | collective-permute-start | bytes 442376 | tf_op jit(solution)/shard_map/ppermute | solution.py:713
  94.9 9.2 %collective-permute-start.27 = (bf16[112,768]{1,0:T(8,128)(2,1)S(1)}, bf16[112,768]{1,0:T(8,128)(2,1)S(1)}, u32[]{:S(2)}, u32[]{:S(2)}) collective-permute-start(bf16[112,768]{1,0:T(8,128)(2,1)S(1)} %get-tuple-element.84.refs_1_), channel_id=1, source_target_pairs={{0,96},{8,104},{16,112},{24,120},{32,192},{40,200},{48,208},{56,21... | collective-permute-start | bytes 516104 | tf_op jit(solution)/shard_map/ppermute | solution.py:713
  (4 other events, 16.4 us)

commit v5 on v4

--- a/solution.py
+++ b/solution.py
@@ -495,29 +495,31 @@
         send_next[n] = added(keep[theirs], got[theirs])
 
 
-def join_out_kernel(keep, got, keep_next, send_next):
-    lo = my_lo()
-    for z in range(8):
-        keep_next[z] = added(keep[z, lo], got[z, lo])
-        send_next[z] = added(keep[z, 1 - lo], got[z, 1 - lo])
-
-
-def pair_blocks(n):
-    mine = by_z([PAIRS[kind_of(z)][pair_of(z)][n] for z in range(8)])
-    theirs = by_z([PAIRS[kind_of(z)][1 - pair_of(z)][n] for z in range(8)])
-    return mine, theirs
-
-
-def join_pair_kernel(keep, got, keep_next, send_next):
-    for n in range(2):
-        mine, theirs = pair_blocks(n)
+def turned(z, turn):
+    return (z - turn) % 8
+
+
+def join_half_kernel(turn, keep, got, keep_next, send_next):
+    for n in range(4):
+        kinds = [kind_of(turned(z, turn)) for z in range(8)]
+        mine = by_z([(HALVES[kind][n] + turn) % 8 for kind in kinds])
+        theirs = by_z([(HALVES[1 - kind][n] + turn) % 8 for kind in kinds])
         keep_next[n] = added(keep[mine], got[mine])
         send_next[n] = added(keep[theirs], got[theirs])
 
 
+def join_pair_kernel(turn, keep, got, keep_next, send_next):
+    for n in range(2):
+        places = [turned(z, turn) for z in range(8)]
+        mine = by_z([PAIRS[kind_of(z)][pair_of(z)][n] for z in places])
+        theirs = by_z([PAIRS[kind_of(z)][1 - pair_of(z)][n] for z in places])
+        keep_next[n] = added(keep[mine], got[mine])
+        send_next[n] = added(keep[theirs], got[theirs])
+
+
 def join_lo_kernel(keep, got, keep_next, send_next):
     lo = my_lo()
-    for n in range(2):
+    for n in range(keep.shape[0]):
         keep_next[n] = added(keep[n, lo], got[n, lo])
         send_next[n] = added(keep[n, 1 - lo], got[n, 1 - lo])
 
@@ -533,13 +535,22 @@
     )
 
 
-def join_one_kernel(keep_in, got_in, keep_out, got_out, terms, got, keep_next, send_next):
-    second = by_z([PAIRS[kind_of(z)][pair_of(z)].index(HALVES[kind_of(z)].index(z)) for z in range(8)])
-    for w, (keep, other) in enumerate(((keep_in, got_in), (keep_out, got_out))):
-        rows = slice(48 * w, 48 * w + 48)
-        keep_next[rows, :] = added(keep[second], other[second])
-        send_next[rows, :] = added(keep[1 - second], other[1 - second])
-    put_terms(send_next, 96, (terms[...] + got[...]).astype(BF16))
+def own_place(turn):
+    places = [turned(z, turn) for z in range(8)]
+    return by_z([PAIRS[kind_of(z)][pair_of(z)].index(HALVES[kind_of(z)].index(z)) for z in places])
+
+
+def join_one_in_kernel(keep, got, keep_next, send_next):
+    own = own_place(1)
+    keep_next[...] = added(keep[own], got[own])
+    send_next[...] = added(keep[1 - own], got[1 - own])
+
+
+def join_one_out_kernel(keep, got, terms, got_terms, keep_next, send_next):
+    own = own_place(0)
+    keep_next[...] = added(keep[own], got[own])
+    send_next[:48, :] = added(keep[1 - own], got[1 - own])
+    put_terms(send_next, 48, (terms[...] + got_terms[...]).astype(BF16))
 
 
 def pass_kernel(terms, got, block, o_ref, block_ref):
@@ -551,11 +562,10 @@
     o_ref[...] = sent[PACK:, :].astype(F32) + got[PACK:, :].astype(F32)
 
 
-def last_kernel(scale, keep, sent, got, grad_in, grad_out, grad_kernel):
-    for w, ref in enumerate((grad_in, grad_out)):
-        rows = slice(48 * w, 48 * w + 48)
-        ref[...] = (keep[rows, :].astype(F32) + got[rows, :].astype(F32)) * scale
-    lines = (take_terms(sent, 96) + take_terms(got, 96)) * scale
+def last_kernel(scale, keep_in, got_in, keep_out, sent, got, grad_in, grad_out, grad_kernel):
+    grad_in[...] = (keep_in[...].astype(F32) + got_in[...].astype(F32)) * scale
+    grad_out[...] = (keep_out[...].astype(F32) + got[:48, :].astype(F32)) * scale
+    lines = (take_terms(sent, 48) + take_terms(got, 48)) * scale
     rest = jnp.concatenate([lines[64:89], swap(lines[64:96])[:24]], axis=0)
     for a in range(7):
         grad_kernel[a, :, :128] = lines[7 * a : 7 * a + 7]
@@ -728,8 +738,16 @@
     def first(z):
         return z ^ 1
 
-    keep_out, got_out = exchange(join_out_kernel, keep_out, got_out, (8,), to_lo, 4 << 20, [other_sum])
-    keep_in, got_in = exchange(join_half_kernel, keep_in, got_in, (4, 2), to_z(first), 4 << 20, [other_sum])
+    def half(turn):
+        return lambda *refs: join_half_kernel(turn, *refs)
+
+    def pair(turn):
+        return lambda *refs: join_pair_kernel(turn, *refs)
+
+    keep_out, got_out = exchange(half(0), keep_out, got_out, (4, 2), to_z(first), 4 << 20, [other_sum])
+    keep_in, got_in = exchange(
+        half(1), keep_in, got_in, (4, 2), to_z(second_partner), 4 << 20, [other_sum]
+    )
     grad_conv, sent, terms = call(
         norm_back_kernel,
         [shape((PACK, 128), BF16), shape((PACK + TERMS, 128), BF16), shape((TERMS, 128), F32)],
@@ -747,22 +765,17 @@
     terms = call(open_kernel, shape((TERMS, 128), F32), [sent, grad_core])
     terms = terms + partner_terms(terms, to_lo)
     keep_out, got_out = exchange(
-        join_half_kernel, keep_out, got_out, (4,), to_z(first), 2 << 20, [terms]
-    )
-    keep_in, got_in = exchange(
-        join_pair_kernel, keep_in, got_in, (2, 2), to_z(second_partner), 2 << 20, [terms]
-    )
+        pair(0), keep_out, got_out, (2, 2), to_z(second_partner), 2 << 20, [terms]
+    )
+    keep_in, got_in = exchange(join_lo_kernel, keep_in, got_in, (4,), to_lo, 2 << 20, [grad_side])
     terms, grad_side = call(
         pass_kernel,
         [shape((TERMS, 128), F32), shape((PACK, 128), BF16)],
         [terms, partner_terms(terms, to_z(first)), grad_side],
-        flops=COST_PASS,
         moved=1 << 20,
     )
-    keep_out, got_out = exchange(
-        join_pair_kernel, keep_out, got_out, (2,), to_z(second_partner), 1 << 20, [terms]
-    )
-    keep_in, got_in = exchange(join_lo_kernel, keep_in, got_in, (2,), to_lo, 1 << 20, [terms])
+    keep_out, got_out = exchange(join_lo_kernel, keep_out, got_out, (2,), to_lo, 1 << 20, [terms])
+    keep_in, got_in = exchange(pair(1), keep_in, got_in, (2,), to_z(first), 1 << 20, [terms])
 
     grad_feature = call(
         back_kernel,
@@ -772,17 +785,21 @@
         flops=1 << 23,
         moved=1 << 20,
     )
-    keep, sent = call(
-        join_one_kernel,
-        [shape((96, FF), BF16), shape((112, FF), BF16)],
-        [keep_in, got_in, keep_out, got_out, terms, partner_terms(terms, to_z(second_partner))],
+    keep_out, sent = call(
+        join_one_out_kernel,
+        [shape((48, FF), BF16), shape((64, FF), BF16)],
+        [keep_out, got_out, terms, partner_terms(terms, to_z(second_partner))],
         moved=1 << 20,
     )
     got = move(sent, to_z(third_partner))
+    keep_in, sent_in = call(
+        join_one_in_kernel, [shape((48, FF), BF16)] * 2, [keep_in, got_in], moved=1 << 20
+    )
+    got_in = move(sent_in, to_z(lambda z: (third_partner((z - 1) % 8) + 1) % 8))
     grad_in, grad_out, grad_kernel = call(
         lambda *refs: last_kernel(scale, *refs),
         [shape((48, FF), F32), shape((48, FF), F32), shape((7, 7, CH), F32)],
-        [keep, sent, got],
+        [keep_in, got_in, keep_out, sent, got],
         moved=1 << 20,
     )
     return grad_feature, grad_in, grad_out.T, grad_kernel

time: 106 us -> 101 us (0.953); the launches traced: 105 us -> 101 us
  waiting for transfers between devices: 33.6 us -> 26.2 us
  starting transfers between devices: 49.5 us -> 53 us
    ppermute x3, waiting for transfers between devices: 15.1 us -> 9.97 us  [partner_terms(): return lax.ppermute(terms, 'rows', rows_perm(f))]
    ppermute x7 -> x8, starting transfers between devices: 17.5 us -> 21.6 us  [move(): return lax.ppermute(block, 'rows', rows_perm(f))]
    ppermute x12, waiting for transfers between devices: 12.5 us -> 10.8 us  [shift(): return lax.ppermute(block, 'chan', chan_shift(k, x))]
    ppermute x7 -> x8, waiting for transfers between devices: 4.54 us -> 4.65 us  [move(): return lax.ppermute(block, 'rows', rows_perm(f))]
    pallas_call x20 -> x21, Pallas kernels: 21 us -> 21 us  [call(): pl.pallas_call(body, out_shape=shapes, in_specs=[hbm if n in far else nea...]
  transfers between devices with their start and end apart: 28 -> 29, of which waited for: 11 -> 11; matrix products, arithmetic and copies ran while one was open for 0% -> 0% of each run, Pallas kernels for 12% -> 12%
where the time goes in v5:
time: 101 us
  starting transfers between devices  53 us (52%)
  waiting for transfers between devices  26.2 us (26%)
  Pallas kernels  21 us (21%)
    ppermute x8, starting transfers between devices, move(): return lax.ppermute(block, 'rows', rows_perm(f))  21.6 us
    pallas_call x21, Pallas kernels, call(): pl.pallas_call(body, out_shape=shapes, in_specs=[hbm if n in far else nea...  21 us
    ppermute x12, starting transfers between devices, shift(): return lax.ppermute(block, 'chan', chan_shift(k, x))  20.4 us
    ppermute x12, waiting for transfers between devices, shift(): return lax.ppermute(block, 'chan', chan_shift(k, x))  10.8 us
    ppermute x3, waiting for transfers between devices, partner_terms(): return lax.ppermute(terms, 'rows', rows_perm(f))  9.97 us
    ppermute x3, starting transfers between devices, partner_terms(): return lax.ppermute(terms, 'rows', rows_perm(f))  6.6 us
    ppermute x8, waiting for transfers between devices, move(): return lax.ppermute(block, 'rows', rows_perm(f))  4.65 us
    ppermute x1, starting transfers between devices, shards(): above, below = (lax.ppermute(packed, 'rows', core), other_side(packed))  2.93 us
  transfers between devices with their start and end apart: 29, of which 11 were waited for; matrix products, arithmetic and copies ran while one was open for 0% of the time, Pallas kernels for 12%

profile of v5, /device:TPU:8, one launch (start us, length us, event | category | flops | bytes accessed | tf_op | source)
XLA Modules:
  0.0 101.0 jit_solution(6636256627520729465)
XLA Ops:
  2.4 2.9 %collective-permute-start = (bf16[656,128]{1,0:T(8,128)(2,1)S(1)}, bf16[656,128]{1,0:T(8,128)(2,1)S(1)}, u32[]{:S(2)}, u32[]{:S(2)}) collective-permute-start(bf16[656,128]{1,0:T(8,128)(2,1)S(1)} %shard_map.102.refs_1_.refs_9_), channel_id=1, source_target_pairs={{0,8},{8,0},{16,24},{24,16},{32,40},{40,32},{48,56},{56,48},{64,72... | collective-permute-start | bytes 503816 | tf_op jit(solution)/shard_map/ppermute | solution.py:631
  5.3 3.5 %shard_map.103 = (bf16[432,1536]{1,0:T(8,128)(2,1)S(1)}, f32[432,768]{1,0:T(8,128)S(1)}, bf16[1536,768]{1,0:T(8,128)(2,1)S(1)}, f32[1,1536]{1,0:T(1,128)S(1)}, f...) custom-call(bf16[432,1536]{1,0:T(8,128)(2,1)} %bitcast.4, f32[12,128]{1,0:T(8,128)} %bitcast.5, ...), custom_call_target="tpu_custom_call" | custom-call | flops 1019215872 | bytes 8388608 | tf_op jit(solution)/shard_map/pallas_call | solution.py:587
  10.4 2.4 %collective-permute-start.5 = (bf16[656,128]{1,0:T(8,128)(2,1)S(1)}, bf16[656,128]{1,0:T(8,128)(2,1)S(1)}, u32[]{:S(2)}, u32[]{:S(2)}) collective-permute-start(bf16[656,128]{1,0:T(8,128)(2,1)S(1)} %shard_map.104.refs_0_.refs_5_), channel_id=1, source_target_pairs={{0,4},{1,5},{2,6},{3,7},{4,0},{5,1},{6,2},{7,3},{8,12},{9,13},{10,... | collective-permute-start | bytes 503816 | tf_op jit(solution)/shard_map/ppermute | solution.py:669
  12.8 2.7 %collective-permute-start.2 = (bf16[656,128]{1,0:T(8,128)(2,1)S(1)}, bf16[656,128]{1,0:T(8,128)(2,1)S(1)}, u32[]{:S(2)}, u32[]{:S(2)}) collective-permute-start(bf16[656,128]{1,0:T(8,128)(2,1)S(1)} %shard_map.104.refs_0_.refs_5_), channel_id=1, source_target_pairs={{0,1},{1,0},{2,3},{3,2},{4,5},{5,4},{6,7},{7,6},{8,9},{9,8},{10,11... | collective-permute-start | bytes 503816 | tf_op jit(solution)/shard_map/ppermute | solution.py:669
  15.5 2.0 %collective-permute-start.3 = (bf16[656,128]{1,0:T(8,128)(2,1)S(1)}, bf16[656,128]{1,0:T(8,128)(2,1)S(1)}, u32[]{:S(2)}, u32[]{:S(2)}) collective-permute-start(bf16[656,128]{1,0:T(8,128)(2,1)S(1)} %shard_map.104.refs_0_.refs_5_), channel_id=1, source_target_pairs={{0,6},{1,7},{2,0},{3,1},{4,2},{5,3},{6,4},{7,5},{8,14},{9,15},{10,... | collective-permute-start | bytes 503816 | tf_op jit(solution)/shard_map/ppermute | solution.py:669
  18.7 3.2 %collective-permute-start.6 = (bf16[656,128]{1,0:T(8,128)(2,1)S(1)}, bf16[656,128]{1,0:T(8,128)(2,1)S(1)}, u32[]{:S(2)}, u32[]{:S(2)}) collective-permute-start(bf16[656,128]{1,0:T(8,128)(2,1)S(1)} %collective-permute-done.5.refs_4_), channel_id=1, source_target_pairs={{0,1},{1,0},{2,3},{3,2},{4,5},{5,4},{6,7},{7,6},{8,9},{9,8},{10,11... | collective-permute-start | bytes 503816 | tf_op jit(solution)/shard_map/ppermute | solution.py:669
  23.9 2.1 %collective-permute-done.6.refs_5_ = bf16[656,128]{1,0:T(8,128)(2,1)S(1)} collective-permute-done((bf16[656,128]{1,0:T(8,128)(2,1)S(1)}, bf16[656,128]{1,0:T(8,128)(2,1)S(1)}, u32[]{:S(2)}, u32[]{:S(2)}) %collective-permute-start.6) | collective-permute-done | bytes 167968 | tf_op jit(solution)/shard_map/ppermute | solution.py:669
  28.8 5.1 %shard_map.105 = (bf16[432,1536]{1,0:T(8,128)(2,1)S(1)}, bf16[432,768]{1,0:T(8,128)(2,1)S(1)}, bf16[432,768]{1,0:T(8,128)(2,1)S(1)}, f32[432,128]{1,0:T(8,128)S(...) custom-call(bf16[656,128]{1,0:T(8,128)(2,1)S(1)} %shard_map.104.refs, ...), custom_call_target="tpu_custom_call" | custom-call | flops 2038431744 | bytes 8388608 | tf_op jit(solution)/shard_map/pallas_call | solution.py:587
  38.3 4.7 %collective-permute-done.9.refs_1_ = bf16[704,128]{1,0:T(8,128)(2,1)S(1)} collective-permute-done((bf16[704,128]{1,0:T(8,128)(2,1)S(1)}, bf16[704,128]{1,0:T(8,128)(2,1)S(1)}, u32[]{:S(2)}, u32[]{:S(2)}) %collective-permute-start.9) | collective-permute-done | bytes 180256 | tf_op jit(solution)/shard_map/ppermute | solution.py:669
  45.1 2.4 %collective-permute-start.10 = (bf16[704,128]{1,0:T(8,128)(2,1)S(1)}, bf16[704,128]{1,0:T(8,128)(2,1)S(1)}, u32[]{:S(2)}, u32[]{:S(2)}) collective-permute-start(bf16[704,128]{1,0:T(8,128)(2,1)S(1)} %shard_map.106.refs_3_), channel_id=1, source_target_pairs={{0,4},{1,5},{2,6},{3,7},{4,0},{5,1},{6,2},{7,3},{8,12},{9,13},{10,... | collective-permute-start | bytes 540680 | tf_op jit(solution)/shard_map/ppermute | solution.py:669
  47.5 2.8 %collective-permute-start.13 = (bf16[704,128]{1,0:T(8,128)(2,1)S(1)}, bf16[704,128]{1,0:T(8,128)(2,1)S(1)}, u32[]{:S(2)}, u32[]{:S(2)}) collective-permute-start(bf16[704,128]{1,0:T(8,128)(2,1)S(1)} %shard_map.107.refs_2_), channel_id=1, source_target_pairs={{0,1},{1,0},{2,3},{3,2},{4,5},{5,4},{6,7},{7,6},{8,9},{9,8},{10,11... | collective-permute-start | bytes 540680 | tf_op jit(solution)/shard_map/ppermute | solution.py:669
  50.6 3.7 %collective-permute-start.24 = (bf16[4,2,48,768]{3,2,1,0:T(8,128)(2,1)S(1)}, bf16[4,2,48,768]{3,2,1,0:T(8,128)(2,1)S(1)}, u32[]{:S(2)}, u32[]{:S(2)}) collective-permute-start(bf16[4,2,48,768]{3,2,1,0:T(8,128)(2,1)S(1)} %get-tuple-element.82), channel_id=1, source_target_pairs={{0,32},{8,40},{16,48},{24,56},{32,0},{40,8},{48,16},{56,24},{64,96... | collective-permute-start | bytes 1769480 | tf_op jit(solution)/shard_map/ppermute | solution.py:723
  54.5 5.0 %collective-permute-start.19 = (bf16[4,2,48,768]{3,2,1,0:T(8,128)(2,1)S(1)}, bf16[4,2,48,768]{3,2,1,0:T(8,128)(2,1)S(1)}, u32[]{:S(2)}, u32[]{:S(2)}) collective-permute-start(bf16[4,2,48,768]{3,2,1,0:T(8,128)(2,1)S(1)} %get-tuple-element.69), channel_id=1, source_target_pairs={{0,224},{8,232},{16,240},{24,248},{32,64},{40,72},{48,80},{56,88},... | collective-permute-start | bytes 1769480 | tf_op jit(solution)/shard_map/ppermute | solution.py:723
  59.5 2.4 %shard_map.108 = (bf16[656,128]{1,0:T(8,128)(2,1)S(1)}, bf16[752,128]{1,0:T(8,128)(2,1)S(1)}, f32[96,128]{1,0:T(8,128)}) custom-call(bf16[704,128]{1,0:T(8,128)(2,1)S(1)} %get-tuple-element.52.refs_0_, bf16[704,128]{1,0:T(8,128)(2,1)S(1)} %collective-permute-done.10.refs_1_, bf16[2,704,128]{2,1,0:T(8,128)(2,1)S(1)} %collective-permute-done.11.refs_1_.refs_2_, ...), custom_call_target="tpu_custom_call" | custom-call | flops 34359738368 | bytes 2097152 | tf_op jit(solution)/shard_map/pallas_call | solution.py:587
  63.4 2.7 %collective-permute-start.15 = (f32[96,128]{1,0:T(8,128)S(1)}, f32[96,128]{1,0:T(8,128)S(1)}, u32[]{:S(2)}, u32[]{:S(2)}) collective-permute-start(f32[96,128]{1,0:T(8,128)S(1)} %shard_map.109), channel_id=1, source_target_pairs={{0,16},{8,24},{16,0},{24,8},{32,48},{40,56},{48,32},{56,40},{64,80... | collective-permute-start | bytes 147464 | tf_op jit(solution)/shard_map/ppermute | solution.py:761
  66.1 3.8 %collective-permute-done.15 = f32[96,128]{1,0:T(8,128)S(1)} collective-permute-done((f32[96,128]{1,0:T(8,128)S(1)}, f32[96,128]{1,0:T(8,128)S(1)}, u32[]{:S(2)}, u32[]{:S(2)}) %collective-permute-start.15) | collective-permute-done | bytes 49184 | tf_op jit(solution)/shard_map/ppermute | solution.py:761
  70.1 4.9 %collective-permute-start.25 = (bf16[2,2,48,768]{3,2,1,0:T(8,128)(2,1)S(1)}, bf16[2,2,48,768]{3,2,1,0:T(8,128)(2,1)S(1)}, u32[]{:S(2)}, u32[]{:S(2)}) collective-permute-start(bf16[2,2,48,768]{3,2,1,0:T(8,128)(2,1)S(1)} %get-tuple-element.84), channel_id=1, source_target_pairs={{0,224},{8,232},{16,240},{24,248},{32,64},{40,72},{48,80},{56,88},... | collective-permute-start | bytes 884744 | tf_op jit(solution)/shard_map/ppermute | solution.py:723
  75.3 4.1 %collective-permute-done.16.refs_1_ = f32[96,128]{1,0:T(8,128)S(1)} collective-permute-done((f32[96,128]{1,0:T(8,128)S(1)}, f32[96,128]{1,0:T(8,128)S(1)}, u32[]{:S(2)}, u32[]{:S(2)}) %collective-permute-start.16) | collective-permute-done | bytes 49184 | tf_op jit(solution)/shard_map/ppermute | solution.py:761
  79.7 2.6 %collective-permute-start.26 = (bf16[2,48,768]{2,1,0:T(8,128)(2,1)S(1)}, bf16[2,48,768]{2,1,0:T(8,128)(2,1)S(1)}, u32[]{:S(2)}, u32[]{:S(2)}) collective-permute-start(bf16[2,48,768]{2,1,0:T(8,128)(2,1)S(1)} %get-tuple-element.86), channel_id=1, source_target_pairs={{0,16},{8,24},{16,0},{24,8},{32,48},{40,56},{48,32},{56,40},{64,80... | collective-permute-start | bytes 442376 | tf_op jit(solution)/shard_map/ppermute | solution.py:723
  82.5 3.8 %collective-permute-start.27 = (f32[96,128]{1,0:T(8,128)S(1)}, f32[96,128]{1,0:T(8,128)S(1)}, u32[]{:S(2)}, u32[]{:S(2)}) collective-permute-start(f32[96,128]{1,0:T(8,128)S(1)} %get-tuple-element.72.refs_2_), channel_id=1, source_target_pairs={{0,224},{8,232},{16,240},{24,248},{32,64},{40,72},{48,80},{56,88},... | collective-permute-start | bytes 147464 | tf_op jit(solution)/shard_map/ppermute | solution.py:761
  86.3 2.1 %collective-permute-done.27.refs_3_ = f32[96,128]{1,0:T(8,128)S(1)} collective-permute-done((f32[96,128]{1,0:T(8,128)S(1)}, f32[96,128]{1,0:T(8,128)S(1)}, u32[]{:S(2)}, u32[]{:S(2)}) %collective-permute-start.27) | collective-permute-done | bytes 49184 | tf_op jit(solution)/shard_map/ppermute | solution.py:761
  88.4 3.3 %collective-permute-start.28 = (bf16[64,768]{1,0:T(8,128)(2,1)S(1)}, bf16[64,768]{1,0:T(8,128)(2,1)S(1)}, u32[]{:S(2)}, u32[]{:S(2)}) collective-permute-start(bf16[64,768]{1,0:T(8,128)(2,1)S(1)} %get-tuple-element.88.refs_3_), channel_id=1, source_target_pairs={{0,96},{8,104},{16,112},{24,120},{32,192},{40,200},{48,208},{56,21... | collective-permute-start | bytes 294920 | tf_op jit(solution)/shard_map/ppermute | solution.py:723
  93.7 2.2 %shard_map.111 = bf16[3,144,192]{2,1,0:T(8,128)(2,1)} custom-call(bf16[752,128]{1,0:T(8,128)(2,1)S(1)} %collective-permute-done.14.refs_1_.refs_0_, bf16[656,128]{1,0:T(8,128)(2,1)S(1)} %get-tuple-element.61.refs_1_, bf16[656,128]{1,0:T(8,128)(2,1)S(1)} %get-tuple-element.62.refs_2_, f32[49,256]{1,0:T(8,128)S(1)} %get-tuple-element.48.refs_3_, ...), custom_call_target="tpu_custom_call" | custom-call | flops 8388608 | bytes 1048576 | tf_op jit(solution)/shard_map/pallas_call | solution.py:587
  95.8 4.4 %collective-permute-done.22.refs_1_ = bf16[48,768]{1,0:T(8,128)(2,1)S(1)} collective-permute-done((bf16[48,768]{1,0:T(8,128)(2,1)S(1)}, bf16[48,768]{1,0:T(8,128)(2,1)S(1)}, u32[]{:S(2)}, u32[]{:S(2)}) %collective-permute-start.22) | collective-permute-done | bytes 73760 | tf_op jit(solution)/shard_map/ppermute | solution.py:723
  (56 shorter events, 21.5 us)
Async XLA Ops:
  1.7 7.2 %collective-permute-start.1 = (bf16[656,128]{1,0:T(8,128)(2,1)S(1)}, bf16[656,128]{1,0:T(8,128)(2,1)S(1)}, u32[]{:S(2)}, u32[]{:S(2)}) collective-permute-start(bf16[656,128]{1,0:T(8,128)(2,1)S(1)} %shard_map.102.refs_1_.refs_9_), channel_id=1, source_target_pairs={{8,16},{24,32},{40,48},{56,64},{72,80},{88,96},{104,112},{120,128}... | collective-permute-start | bytes 503816 | tf_op jit(solution)/shard_map/ppermute | solution.py:616
  2.4 6.5 %collective-permute-start = (bf16[656,128]{1,0:T(8,128)(2,1)S(1)}, bf16[656,128]{1,0:T(8,128)(2,1)S(1)}, u32[]{:S(2)}, u32[]{:S(2)}) collective-permute-start(bf16[656,128]{1,0:T(8,128)(2,1)S(1)} %shard_map.102.refs_1_.refs_9_), channel_id=1, source_target_pairs={{0,8},{8,0},{16,24},{24,16},{32,40},{40,32},{48,56},{56,48},{64,72... | collective-permute-start | bytes 503816 | tf_op jit(solution)/shard_map/ppermute | solution.py:631
  10.4 8.3 %collective-permute-start.5 = (bf16[656,128]{1,0:T(8,128)(2,1)S(1)}, bf16[656,128]{1,0:T(8,128)(2,1)S(1)}, u32[]{:S(2)}, u32[]{:S(2)}) collective-permute-start(bf16[656,128]{1,0:T(8,128)(2,1)S(1)} %shard_map.104.refs_0_.refs_5_), channel_id=1, source_target_pairs={{0,4},{1,5},{2,6},{3,7},{4,0},{5,1},{6,2},{7,3},{8,12},{9,13},{10,... | collective-permute-start | bytes 503816 | tf_op jit(solution)/shard_map/ppermute | solution.py:669
  12.8 9.1 %collective-permute-start.2 = (bf16[656,128]{1,0:T(8,128)(2,1)S(1)}, bf16[656,128]{1,0:T(8,128)(2,1)S(1)}, u32[]{:S(2)}, u32[]{:S(2)}) collective-permute-start(bf16[656,128]{1,0:T(8,128)(2,1)S(1)} %shard_map.104.refs_0_.refs_5_), channel_id=1, source_target_pairs={{0,1},{1,0},{2,3},{3,2},{4,5},{5,4},{6,7},{7,6},{8,9},{9,8},{10,11... | collective-permute-start | bytes 503816 | tf_op jit(solution)/shard_map/ppermute | solution.py:669
  15.5 8.4 %collective-permute-start.7 = (bf16[656,128]{1,0:T(8,128)(2,1)S(1)}, bf16[656,128]{1,0:T(8,128)(2,1)S(1)}, u32[]{:S(2)}, u32[]{:S(2)}) collective-permute-start(bf16[656,128]{1,0:T(8,128)(2,1)S(1)} %shard_map.104.refs_0_.refs_5_), channel_id=1, source_target_pairs={{0,2},{1,3},{2,4},{3,5},{4,6},{5,7},{6,0},{7,1},{8,10},{9,11},{10,... | collective-permute-start | bytes 503816 | tf_op jit(solution)/shard_map/ppermute | solution.py:669
  15.5 8.4 %collective-permute-start.3 = (bf16[656,128]{1,0:T(8,128)(2,1)S(1)}, bf16[656,128]{1,0:T(8,128)(2,1)S(1)}, u32[]{:S(2)}, u32[]{:S(2)}) collective-permute-start(bf16[656,128]{1,0:T(8,128)(2,1)S(1)} %shard_map.104.refs_0_.refs_5_), channel_id=1, source_target_pairs={{0,6},{1,7},{2,0},{3,1},{4,2},{5,3},{6,4},{7,5},{8,14},{9,15},{10,... | collective-permute-start | bytes 503816 | tf_op jit(solution)/shard_map/ppermute | solution.py:669
  18.7 7.3 %collective-permute-start.6 = (bf16[656,128]{1,0:T(8,128)(2,1)S(1)}, bf16[656,128]{1,0:T(8,128)(2,1)S(1)}, u32[]{:S(2)}, u32[]{:S(2)}) collective-permute-start(bf16[656,128]{1,0:T(8,128)(2,1)S(1)} %collective-permute-done.5.refs_4_), channel_id=1, source_target_pairs={{0,1},{1,0},{2,3},{3,2},{4,5},{5,4},{6,7},{7,6},{8,9},{9,8},{10,11... | collective-permute-start | bytes 503816 | tf_op jit(solution)/shard_map/ppermute | solution.py:669
  34.0 9.3 %collective-permute-start.11 = (bf16[2,704,128]{2,1,0:T(8,128)(2,1)S(1)}, bf16[2,704,128]{2,1,0:T(8,128)(2,1)S(1)}, u32[]{:S(2)}, u32[]{:S(2)}) collective-permute-start(bf16[2,704,128]{2,1,0:T(8,128)(2,1)S(1)} %get-tuple-element.55), channel_id=1, source_target_pairs={{0,2},{1,3},{2,4},{3,5},{4,6},{5,7},{6,0},{7,1},{8,10},{9,11},{10,... | collective-permute-start | bytes 1081352 | tf_op jit(solution)/shard_map/ppermute | solution.py:669
  35.3 8.0 %collective-permute-start.12 = (bf16[2,704,128]{2,1,0:T(8,128)(2,1)S(1)}, bf16[2,704,128]{2,1,0:T(8,128)(2,1)S(1)}, u32[]{:S(2)}, u32[]{:S(2)}) collective-permute-start(bf16[2,704,128]{2,1,0:T(8,128)(2,1)S(1)} %get-tuple-element.56), channel_id=1, source_target_pairs={{0,6},{1,7},{2,0},{3,1},{4,2},{5,3},{6,4},{7,5},{8,14},{9,15},{10,... | collective-permute-start | bytes 1081352 | tf_op jit(solution)/shard_map/ppermute | solution.py:669
  36.1 7.0 %collective-permute-start.9 = (bf16[704,128]{1,0:T(8,128)(2,1)S(1)}, bf16[704,128]{1,0:T(8,128)(2,1)S(1)}, u32[]{:S(2)}, u32[]{:S(2)}) collective-permute-start(bf16[704,128]{1,0:T(8,128)(2,1)S(1)} %get-tuple-element.54), channel_id=1, source_target_pairs={{0,1},{1,0},{2,3},{3,2},{4,5},{5,4},{6,7},{7,6},{8,9},{9,8},{10,11... | collective-permute-start | bytes 540680 | tf_op jit(solution)/shard_map/ppermute | solution.py:669
  38.2 12.0 %collective-permute-start.23 = (bf16[8,2,48,768]{3,2,1,0:T(8,128)(2,1)S(1)}, bf16[8,2,48,768]{3,2,1,0:T(8,128)(2,1)S(1)}, u32[]{:S(2)}, u32[]{:S(2)}) collective-permute-start(bf16[8,2,48,768]{3,2,1,0:T(8,128)(2,1)S(1)} %get-tuple-element.80), channel_id=1, source_target_pairs={{0,8},{8,0},{16,24},{24,16},{32,40},{40,32},{48,56},{56,48},{64,72... | collective-permute-start | bytes 3538952 | tf_op jit(solution)/shard_map/ppermute | solution.py:717
  45.0 9.2 %collective-permute-start.18 = (bf16[8,2,48,768]{3,2,1,0:T(8,128)(2,1)S(1)}, bf16[8,2,48,768]{3,2,1,0:T(8,128)(2,1)S(1)}, u32[]{:S(2)}, u32[]{:S(2)}) collective-permute-start(bf16[8,2,48,768]{3,2,1,0:T(8,128)(2,1)S(1)} %get-tuple-element.67), channel_id=1, source_target_pairs={{0,8},{8,0},{16,24},{24,16},{32,40},{40,32},{48,56},{56,48},{64,72... | collective-permute-start | bytes 3538952 | tf_op jit(solution)/shard_map/ppermute | solution.py:721
  45.1 14.4 %collective-permute-start.10 = (bf16[704,128]{1,0:T(8,128)(2,1)S(1)}, bf16[704,128]{1,0:T(8,128)(2,1)S(1)}, u32[]{:S(2)}, u32[]{:S(2)}) collective-permute-start(bf16[704,128]{1,0:T(8,128)(2,1)S(1)} %shard_map.106.refs_3_), channel_id=1, source_target_pairs={{0,4},{1,5},{2,6},{3,7},{4,0},{5,1},{6,2},{7,3},{8,12},{9,13},{10,... | collective-permute-start | bytes 540680 | tf_op jit(solution)/shard_map/ppermute | solution.py:669
  47.5 12.1 %collective-permute-start.13 = (bf16[704,128]{1,0:T(8,128)(2,1)S(1)}, bf16[704,128]{1,0:T(8,128)(2,1)S(1)}, u32[]{:S(2)}, u32[]{:S(2)}) collective-permute-start(bf16[704,128]{1,0:T(8,128)(2,1)S(1)} %shard_map.107.refs_2_), channel_id=1, source_target_pairs={{0,1},{1,0},{2,3},{3,2},{4,5},{5,4},{6,7},{7,6},{8,9},{9,8},{10,11... | collective-permute-start | bytes 540680 | tf_op jit(solution)/shard_map/ppermute | solution.py:669
  50.6 19.4 %collective-permute-start.24 = (bf16[4,2,48,768]{3,2,1,0:T(8,128)(2,1)S(1)}, bf16[4,2,48,768]{3,2,1,0:T(8,128)(2,1)S(1)}, u32[]{:S(2)}, u32[]{:S(2)}) collective-permute-start(bf16[4,2,48,768]{3,2,1,0:T(8,128)(2,1)S(1)} %get-tuple-element.82), channel_id=1, source_target_pairs={{0,32},{8,40},{16,48},{24,56},{32,0},{40,8},{48,16},{56,24},{64,96... | collective-permute-start | bytes 1769480 | tf_op jit(solution)/shard_map/ppermute | solution.py:723
  54.5 20.5 %collective-permute-start.19 = (bf16[4,2,48,768]{3,2,1,0:T(8,128)(2,1)S(1)}, bf16[4,2,48,768]{3,2,1,0:T(8,128)(2,1)S(1)}, u32[]{:S(2)}, u32[]{:S(2)}) collective-permute-start(bf16[4,2,48,768]{3,2,1,0:T(8,128)(2,1)S(1)} %get-tuple-element.69), channel_id=1, source_target_pairs={{0,224},{8,232},{16,240},{24,248},{32,64},{40,72},{48,80},{56,88},... | collective-permute-start | bytes 1769480 | tf_op jit(solution)/shard_map/ppermute | solution.py:723
  61.9 13.0 %collective-permute-start.17 = (bf16[656,128]{1,0:T(8,128)(2,1)S(1)}, bf16[656,128]{1,0:T(8,128)(2,1)S(1)}, u32[]{:S(2)}, u32[]{:S(2)}) collective-permute-start(bf16[656,128]{1,0:T(8,128)(2,1)S(1)} %get-tuple-element.61.refs_1_), channel_id=1, source_target_pairs={{8,16},{24,32},{40,48},{56,64},{72,80},{88,96},{104,112},{120,128}... | collective-permute-start | bytes 503816 | tf_op jit(solution)/shard_map/ppermute | solution.py:616
  63.4 6.5 %collective-permute-start.15 = (f32[96,128]{1,0:T(8,128)S(1)}, f32[96,128]{1,0:T(8,128)S(1)}, u32[]{:S(2)}, u32[]{:S(2)}) collective-permute-start(f32[96,128]{1,0:T(8,128)S(1)} %shard_map.109), channel_id=1, source_target_pairs={{0,16},{8,24},{16,0},{24,8},{32,48},{40,56},{48,32},{56,40},{64,80... | collective-permute-start | bytes 147464 | tf_op jit(solution)/shard_map/ppermute | solution.py:761
  70.1 9.6 %collective-permute-start.25 = (bf16[2,2,48,768]{3,2,1,0:T(8,128)(2,1)S(1)}, bf16[2,2,48,768]{3,2,1,0:T(8,128)(2,1)S(1)}, u32[]{:S(2)}, u32[]{:S(2)}) collective-permute-start(bf16[2,2,48,768]{3,2,1,0:T(8,128)(2,1)S(1)} %get-tuple-element.84), channel_id=1, source_target_pairs={{0,224},{8,232},{16,240},{24,248},{32,64},{40,72},{48,80},{56,88},... | collective-permute-start | bytes 884744 | tf_op jit(solution)/shard_map/ppermute | solution.py:723
  75.1 7.2 %collective-permute-start.20 = (bf16[4,48,768]{2,1,0:T(8,128)(2,1)S(1)}, bf16[4,48,768]{2,1,0:T(8,128)(2,1)S(1)}, u32[]{:S(2)}, u32[]{:S(2)}) collective-permute-start(bf16[4,48,768]{2,1,0:T(8,128)(2,1)S(1)} %get-tuple-element.71), channel_id=1, source_target_pairs={{0,16},{8,24},{16,0},{24,8},{32,48},{40,56},{48,32},{56,40},{64,80... | collective-permute-start | bytes 884744 | tf_op jit(solution)/shard_map/ppermute | solution.py:723
  79.7 8.6 %collective-permute-start.26 = (bf16[2,48,768]{2,1,0:T(8,128)(2,1)S(1)}, bf16[2,48,768]{2,1,0:T(8,128)(2,1)S(1)}, u32[]{:S(2)}, u32[]{:S(2)}) collective-permute-start(bf16[2,48,768]{2,1,0:T(8,128)(2,1)S(1)} %get-tuple-element.86), channel_id=1, source_target_pairs={{0,16},{8,24},{16,0},{24,8},{32,48},{40,56},{48,32},{56,40},{64,80... | collective-permute-start | bytes 442376 | tf_op jit(solution)/shard_map/ppermute | solution.py:723
  82.4 9.3 %collective-permute-start.21 = (bf16[2,48,768]{2,1,0:T(8,128)(2,1)S(1)}, bf16[2,48,768]{2,1,0:T(8,128)(2,1)S(1)}, u32[]{:S(2)}, u32[]{:S(2)}) collective-permute-start(bf16[2,48,768]{2,1,0:T(8,128)(2,1)S(1)} %get-tuple-element.74), channel_id=1, source_target_pairs={{0,32},{8,40},{16,48},{24,56},{32,0},{40,8},{48,16},{56,24},{64,96... | collective-permute-start | bytes 442376 | tf_op jit(solution)/shard_map/ppermute | solution.py:723
  88.4 7.4 %collective-permute-start.28 = (bf16[64,768]{1,0:T(8,128)(2,1)S(1)}, bf16[64,768]{1,0:T(8,128)(2,1)S(1)}, u32[]{:S(2)}, u32[]{:S(2)}) collective-permute-start(bf16[64,768]{1,0:T(8,128)(2,1)S(1)} %get-tuple-element.88.refs_3_), channel_id=1, source_target_pairs={{0,96},{8,104},{16,112},{24,120},{32,192},{40,200},{48,208},{56,21... | collective-permute-start | bytes 294920 | tf_op jit(solution)/shard_map/ppermute | solution.py:723
  91.7 8.5 %collective-permute-start.22 = (bf16[48,768]{1,0:T(8,128)(2,1)S(1)}, bf16[48,768]{1,0:T(8,128)(2,1)S(1)}, u32[]{:S(2)}, u32[]{:S(2)}) collective-permute-start(bf16[48,768]{1,0:T(8,128)(2,1)S(1)} %get-tuple-element.76), channel_id=1, source_target_pairs={{0,160},{8,168},{16,176},{24,184},{32,128},{40,136},{48,144},{56,1... | collective-permute-start | bytes 221192 | tf_op jit(solution)/shard_map/ppermute | solution.py:723
  (5 other events, 22.2 us)

commit v6 on v5

--- a/solution.py
+++ b/solution.py
@@ -25,7 +25,7 @@
 COST_PASS = 1 << 20
 COST_FAR = 1 << 20
 COST_IN = 1 << 30
-COST_SUMS = 1 << 20
+COST_SUMS = 1 << 34
 GRP = 48
 CALL = 1536
 FF = 768
@@ -716,7 +716,7 @@
     )
     got_out = lax.ppermute(send_out, "rows", core)
     keep_in, send_in = call(
-        weights_in_kernel, pairs, [normed, grad_hidden], after=[other_sum, far_sum], flops=COST_IN, moved=8 << 20
+        weights_in_kernel, pairs, [normed, grad_hidden], after=[across], flops=COST_IN, moved=8 << 20
     )
     got_in = lax.ppermute(send_in, "rows", core)
     def move(block, f):

time: 101 us -> 101 us (level)
  starting transfers between devices: 53 us -> 50.2 us
  waiting for transfers between devices: 26.2 us -> 28.7 us
    ppermute x3, starting transfers between devices: 6.6 us -> 4.92 us  [partner_terms(): return lax.ppermute(terms, 'rows', rows_perm(f))]
    ppermute x8, waiting for transfers between devices: 4.65 us -> 5.95 us  [move(): return lax.ppermute(block, 'rows', rows_perm(f))]
    ppermute x3, waiting for transfers between devices: 9.97 us -> 11.2 us  [partner_terms(): return lax.ppermute(terms, 'rows', rows_perm(f))]
  transfers between devices with their start and end apart: 29 -> 29, of which waited for: 11 -> 12; matrix products, arithmetic and copies ran while one was open for 0% -> 0% of each run, Pallas kernels for 12% -> 12%
where the time goes in v6:
time: 101 us
  starting transfers between devices  50.2 us (50%)
  waiting for transfers between devices  28.7 us (28%)
  Pallas kernels  21 us (21%)
    ppermute x8, starting transfers between devices, move(): return lax.ppermute(block, 'rows', rows_perm(f))  21 us
    pallas_call x21, Pallas kernels, call(): pl.pallas_call(body, out_shape=shapes, in_specs=[hbm if n in far else nea...  21 us
    ppermute x12, starting transfers between devices, shift(): return lax.ppermute(block, 'chan', chan_shift(k, x))  19.8 us
    ppermute x3, waiting for transfers between devices, partner_terms(): return lax.ppermute(terms, 'rows', rows_perm(f))  11.2 us
    ppermute x12, waiting for transfers between devices, shift(): return lax.ppermute(block, 'chan', chan_shift(k, x))  10.8 us
    ppermute x8, waiting for transfers between devices, move(): return lax.ppermute(block, 'rows', rows_perm(f))  5.95 us
    ppermute x3, starting transfers between devices, partner_terms(): return lax.ppermute(terms, 'rows', rows_perm(f))  4.92 us
    ppermute x1, starting transfers between devices, shards(): above, below = (lax.ppermute(packed, 'rows', core), other_side(packed))  2.93 us
  transfers between devices with their start and end apart: 29, of which 12 were waited for; matrix products, arithmetic and copies ran while one was open for 0% of the time, Pallas kernels for 12%

profile of v6, /device:TPU:8, one launch (start us, length us, event | category | flops | bytes accessed | tf_op | source)
XLA Modules:
  0.0 100.7 jit_solution(4660595358135860293)
XLA Ops:
  2.4 2.9 %collective-permute-start = (bf16[656,128]{1,0:T(8,128)(2,1)S(1)}, bf16[656,128]{1,0:T(8,128)(2,1)S(1)}, u32[]{:S(2)}, u32[]{:S(2)}) collective-permute-start(bf16[656,128]{1,0:T(8,128)(2,1)S(1)} %shard_map.102.refs_1_.refs_9_), channel_id=1, source_target_pairs={{0,8},{8,0},{16,24},{24,16},{32,40},{40,32},{48,56},{56,48},{64,72... | collective-permute-start | bytes 503816 | tf_op jit(solution)/shard_map/ppermute | solution.py:631
  5.3 3.5 %shard_map.103 = (bf16[432,1536]{1,0:T(8,128)(2,1)S(1)}, f32[432,768]{1,0:T(8,128)S(1)}, bf16[1536,768]{1,0:T(8,128)(2,1)S(1)}, f32[1,1536]{1,0:T(1,128)S(1)}, f...) custom-call(bf16[432,1536]{1,0:T(8,128)(2,1)} %bitcast.4, f32[12,128]{1,0:T(8,128)} %bitcast.5, ...), custom_call_target="tpu_custom_call" | custom-call | flops 1019215872 | bytes 8388608 | tf_op jit(solution)/shard_map/pallas_call | solution.py:587
  10.4 2.4 %collective-permute-start.5 = (bf16[656,128]{1,0:T(8,128)(2,1)S(1)}, bf16[656,128]{1,0:T(8,128)(2,1)S(1)}, u32[]{:S(2)}, u32[]{:S(2)}) collective-permute-start(bf16[656,128]{1,0:T(8,128)(2,1)S(1)} %shard_map.104.refs_0_.refs_5_), channel_id=1, source_target_pairs={{0,4},{1,5},{2,6},{3,7},{4,0},{5,1},{6,2},{7,3},{8,12},{9,13},{10,... | collective-permute-start | bytes 503816 | tf_op jit(solution)/shard_map/ppermute | solution.py:669
  12.8 2.7 %collective-permute-start.2 = (bf16[656,128]{1,0:T(8,128)(2,1)S(1)}, bf16[656,128]{1,0:T(8,128)(2,1)S(1)}, u32[]{:S(2)}, u32[]{:S(2)}) collective-permute-start(bf16[656,128]{1,0:T(8,128)(2,1)S(1)} %shard_map.104.refs_0_.refs_5_), channel_id=1, source_target_pairs={{0,1},{1,0},{2,3},{3,2},{4,5},{5,4},{6,7},{7,6},{8,9},{9,8},{10,11... | collective-permute-start | bytes 503816 | tf_op jit(solution)/shard_map/ppermute | solution.py:669
  15.5 2.0 %collective-permute-start.3 = (bf16[656,128]{1,0:T(8,128)(2,1)S(1)}, bf16[656,128]{1,0:T(8,128)(2,1)S(1)}, u32[]{:S(2)}, u32[]{:S(2)}) collective-permute-start(bf16[656,128]{1,0:T(8,128)(2,1)S(1)} %shard_map.104.refs_0_.refs_5_), channel_id=1, source_target_pairs={{0,6},{1,7},{2,0},{3,1},{4,2},{5,3},{6,4},{7,5},{8,14},{9,15},{10,... | collective-permute-start | bytes 503816 | tf_op jit(solution)/shard_map/ppermute | solution.py:669
  18.7 3.2 %collective-permute-start.6 = (bf16[656,128]{1,0:T(8,128)(2,1)S(1)}, bf16[656,128]{1,0:T(8,128)(2,1)S(1)}, u32[]{:S(2)}, u32[]{:S(2)}) collective-permute-start(bf16[656,128]{1,0:T(8,128)(2,1)S(1)} %collective-permute-done.5.refs_4_), channel_id=1, source_target_pairs={{0,1},{1,0},{2,3},{3,2},{4,5},{5,4},{6,7},{7,6},{8,9},{9,8},{10,11... | collective-permute-start | bytes 503816 | tf_op jit(solution)/shard_map/ppermute | solution.py:669
  23.9 2.1 %collective-permute-done.6.refs_5_ = bf16[656,128]{1,0:T(8,128)(2,1)S(1)} collective-permute-done((bf16[656,128]{1,0:T(8,128)(2,1)S(1)}, bf16[656,128]{1,0:T(8,128)(2,1)S(1)}, u32[]{:S(2)}, u32[]{:S(2)}) %collective-permute-start.6) | collective-permute-done | bytes 167968 | tf_op jit(solution)/shard_map/ppermute | solution.py:669
  28.8 5.1 %shard_map.105 = (bf16[432,1536]{1,0:T(8,128)(2,1)S(1)}, bf16[432,768]{1,0:T(8,128)(2,1)S(1)}, bf16[432,768]{1,0:T(8,128)(2,1)S(1)}, f32[432,128]{1,0:T(8,128)S(...) custom-call(bf16[656,128]{1,0:T(8,128)(2,1)S(1)} %shard_map.104.refs, ...), custom_call_target="tpu_custom_call" | custom-call | flops 2038431744 | bytes 8388608 | tf_op jit(solution)/shard_map/pallas_call | solution.py:587
  38.3 4.7 %collective-permute-done.9.refs_1_.refs_2_ = bf16[704,128]{1,0:T(8,128)(2,1)S(1)} collective-permute-done((bf16[704,128]{1,0:T(8,128)(2,1)S(1)}, bf16[704,128]{1,0:T(8,128)(2,1)S(1)}, u32[]{:S(2)}, u32[]{:S(2)}) %collective-permute-start.9) | collective-permute-done | bytes 180256 | tf_op jit(solution)/shard_map/ppermute | solution.py:669
  43.3 2.1 %collective-permute-start.10 = (bf16[704,128]{1,0:T(8,128)(2,1)S(1)}, bf16[704,128]{1,0:T(8,128)(2,1)S(1)}, u32[]{:S(2)}, u32[]{:S(2)}) collective-permute-start(bf16[704,128]{1,0:T(8,128)(2,1)S(1)} %shard_map.106), channel_id=1, source_target_pairs={{0,4},{1,5},{2,6},{3,7},{4,0},{5,1},{6,2},{7,3},{8,12},{9,13},{10,... | collective-permute-start | bytes 540680 | tf_op jit(solution)/shard_map/ppermute | solution.py:669
  47.2 2.5 %collective-permute-start.13 = (bf16[704,128]{1,0:T(8,128)(2,1)S(1)}, bf16[704,128]{1,0:T(8,128)(2,1)S(1)}, u32[]{:S(2)}, u32[]{:S(2)}) collective-permute-start(bf16[704,128]{1,0:T(8,128)(2,1)S(1)} %shard_map.107.refs_2_), channel_id=1, source_target_pairs={{0,1},{1,0},{2,3},{3,2},{4,5},{5,4},{6,7},{7,6},{8,9},{9,8},{10,11... | collective-permute-start | bytes 540680 | tf_op jit(solution)/shard_map/ppermute | solution.py:669
  50.0 3.3 %collective-permute-start.24 = (bf16[4,2,48,768]{3,2,1,0:T(8,128)(2,1)S(1)}, bf16[4,2,48,768]{3,2,1,0:T(8,128)(2,1)S(1)}, u32[]{:S(2)}, u32[]{:S(2)}) collective-permute-start(bf16[4,2,48,768]{3,2,1,0:T(8,128)(2,1)S(1)} %get-tuple-element.82), channel_id=1, source_target_pairs={{0,32},{8,40},{16,48},{24,56},{32,0},{40,8},{48,16},{56,24},{64,96... | collective-permute-start | bytes 1769480 | tf_op jit(solution)/shard_map/ppermute | solution.py:723
  53.6 5.0 %collective-permute-start.19 = (bf16[4,2,48,768]{3,2,1,0:T(8,128)(2,1)S(1)}, bf16[4,2,48,768]{3,2,1,0:T(8,128)(2,1)S(1)}, u32[]{:S(2)}, u32[]{:S(2)}) collective-permute-start(bf16[4,2,48,768]{3,2,1,0:T(8,128)(2,1)S(1)} %get-tuple-element.69), channel_id=1, source_target_pairs={{0,224},{8,232},{16,240},{24,248},{32,64},{40,72},{48,80},{56,88},... | collective-permute-start | bytes 1769480 | tf_op jit(solution)/shard_map/ppermute | solution.py:723
  58.6 2.4 %shard_map.108 = (bf16[656,128]{1,0:T(8,128)(2,1)S(1)}, bf16[752,128]{1,0:T(8,128)(2,1)S(1)}, f32[96,128]{1,0:T(8,128)}) custom-call(bf16[704,128]{1,0:T(8,128)(2,1)S(1)} %get-tuple-element.52.refs_0_, bf16[704,128]{1,0:T(8,128)(2,1)S(1)} %collective-permute-done.10.refs_1_, bf16[2,704,128]{2,1,0:T(8,128)(2,1)S(1)} %collective-permute-done.11.refs_1_.refs_2_, ...), custom_call_target="tpu_custom_call" | custom-call | flops 34359738368 | bytes 2097152 | tf_op jit(solution)/shard_map/pallas_call | solution.py:587
  62.4 2.7 %collective-permute-start.15 = (f32[96,128]{1,0:T(8,128)S(1)}, f32[96,128]{1,0:T(8,128)S(1)}, u32[]{:S(2)}, u32[]{:S(2)}) collective-permute-start(f32[96,128]{1,0:T(8,128)S(1)} %shard_map.109), channel_id=1, source_target_pairs={{0,16},{8,24},{16,0},{24,8},{32,48},{40,56},{48,32},{56,40},{64,80... | collective-permute-start | bytes 147464 | tf_op jit(solution)/shard_map/ppermute | solution.py:761
  65.1 3.8 %collective-permute-done.15 = f32[96,128]{1,0:T(8,128)S(1)} collective-permute-done((f32[96,128]{1,0:T(8,128)S(1)}, f32[96,128]{1,0:T(8,128)S(1)}, u32[]{:S(2)}, u32[]{:S(2)}) %collective-permute-start.15) | collective-permute-done | bytes 49184 | tf_op jit(solution)/shard_map/ppermute | solution.py:761
  69.1 5.7 %collective-permute-start.25 = (bf16[2,2,48,768]{3,2,1,0:T(8,128)(2,1)S(1)}, bf16[2,2,48,768]{3,2,1,0:T(8,128)(2,1)S(1)}, u32[]{:S(2)}, u32[]{:S(2)}) collective-permute-start(bf16[2,2,48,768]{3,2,1,0:T(8,128)(2,1)S(1)} %get-tuple-element.84), channel_id=1, source_target_pairs={{0,224},{8,232},{16,240},{24,248},{32,64},{40,72},{48,80},{56,88},... | collective-permute-start | bytes 884744 | tf_op jit(solution)/shard_map/ppermute | solution.py:723
  75.2 4.1 %collective-permute-done.16.refs_1_ = f32[96,128]{1,0:T(8,128)S(1)} collective-permute-done((f32[96,128]{1,0:T(8,128)S(1)}, f32[96,128]{1,0:T(8,128)S(1)}, u32[]{:S(2)}, u32[]{:S(2)}) %collective-permute-start.16) | collective-permute-done | bytes 49184 | tf_op jit(solution)/shard_map/ppermute | solution.py:761
  83.1 2.1 %collective-permute-start.27 = (f32[96,128]{1,0:T(8,128)S(1)}, f32[96,128]{1,0:T(8,128)S(1)}, u32[]{:S(2)}, u32[]{:S(2)}) collective-permute-start(f32[96,128]{1,0:T(8,128)S(1)} %get-tuple-element.72.refs_2_), channel_id=1, source_target_pairs={{0,224},{8,232},{16,240},{24,248},{32,64},{40,72},{48,80},{56,88},... | collective-permute-start | bytes 147464 | tf_op jit(solution)/shard_map/ppermute | solution.py:761
  85.2 3.3 %collective-permute-done.27.refs_3_ = f32[96,128]{1,0:T(8,128)S(1)} collective-permute-done((f32[96,128]{1,0:T(8,128)S(1)}, f32[96,128]{1,0:T(8,128)S(1)}, u32[]{:S(2)}, u32[]{:S(2)}) %collective-permute-start.27) | collective-permute-done | bytes 49184 | tf_op jit(solution)/shard_map/ppermute | solution.py:761
  88.6 2.8 %collective-permute-start.28 = (bf16[64,768]{1,0:T(8,128)(2,1)S(1)}, bf16[64,768]{1,0:T(8,128)(2,1)S(1)}, u32[]{:S(2)}, u32[]{:S(2)}) collective-permute-start(bf16[64,768]{1,0:T(8,128)(2,1)S(1)} %get-tuple-element.88.refs_3_), channel_id=1, source_target_pairs={{0,96},{8,104},{16,112},{24,120},{32,192},{40,200},{48,208},{56,21... | collective-permute-start | bytes 294920 | tf_op jit(solution)/shard_map/ppermute | solution.py:723
  91.5 2.2 %collective-permute-start.22 = (bf16[48,768]{1,0:T(8,128)(2,1)S(1)}, bf16[48,768]{1,0:T(8,128)(2,1)S(1)}, u32[]{:S(2)}, u32[]{:S(2)}) collective-permute-start(bf16[48,768]{1,0:T(8,128)(2,1)S(1)} %get-tuple-element.76), channel_id=1, source_target_pairs={{0,160},{8,168},{16,176},{24,184},{32,128},{40,136},{48,144},{56,1... | collective-permute-start | bytes 221192 | tf_op jit(solution)/shard_map/ppermute | solution.py:723
  93.6 2.2 %shard_map.111 = bf16[3,144,192]{2,1,0:T(8,128)(2,1)} custom-call(bf16[752,128]{1,0:T(8,128)(2,1)S(1)} %collective-permute-done.14.refs_1_.refs_0_, bf16[656,128]{1,0:T(8,128)(2,1)S(1)} %get-tuple-element.61.refs_1_, bf16[656,128]{1,0:T(8,128)(2,1)S(1)} %get-tuple-element.62.refs_2_, f32[49,256]{1,0:T(8,128)S(1)} %get-tuple-element.48.refs_3_, ...), custom_call_target="tpu_custom_call" | custom-call | flops 8388608 | bytes 1048576 | tf_op jit(solution)/shard_map/pallas_call | solution.py:587
  95.8 4.1 %collective-permute-done.22.refs_1_ = bf16[48,768]{1,0:T(8,128)(2,1)S(1)} collective-permute-done((bf16[48,768]{1,0:T(8,128)(2,1)S(1)}, bf16[48,768]{1,0:T(8,128)(2,1)S(1)}, u32[]{:S(2)}, u32[]{:S(2)}) %collective-permute-start.22) | collective-permute-done | bytes 73760 | tf_op jit(solution)/shard_map/ppermute | solution.py:723
  (56 shorter events, 22.8 us)
Async XLA Ops:
  1.7 7.2 %collective-permute-start.1 = (bf16[656,128]{1,0:T(8,128)(2,1)S(1)}, bf16[656,128]{1,0:T(8,128)(2,1)S(1)}, u32[]{:S(2)}, u32[]{:S(2)}) collective-permute-start(bf16[656,128]{1,0:T(8,128)(2,1)S(1)} %shard_map.102.refs_1_.refs_9_), channel_id=1, source_target_pairs={{8,16},{24,32},{40,48},{56,64},{72,80},{88,96},{104,112},{120,128}... | collective-permute-start | bytes 503816 | tf_op jit(solution)/shard_map/ppermute | solution.py:616
  2.4 6.5 %collective-permute-start = (bf16[656,128]{1,0:T(8,128)(2,1)S(1)}, bf16[656,128]{1,0:T(8,128)(2,1)S(1)}, u32[]{:S(2)}, u32[]{:S(2)}) collective-permute-start(bf16[656,128]{1,0:T(8,128)(2,1)S(1)} %shard_map.102.refs_1_.refs_9_), channel_id=1, source_target_pairs={{0,8},{8,0},{16,24},{24,16},{32,40},{40,32},{48,56},{56,48},{64,72... | collective-permute-start | bytes 503816 | tf_op jit(solution)/shard_map/ppermute | solution.py:631
  10.4 8.3 %collective-permute-start.5 = (bf16[656,128]{1,0:T(8,128)(2,1)S(1)}, bf16[656,128]{1,0:T(8,128)(2,1)S(1)}, u32[]{:S(2)}, u32[]{:S(2)}) collective-permute-start(bf16[656,128]{1,0:T(8,128)(2,1)S(1)} %shard_map.104.refs_0_.refs_5_), channel_id=1, source_target_pairs={{0,4},{1,5},{2,6},{3,7},{4,0},{5,1},{6,2},{7,3},{8,12},{9,13},{10,... | collective-permute-start | bytes 503816 | tf_op jit(solution)/shard_map/ppermute | solution.py:669
  12.8 9.1 %collective-permute-start.2 = (bf16[656,128]{1,0:T(8,128)(2,1)S(1)}, bf16[656,128]{1,0:T(8,128)(2,1)S(1)}, u32[]{:S(2)}, u32[]{:S(2)}) collective-permute-start(bf16[656,128]{1,0:T(8,128)(2,1)S(1)} %shard_map.104.refs_0_.refs_5_), channel_id=1, source_target_pairs={{0,1},{1,0},{2,3},{3,2},{4,5},{5,4},{6,7},{7,6},{8,9},{9,8},{10,11... | collective-permute-start | bytes 503816 | tf_op jit(solution)/shard_map/ppermute | solution.py:669
  15.5 8.4 %collective-permute-start.7 = (bf16[656,128]{1,0:T(8,128)(2,1)S(1)}, bf16[656,128]{1,0:T(8,128)(2,1)S(1)}, u32[]{:S(2)}, u32[]{:S(2)}) collective-permute-start(bf16[656,128]{1,0:T(8,128)(2,1)S(1)} %shard_map.104.refs_0_.refs_5_), channel_id=1, source_target_pairs={{0,2},{1,3},{2,4},{3,5},{4,6},{5,7},{6,0},{7,1},{8,10},{9,11},{10,... | collective-permute-start | bytes 503816 | tf_op jit(solution)/shard_map/ppermute | solution.py:669
  15.5 8.4 %collective-permute-start.3 = (bf16[656,128]{1,0:T(8,128)(2,1)S(1)}, bf16[656,128]{1,0:T(8,128)(2,1)S(1)}, u32[]{:S(2)}, u32[]{:S(2)}) collective-permute-start(bf16[656,128]{1,0:T(8,128)(2,1)S(1)} %shard_map.104.refs_0_.refs_5_), channel_id=1, source_target_pairs={{0,6},{1,7},{2,0},{3,1},{4,2},{5,3},{6,4},{7,5},{8,14},{9,15},{10,... | collective-permute-start | bytes 503816 | tf_op jit(solution)/shard_map/ppermute | solution.py:669
  18.7 7.3 %collective-permute-start.6 = (bf16[656,128]{1,0:T(8,128)(2,1)S(1)}, bf16[656,128]{1,0:T(8,128)(2,1)S(1)}, u32[]{:S(2)}, u32[]{:S(2)}) collective-permute-start(bf16[656,128]{1,0:T(8,128)(2,1)S(1)} %collective-permute-done.5.refs_4_), channel_id=1, source_target_pairs={{0,1},{1,0},{2,3},{3,2},{4,5},{5,4},{6,7},{7,6},{8,9},{9,8},{10,11... | collective-permute-start | bytes 503816 | tf_op jit(solution)/shard_map/ppermute | solution.py:669
  34.0 13.0 %collective-permute-start.11 = (bf16[2,704,128]{2,1,0:T(8,128)(2,1)S(1)}, bf16[2,704,128]{2,1,0:T(8,128)(2,1)S(1)}, u32[]{:S(2)}, u32[]{:S(2)}) collective-permute-start(bf16[2,704,128]{2,1,0:T(8,128)(2,1)S(1)} %get-tuple-element.55), channel_id=1, source_target_pairs={{0,2},{1,3},{2,4},{3,5},{4,6},{5,7},{6,0},{7,1},{8,10},{9,11},{10,... | collective-permute-start | bytes 1081352 | tf_op jit(solution)/shard_map/ppermute | solution.py:669
  35.3 11.7 %collective-permute-start.12 = (bf16[2,704,128]{2,1,0:T(8,128)(2,1)S(1)}, bf16[2,704,128]{2,1,0:T(8,128)(2,1)S(1)}, u32[]{:S(2)}, u32[]{:S(2)}) collective-permute-start(bf16[2,704,128]{2,1,0:T(8,128)(2,1)S(1)} %get-tuple-element.56), channel_id=1, source_target_pairs={{0,6},{1,7},{2,0},{3,1},{4,2},{5,3},{6,4},{7,5},{8,14},{9,15},{10,... | collective-permute-start | bytes 1081352 | tf_op jit(solution)/shard_map/ppermute | solution.py:669
  36.1 7.0 %collective-permute-start.9 = (bf16[704,128]{1,0:T(8,128)(2,1)S(1)}, bf16[704,128]{1,0:T(8,128)(2,1)S(1)}, u32[]{:S(2)}, u32[]{:S(2)}) collective-permute-start(bf16[704,128]{1,0:T(8,128)(2,1)S(1)} %get-tuple-element.54), channel_id=1, source_target_pairs={{0,1},{1,0},{2,3},{3,2},{4,5},{5,4},{6,7},{7,6},{8,9},{9,8},{10,11... | collective-permute-start | bytes 540680 | tf_op jit(solution)/shard_map/ppermute | solution.py:669
  38.2 11.5 %collective-permute-start.23 = (bf16[8,2,48,768]{3,2,1,0:T(8,128)(2,1)S(1)}, bf16[8,2,48,768]{3,2,1,0:T(8,128)(2,1)S(1)}, u32[]{:S(2)}, u32[]{:S(2)}) collective-permute-start(bf16[8,2,48,768]{3,2,1,0:T(8,128)(2,1)S(1)} %get-tuple-element.80), channel_id=1, source_target_pairs={{0,8},{8,0},{16,24},{24,16},{32,40},{40,32},{48,56},{56,48},{64,72... | collective-permute-start | bytes 3538952 | tf_op jit(solution)/shard_map/ppermute | solution.py:717
  43.3 15.3 %collective-permute-start.10 = (bf16[704,128]{1,0:T(8,128)(2,1)S(1)}, bf16[704,128]{1,0:T(8,128)(2,1)S(1)}, u32[]{:S(2)}, u32[]{:S(2)}) collective-permute-start(bf16[704,128]{1,0:T(8,128)(2,1)S(1)} %shard_map.106), channel_id=1, source_target_pairs={{0,4},{1,5},{2,6},{3,7},{4,0},{5,1},{6,2},{7,3},{8,12},{9,13},{10,... | collective-permute-start | bytes 540680 | tf_op jit(solution)/shard_map/ppermute | solution.py:669
  46.9 6.4 %collective-permute-start.18 = (bf16[8,2,48,768]{3,2,1,0:T(8,128)(2,1)S(1)}, bf16[8,2,48,768]{3,2,1,0:T(8,128)(2,1)S(1)}, u32[]{:S(2)}, u32[]{:S(2)}) collective-permute-start(bf16[8,2,48,768]{3,2,1,0:T(8,128)(2,1)S(1)} %get-tuple-element.67), channel_id=1, source_target_pairs={{0,8},{8,0},{16,24},{24,16},{32,40},{40,32},{48,56},{56,48},{64,72... | collective-permute-start | bytes 3538952 | tf_op jit(solution)/shard_map/ppermute | solution.py:721
  47.2 11.4 %collective-permute-start.13 = (bf16[704,128]{1,0:T(8,128)(2,1)S(1)}, bf16[704,128]{1,0:T(8,128)(2,1)S(1)}, u32[]{:S(2)}, u32[]{:S(2)}) collective-permute-start(bf16[704,128]{1,0:T(8,128)(2,1)S(1)} %shard_map.107.refs_2_), channel_id=1, source_target_pairs={{0,1},{1,0},{2,3},{3,2},{4,5},{5,4},{6,7},{7,6},{8,9},{9,8},{10,11... | collective-permute-start | bytes 540680 | tf_op jit(solution)/shard_map/ppermute | solution.py:669
  50.0 19.0 %collective-permute-start.24 = (bf16[4,2,48,768]{3,2,1,0:T(8,128)(2,1)S(1)}, bf16[4,2,48,768]{3,2,1,0:T(8,128)(2,1)S(1)}, u32[]{:S(2)}, u32[]{:S(2)}) collective-permute-start(bf16[4,2,48,768]{3,2,1,0:T(8,128)(2,1)S(1)} %get-tuple-element.82), channel_id=1, source_target_pairs={{0,32},{8,40},{16,48},{24,56},{32,0},{40,8},{48,16},{56,24},{64,96... | collective-permute-start | bytes 1769480 | tf_op jit(solution)/shard_map/ppermute | solution.py:723
  53.6 21.3 %collective-permute-start.19 = (bf16[4,2,48,768]{3,2,1,0:T(8,128)(2,1)S(1)}, bf16[4,2,48,768]{3,2,1,0:T(8,128)(2,1)S(1)}, u32[]{:S(2)}, u32[]{:S(2)}) collective-permute-start(bf16[4,2,48,768]{3,2,1,0:T(8,128)(2,1)S(1)} %get-tuple-element.69), channel_id=1, source_target_pairs={{0,224},{8,232},{16,240},{24,248},{32,64},{40,72},{48,80},{56,88},... | collective-permute-start | bytes 1769480 | tf_op jit(solution)/shard_map/ppermute | solution.py:723
  61.0 13.9 %collective-permute-start.17 = (bf16[656,128]{1,0:T(8,128)(2,1)S(1)}, bf16[656,128]{1,0:T(8,128)(2,1)S(1)}, u32[]{:S(2)}, u32[]{:S(2)}) collective-permute-start(bf16[656,128]{1,0:T(8,128)(2,1)S(1)} %get-tuple-element.61.refs_1_), channel_id=1, source_target_pairs={{8,16},{24,32},{40,48},{56,64},{72,80},{88,96},{104,112},{120,128}... | collective-permute-start | bytes 503816 | tf_op jit(solution)/shard_map/ppermute | solution.py:616
  62.4 6.5 %collective-permute-start.15 = (f32[96,128]{1,0:T(8,128)S(1)}, f32[96,128]{1,0:T(8,128)S(1)}, u32[]{:S(2)}, u32[]{:S(2)}) collective-permute-start(f32[96,128]{1,0:T(8,128)S(1)} %shard_map.109), channel_id=1, source_target_pairs={{0,16},{8,24},{16,0},{24,8},{32,48},{40,56},{48,32},{56,40},{64,80... | collective-permute-start | bytes 147464 | tf_op jit(solution)/shard_map/ppermute | solution.py:761
  69.1 10.4 %collective-permute-start.25 = (bf16[2,2,48,768]{3,2,1,0:T(8,128)(2,1)S(1)}, bf16[2,2,48,768]{3,2,1,0:T(8,128)(2,1)S(1)}, u32[]{:S(2)}, u32[]{:S(2)}) collective-permute-start(bf16[2,2,48,768]{3,2,1,0:T(8,128)(2,1)S(1)} %get-tuple-element.84), channel_id=1, source_target_pairs={{0,224},{8,232},{16,240},{24,248},{32,64},{40,72},{48,80},{56,88},... | collective-permute-start | bytes 884744 | tf_op jit(solution)/shard_map/ppermute | solution.py:723
  75.0 8.0 %collective-permute-start.20 = (bf16[4,48,768]{2,1,0:T(8,128)(2,1)S(1)}, bf16[4,48,768]{2,1,0:T(8,128)(2,1)S(1)}, u32[]{:S(2)}, u32[]{:S(2)}) collective-permute-start(bf16[4,48,768]{2,1,0:T(8,128)(2,1)S(1)} %get-tuple-element.71), channel_id=1, source_target_pairs={{0,16},{8,24},{16,0},{24,8},{32,48},{40,56},{48,32},{56,40},{64,80... | collective-permute-start | bytes 884744 | tf_op jit(solution)/shard_map/ppermute | solution.py:723
  79.6 8.9 %collective-permute-start.26 = (bf16[2,48,768]{2,1,0:T(8,128)(2,1)S(1)}, bf16[2,48,768]{2,1,0:T(8,128)(2,1)S(1)}, u32[]{:S(2)}, u32[]{:S(2)}) collective-permute-start(bf16[2,48,768]{2,1,0:T(8,128)(2,1)S(1)} %get-tuple-element.86), channel_id=1, source_target_pairs={{0,16},{8,24},{16,0},{24,8},{32,48},{40,56},{48,32},{56,40},{64,80... | collective-permute-start | bytes 442376 | tf_op jit(solution)/shard_map/ppermute | solution.py:723
  83.0 8.4 %collective-permute-start.21 = (bf16[2,48,768]{2,1,0:T(8,128)(2,1)S(1)}, bf16[2,48,768]{2,1,0:T(8,128)(2,1)S(1)}, u32[]{:S(2)}, u32[]{:S(2)}) collective-permute-start(bf16[2,48,768]{2,1,0:T(8,128)(2,1)S(1)} %get-tuple-element.74), channel_id=1, source_target_pairs={{0,32},{8,40},{16,48},{24,56},{32,0},{40,8},{48,16},{56,24},{64,96... | collective-permute-start | bytes 442376 | tf_op jit(solution)/shard_map/ppermute | solution.py:723
  88.6 7.2 %collective-permute-start.28 = (bf16[64,768]{1,0:T(8,128)(2,1)S(1)}, bf16[64,768]{1,0:T(8,128)(2,1)S(1)}, u32[]{:S(2)}, u32[]{:S(2)}) collective-permute-start(bf16[64,768]{1,0:T(8,128)(2,1)S(1)} %get-tuple-element.88.refs_3_), channel_id=1, source_target_pairs={{0,96},{8,104},{16,112},{24,120},{32,192},{40,200},{48,208},{56,21... | collective-permute-start | bytes 294920 | tf_op jit(solution)/shard_map/ppermute | solution.py:723
  91.5 8.5 %collective-permute-start.22 = (bf16[48,768]{1,0:T(8,128)(2,1)S(1)}, bf16[48,768]{1,0:T(8,128)(2,1)S(1)}, u32[]{:S(2)}, u32[]{:S(2)}) collective-permute-start(bf16[48,768]{1,0:T(8,128)(2,1)S(1)} %get-tuple-element.76), channel_id=1, source_target_pairs={{0,160},{8,168},{16,176},{24,184},{32,128},{40,136},{48,144},{56,1... | collective-permute-start | bytes 221192 | tf_op jit(solution)/shard_map/ppermute | solution.py:723
  (5 other events, 21.7 us)
